TPU v7x, 32 devices: a whole 2x2x4 slice. The times are simulated.
32 devices in a mesh: dom: 8 (over z, y), feat: 4 (over x, core).
Axes of the slice: x: 2, y: 2, z: 4, core: 2. Of those that a mesh axis runs over, the one named last changes fastest.
Arguments:
- features: bfloat16 [128, 8192], P('feat', 'dom'), may hold values from -6 to 6
- tile_mask: int32 [192, 6, 128, 128], P('dom'), may hold values 0 or 1
- tile_cols: int32 [192, 6], P('dom'), may hold values from 0 to 23, as said below
- replicas: int32 [3, 16384], P(None, 'dom'), may hold values from 0 to 1023, as said below
- degree: int32 [8192], P('dom'), may hold values from 12 to 47
- self_one: bfloat16 [128, 256], replicated, may hold values from -0.5 to 0.5
- neigh_one: bfloat16 [128, 256], replicated, may hold values from -2 to 2
- self_two: bfloat16 [256, 256], replicated, may hold values from -0.375 to 0.375
- neigh_two: bfloat16 [256, 256], replicated, may hold values from -1.5 to 1.5
Outputs:
- embed: bfloat16 [256, 8192], P('feat', 'dom')
Inputs may be any that keep to these rules, and one draw needn't show every extreme that they name: replicas[0] never names the mirror's own partition; a partition's mirrors with one master partition have distinct slots 0 to at most 511 and distinct master rows; in every draw some master partition receives exactly 512 mirrors from every other partition. `tile_cols`: the 6 column blocks of one row of blocks are distinct.
All inputs are finite; a program needn't handle non-finite values. No bound on the sum of `tile_mask` on one device may be relied on, other than what follows from the above.
Results may differ from a plain program's by a relative error of at most 0.0027.
The roundings to bfloat16 on the way count: a program that leaves them out, or rounds other values in their place, can miss the bound.
Values may be sent and summed in bfloat16 or wider, within the bound.
No kernel may reach another device: no remote copies, remote signals or barrier semaphores. Data moves between devices by JAX's collectives and lax.ppermute only.
A program may use at most 64 MiB of HBM per device.

v0:
```python
import jax
import jax.numpy as jnp
from jax import lax
from jax.sharding import PartitionSpec as P


def aggregate_rows(local_values, masks_bf, column_tiles, tile_size):
    feature_row_block, local_rows = local_values.shape
    tiled = local_values.reshape(feature_row_block, local_rows // tile_size, tile_size)
    selected = jnp.take(tiled, column_tiles, axis=1)
    summed = jnp.einsum("fiku,ikvu->fiv", selected, masks_bf, preferred_element_type=jnp.float32)
    return summed.reshape(feature_row_block, local_rows)


def contract(weights, value_rows):
    return lax.dot_general(
        weights, value_rows, (((0,), (0,)), ((), ())), preferred_element_type=jnp.float32
    )


def mix(inputs, neighbours, w_self, w_neigh):
    feat_count = lax.axis_size("feat")
    out_rows = w_self.shape[1] // feat_count
    whole_in, whole_nb = (
        lax.all_gather(inputs, "feat", axis=0, tiled=True),
        lax.all_gather(neighbours, "feat", axis=0, tiled=True),
    )
    column_start = lax.axis_index("feat") * out_rows
    self_cols = lax.dynamic_slice_in_dim(w_self, column_start, out_rows, 1)
    neigh_cols = lax.dynamic_slice_in_dim(w_neigh, column_start, out_rows, 1)
    result = contract(self_cols, whole_in) + contract(neigh_cols, whole_nb)
    return result


def on_device(
    features, tile_mask, tile_cols, replicas, degree, self_one, neigh_one, self_two, neigh_two
):
    dom_count = lax.axis_size("dom")
    masters = features.shape[1]
    mirrors = replicas.shape[1]
    tile_size = tile_mask.shape[-1]
    capacity = 2 * mirrors // dom_count
    slot_count = dom_count * capacity
    position = replicas[0] * capacity + replicas[1]
    send_index = (
        jnp.full((slot_count,), mirrors, jnp.int32)
        .at[position]
        .set(jnp.arange(mirrors, dtype=jnp.int32))
    )
    send_rows = jnp.full((1, slot_count), masters, jnp.int32).at[0, position].set(replicas[2])
    wanted = lax.all_to_all(send_rows, "dom", split_axis=1, concat_axis=1, tiled=True)[0]
    masks_bf = tile_mask.astype(jnp.bfloat16)
    scale = degree.astype(jnp.float32)[None, :]

    def serve(value_rows):
        padded = jnp.concatenate(
            [value_rows, jnp.zeros((value_rows.shape[0], 1), value_rows.dtype)], axis=1
        )
        return jnp.take(padded, wanted, axis=1)

    def collect(received):
        return jnp.take(received, position, axis=1)

    def combine(partial_sum):
        feature_row_block = partial_sum.shape[0]
        rounded_down = partial_sum[:, masters:].astype(jnp.bfloat16)
        padded = jnp.concatenate(
            [rounded_down, jnp.zeros((feature_row_block, 1), jnp.bfloat16)], axis=1
        )
        outgoing = jnp.take(padded, send_index, axis=1)
        received = lax.all_to_all(outgoing, "dom", split_axis=1, concat_axis=1, tiled=True)
        incoming = (
            jnp.zeros((feature_row_block, masters + 1), jnp.float32)
            .at[:, wanted]
            .add(received.astype(jnp.float32))
        )
        total = partial_sum[:, :masters] + incoming[:, :masters]
        return (total / scale).astype(jnp.bfloat16)

    mirror_in = collect(
        lax.all_to_all(serve(features), "dom", split_axis=1, concat_axis=1, tiled=True)
    )
    local_in = jnp.concatenate([features, mirror_in], axis=1)
    mean_one = combine(aggregate_rows(local_in, masks_bf, tile_cols, tile_size))
    hidden_master = jax.nn.relu(mix(features, mean_one, self_one, neigh_one)).astype(jnp.bfloat16)
    hidden_mirror = collect(
        lax.all_to_all(serve(hidden_master), "dom", split_axis=1, concat_axis=1, tiled=True)
    )
    local_hidden = jnp.concatenate([hidden_master, hidden_mirror], axis=1)
    mean_two = combine(aggregate_rows(local_hidden, masks_bf, tile_cols, tile_size))
    return mix(hidden_master, mean_two, self_two, neigh_two).astype(jnp.bfloat16)


def solution(mesh):
    return jax.shard_map(
        on_device,
        mesh=mesh,
        in_specs=(
            P("feat", "dom"),
            P("dom", None, None, None),
            P("dom", None),
            P(None, "dom"),
            P("dom"),
            P(),
            P(),
            P(),
            P(),
        ),
        out_specs=P("feat", "dom"),
        check_vma=False,
    )
```

profile of v0, /device:TPU:5, one launch (start us, length us, event | category | flops | bytes accessed | tf_op | source)
XLA Modules:
  0.0 257.7 jit_solution(13466576289845210008)
XLA Ops:
  0.0 0.9 compare_select_fusion.1
  0.9 0.8 slice.31
  1.6 0.7 fusion.37
  2.4 0.8 and_reduce_fusion
  3.2 8.6 %scatter_custom_fusion.3 = s32[4096]{0:T(1024)} fusion(s32[2048]{0:T(1024)S(1)} %broadcast_select_fusion.4, s32[2048]{0:T(1024)S(1)} %bitcast.100, s32[]{:T(128)} %constant.96.clone.1), kind=kCustom, calls=%fused_computation.75 | custom fusion | bytes 16388
  11.8 5.8 %all-to-all-start = ((s32[1,8,512]{2,0,1:T(1,128)}), s32[1,8,512]{2,0,1:T(1,128)S(1)}, u32[]{:S(2)}, u32[]{:S(2)}) async-start(s32[1,8,512]{2,0,1:T(1,128)} %bitcast.3), calls=%async_computation | async-start | bytes 32768 | tf_op jit(solution)/shard_map/all_to_all | solution.py:51
  17.6 0.7 compare_select_fusion.5
  18.3 8.1 %scatter_custom_fusion = s32[4096]{0:T(1024)S(1)} fusion(s32[2048]{0:T(1024)S(1)} %bitcast.94, s32[2048]{0:T(1024)S(1)} %iota.3, s32[]{:T(128)} %constant.107.clone.1), kind=kCustom, calls=%fused_computation.77 | custom fusion | bytes 16388 | tf_op jit(solution)/shard_map/scatter | solution.py:48
  26.4 0.7 compare_and_fusion.3
  27.1 1.0 copy.110
  28.4 0.6 copy-done.7
  29.0 12.1 %gather_fusion = bf16[4096,32]{1,0:T(8,128)(2,1)S(1)} fusion(bf16[32,1025]{0,1:T(8,128)(2,1)S(1)} %concatenate.22, s32[4096]{0:T(1024)S(1)} %broadcast_clamp_fusion), kind=kCustom, calls=%fused_computation | custom fusion | bytes 540672 | tf_op jit(solution)/shard_map/jit(_take)/gather | solution.py:59
  41.1 0.3 copy.111
  41.5 0.7 broadcast_select_fusion.3
  42.2 5.4 %all-to-all-start.1 = ((bf16[32,8,512]{2,0,1:T(8,128)(2,1)}), bf16[32,8,512]{2,0,1:T(8,128)(2,1)S(1)}, u32[]{:S(2)}, u32[]{:S(2)}) async-start(bf16[32,8,512]{2,0,1:T(8,128)(2,1)} %broadcast_select_fusion.3), calls=%async_computation.1 | async-start | bytes 524288 | tf_op jit(solution)/shard_map/all_to_all | solution.py:81
  47.9 5.5 %all-to-all-done.1 = bf16[32,8,512]{2,0,1:T(8,128)(2,1)S(1)} async-done(((bf16[32,8,512]{2,0,1:T(8,128)(2,1)}), bf16[32,8,512]{2,0,1:T(8,128)(2,1)S(1)}, u32[]{:S(2)}, u32[]{:S(2)}) %all-to-all-start.1) | async-done | bytes 262176 | tf_op jit(solution)/shard_map/all_to_all | solution.py:81
  53.4 0.5 copy.112
  53.8 6.2 %gather_fusion.1 = bf16[2048,32]{1,0:T(8,128)(2,1)S(1)} fusion(bf16[32,4096]{0,1:T(8,128)(2,1)S(1)} %bitcast.82, s32[2048]{0:T(1024)S(1)} %broadcast_clamp_fusion.1), kind=kCustom, calls=%fused_computation.1 | custom fusion | bytes 270336 | tf_op jit(solution)/shard_map/jit(_take)/gather | solution.py:62
  60.6 0.8 gather_fusion.2
  61.5 5.4 %fusion.12 = f32[24,4,8,128]{3,2,1,0:T(8,128)S(1)} fusion(s32[24,6,128,128]{3,2,1,0:T(8,128)} %param.10, bf16[24,6,32,128]{3,2,1,0:T(8,128)(2,1)S(1)} %bitcast.81, pred[24,6]{1,0:T(8,128)(4,1)S(1)} %copy.109), kind=kOutput, calls=%fused_computation.20 | convolution fusion | flops 153944064 | bytes 11010192 | tf_op jit(solution)/shard_map/fiku,ikvu->fiv/dot_general | solution.py:11
  66.9 0.7 copy-done.1
  68.1 12.1 %gather_fusion.3 = bf16[4096,32]{1,0:T(8,128)(2,1)S(1)} fusion(bf16[32,2049]{0,1:T(8,128)(2,1)S(1)} %concatenate.24.clone, s32[4096]{0:T(1024)S(1)} %fusion.38), kind=kCustom, calls=%fused_computation.3 | custom fusion | bytes 540672 | tf_op jit(solution)/shard_map/jit(_take)/gather | solution.py:70
  80.5 0.7 broadcast_select_fusion.2
  81.3 6.3 %all-to-all-start.2 = ((bf16[32,8,512]{2,0,1:T(8,128)(2,1)}), bf16[32,8,512]{2,0,1:T(8,128)(2,1)S(1)}, u32[]{:S(2)}, u32[]{:S(2)}) async-start(bf16[32,8,512]{2,0,1:T(8,128)(2,1)} %broadcast_select_fusion.2), calls=%async_computation.2 | async-start | bytes 524288 | tf_op jit(solution)/shard_map/all_to_all | solution.py:71
  87.6 0.6 convert_element_type.35
  88.2 7.3 %all_gather.12 = bf16[128,1024]{1,0:T(8,128)(2,1)S(1)} all-gather(bf16[32,1024]{1,0:T(8,128)(2,1)S(1)} %copy-done.2), channel_id=1, replica_groups=mesh['dom'=8,'feat'=4] {'feat'}, dimensions={0}, use_global_device_ids=true | all-gather | bytes 327680 | tf_op jit(solution)/shard_map/all_gather | solution.py:25
  95.9 0.6 copy.120
  96.5 26.2 %scatter_custom_fusion.1 = f32[32,1025]{0,1:T(8,128)S(1)} fusion(s32[4096]{0:T(1024)} %bitcast.97, f32[4096,32]{1,0:T(8,128)S(1)} %copy.120, f32[]{:T(128)} %constant.106.clone.1), kind=kCustom, calls=%fused_computation.46 | custom fusion | flops 131072 | bytes 131712 | tf_op jit(solution)/shard_map/scatter-add | solution.py:75
  122.9 0.9 fusion.30
  123.9 7.0 %all_gather.13 = bf16[128,1024]{1,0:T(8,128)(2,1)S(1)} all-gather(bf16[32,1024]{1,0:T(8,128)(2,1)S(1)} %fusion.30), channel_id=1, replica_groups=mesh['dom'=8,'feat'=4] {'feat'}, dimensions={0}, use_global_device_ids=true | all-gather | bytes 327680 | tf_op jit(solution)/shard_map/all_gather | solution.py:26
  131.4 12.1 %gather_fusion.4 = bf16[4096,64]{1,0:T(8,128)(2,1)S(1)} fusion(bf16[64,1025]{0,1:T(8,128)(2,1)S(1)} %concatenate.25.clone, s32[4096]{0:T(1024)S(1)} %copy-done.6), kind=kCustom, calls=%fused_computation.4 | custom fusion | bytes 1064960 | tf_op jit(solution)/shard_map/jit(_take)/gather | solution.py:59
  144.0 17.7 %all_to_all.39 = bf16[64,8,512]{2,0,1:T(8,128)(2,1)S(1)} all-to-all(bf16[64,8,512]{2,0,1:T(8,128)(2,1)S(1)} %broadcast_select_fusion.1), channel_id=1, replica_groups=mesh['dom'=8,'feat'=4] {'dom'}, dimensions={1} | all-to-all | bytes 1048576 | tf_op jit(solution)/shard_map/all_to_all | solution.py:87
  161.7 0.5 copy.125
  162.1 6.2 %gather_fusion.5 = bf16[2048,64]{1,0:T(8,128)(2,1)S(1)} fusion(bf16[64,4096]{0,1:T(8,128)(2,1)S(1)} %bitcast.79, s32[2048]{0:T(1024)S(1)} %broadcast_clamp_fusion.1), kind=kCustom, calls=%fused_computation.5 | custom fusion | bytes 532480 | tf_op jit(solution)/shard_map/jit(_take)/gather | solution.py:62
  168.9 7.5 %gather_fusion.6 = bf16[144,64,128]{1,2,0:T(8,128)(2,1)} fusion(bf16[64,24,128]{0,2,1:T(8,128)(2,1)S(1)} %bitcast.78, s32[1024]{0:T(1024)S(1)} %pad_clamp_fusion), kind=kCustom, calls=%fused_computation.6 | custom fusion | bytes 4719168 | tf_op jit(solution)/shard_map/jit(_take)/gather | solution.py:10
  176.4 5.4 %copy.127 = bf16[144,64,128]{2,1,0:T(8,128)(2,1)S(1)} copy(bf16[144,64,128]{1,2,0:T(8,128)(2,1)} %gather_fusion.6) | data formatting | bytes 4718592 | tf_op jit(solution)/shard_map/jit(_take)/gather | solution.py:10
  181.8 5.5 %fusion.7 = f32[24,8,8,128]{3,2,1,0:T(8,128)S(1)} fusion(s32[24,6,128,128]{3,2,1,0:T(8,128)} %param.10, bf16[24,6,64,128]{3,2,1,0:T(8,128)(2,1)S(1)} %bitcast.80, pred[24,6]{1,0:T(8,128)(4,1)S(1)} %copy-done.15), kind=kOutput, calls=%fused_computation.19 | convolution fusion | flops 305528832 | bytes 12583056 | tf_op jit(solution)/shard_map/fiku,ikvu->fiv/dot_general | solution.py:11
  188.0 12.1 %gather_fusion.7 = bf16[4096,64]{1,0:T(8,128)(2,1)S(1)} fusion(bf16[64,2049]{0,1:T(8,128)(2,1)S(1)} %concatenate.27.clone, s32[4096]{0:T(1024)S(1)} %copy-done.4), kind=kCustom, calls=%fused_computation.7 | custom fusion | bytes 1064960 | tf_op jit(solution)/shard_map/jit(_take)/gather | solution.py:70
  200.5 0.9 broadcast_select_fusion
  201.4 4.6 %all-to-all-start.4 = ((bf16[64,8,512]{2,0,1:T(8,128)(2,1)}), bf16[64,8,512]{2,0,1:T(8,128)(2,1)S(1)}, u32[]{:S(2)}, u32[]{:S(2)}) async-start(bf16[64,8,512]{2,0,1:T(8,128)(2,1)} %broadcast_select_fusion), calls=%async_computation.4 | async-start | bytes 1048576 | tf_op jit(solution)/shard_map/all_to_all | solution.py:71
  206.0 8.2 %all_gather.14 = bf16[256,1024]{1,0:T(8,128)(2,1)S(1)} all-gather(bf16[64,1024]{1,0:T(8,128)(2,1)S(1)} %fusion.20), channel_id=1, replica_groups=mesh['dom'=8,'feat'=4] {'feat'}, dimensions={0}, use_global_device_ids=true | all-gather | bytes 655360 | tf_op jit(solution)/shard_map/all_gather | solution.py:25
  214.5 1.0 copy.139
  215.5 4.2 %all-to-all-done.4 = bf16[64,8,512]{2,0,1:T(8,128)(2,1)S(1)} async-done(((bf16[64,8,512]{2,0,1:T(8,128)(2,1)}), bf16[64,8,512]{2,0,1:T(8,128)(2,1)S(1)}, u32[]{:S(2)}, u32[]{:S(2)}) %all-to-all-start.4) | async-done | bytes 524320 | tf_op jit(solution)/shard_map/all_to_all | solution.py:71
  219.9 0.6 copy.133
  220.6 26.3 %scatter_custom_fusion.2 = f32[64,1025]{0,1:T(8,128)S(1)} fusion(s32[4096]{0:T(1024)} %bitcast.98, f32[4096,64]{1,0:T(8,128)S(1)} %copy.133, f32[]{:T(128)} %constant.106.clone.1), kind=kCustom, calls=%fused_computation.44 | custom fusion | flops 262144 | bytes 262912 | tf_op jit(solution)/shard_map/scatter-add | solution.py:75
  246.9 1.2 fusion.24
  248.3 8.4 %all_gather.15 = bf16[256,1024]{1,0:T(8,128)(2,1)S(1)} all-gather(bf16[64,1024]{1,0:T(8,128)(2,1)S(1)} %copy.134), channel_id=1, replica_groups=mesh['dom'=8,'feat'=4] {'feat'}, dimensions={0}, use_global_device_ids=true | all-gather | bytes 655360 | tf_op jit(solution)/shard_map/all_gather | solution.py:26
  256.7 1.0 fusion.21
  (87 shorter events, 5.5 us)
Async XLA Ops:
  0.0 214.1 %copy-start = (bf16[256,256]{1,0:T(8,128)(2,1)S(1)}, bf16[256,256]{1,0:T(8,128)(2,1)}, u32[]{:S(2)}) copy-start(bf16[256,256]{1,0:T(8,128)(2,1)} %param.16) | copy-start | bytes 393220
  11.8 16.5 %all-to-all-start = ((s32[1,8,512]{2,0,1:T(1,128)}), s32[1,8,512]{2,0,1:T(1,128)S(1)}, u32[]{:S(2)}, u32[]{:S(2)}) async-start(s32[1,8,512]{2,0,1:T(1,128)} %bitcast.3), calls=%async_computation | async-start | bytes 32768 | tf_op jit(solution)/shard_map/all_to_all | solution.py:51
  17.6 42.5 %copy-start.16 = (pred[2048]{0:T(1024)(128)(4,1)}, pred[2048]{0:T(1024)(128)(4,1)S(1)}, u32[]{:S(2)}) copy-start(pred[2048]{0:T(1024)(128)(4,1)S(1)} %compare_and_fusion.2) | copy-start | bytes 6148
  28.4 0.6 copy-start.7
  29.0 13.2 %copy-start.5 = (s32[4096]{0:T(1024)}, s32[4096]{0:T(1024)S(1)}, u32[]{:S(2)}) copy-start(s32[4096]{0:T(1024)S(1)} %broadcast_clamp_fusion) | copy-start | bytes 49156
  41.5 6.4 %copy-start.8 = (pred[8,512]{1,0:T(8,128)(4,1)}, pred[8,512]{1,0:T(8,128)(4,1)S(1)}, u32[]{:S(2)}) copy-start(pred[8,512]{1,0:T(8,128)(4,1)S(1)} %compare_and_fusion.1) | copy-start | bytes 12292
  42.2 11.1 %all-to-all-start.1 = ((bf16[32,8,512]{2,0,1:T(8,128)(2,1)}), bf16[32,8,512]{2,0,1:T(8,128)(2,1)S(1)}, u32[]{:S(2)}, u32[]{:S(2)}) async-start(bf16[32,8,512]{2,0,1:T(8,128)(2,1)} %broadcast_select_fusion.3), calls=%async_computation.1 | async-start | bytes 524288 | tf_op jit(solution)/shard_map/all_to_all | solution.py:81
  47.8 13.7 %copy-start.14 = (pred[24,6]{1,0:T(8,128)(4,1)}, pred[24,6]{1,0:T(8,128)(4,1)S(1)}, u32[]{:S(2)}) copy-start(pred[24,6]{1,0:T(8,128)(4,1)S(1)} %copy.109) | copy-start | bytes 436
  47.8 32.7 %copy-start.10 = (pred[8,512]{1,0:T(8,128)(4,1)}, pred[8,512]{1,0:T(8,128)(4,1)S(1)}, u32[]{:S(2)}) copy-start(pred[8,512]{1,0:T(8,128)(4,1)S(1)} %broadcast_in_dim.110) | copy-start | bytes 12292
  47.8 20.2 %copy-start.3 = (s32[4096]{0:T(1024)}, s32[4096]{0:T(1024)S(1)}, u32[]{:S(2)}) copy-start(s32[4096]{0:T(1024)S(1)} %fusion.38) | copy-start | bytes 49156
  47.9 12.7 %copy-start.2 = (bf16[32,1024]{1,0:T(8,128)(2,1)S(1)}, bf16[32,1024]{1,0:T(8,128)(2,1)}, u32[]{:S(2)}) copy-start(bf16[32,1024]{1,0:T(8,128)(2,1)} %param.9) | copy-start | bytes 196612
  66.9 0.7 copy-start.1
  68.1 19.5 %copy-start.20 = (s32[1024]{0:T(1024)S(1)}, s32[1024]{0:T(1024)}, u32[]{:S(2)}) copy-start(s32[1024]{0:T(1024)} %param.13) | copy-start | bytes 12292
  68.1 27.5 %copy-start.18 = (bf16[128,256]{1,0:T(8,128)(2,1)S(1)}, bf16[128,256]{1,0:T(8,128)(2,1)}, u32[]{:S(2)}) copy-start(bf16[128,256]{1,0:T(8,128)(2,1)} %param.14) | copy-start | bytes 196612
  81.3 14.5 %all-to-all-start.2 = ((bf16[32,8,512]{2,0,1:T(8,128)(2,1)}), bf16[32,8,512]{2,0,1:T(8,128)(2,1)S(1)}, u32[]{:S(2)}, u32[]{:S(2)}) async-start(bf16[32,8,512]{2,0,1:T(8,128)(2,1)} %broadcast_select_fusion.2), calls=%async_computation.2 | async-start | bytes 524288 | tf_op jit(solution)/shard_map/all_to_all | solution.py:71
  122.7 8.2 %copy-start.19 = (bf16[128,256]{1,0:T(8,128)(2,1)S(1)}, bf16[128,256]{1,0:T(8,128)(2,1)}, u32[]{:S(2)}) copy-start(bf16[128,256]{1,0:T(8,128)(2,1)} %param.15) | copy-start | bytes 196612
  122.7 8.7 %copy-start.6 = (s32[4096]{0:T(1024)S(1)}, s32[4096]{0:T(1024)}, u32[]{:S(2)}) copy-start(s32[4096]{0:T(1024)} %copy-done.5) | copy-start | bytes 49156
  131.4 12.5 %copy-start.9 = (pred[8,512]{1,0:T(8,128)(4,1)S(1)}, pred[8,512]{1,0:T(8,128)(4,1)}, u32[]{:S(2)}) copy-start(pred[8,512]{1,0:T(8,128)(4,1)} %copy-done.8) | copy-start | bytes 12292
  161.7 6.7 %copy-start.17 = (pred[2048]{0:T(1024)(128)(4,1)S(1)}, pred[2048]{0:T(1024)(128)(4,1)}, u32[]{:S(2)}) copy-start(pred[2048]{0:T(1024)(128)(4,1)} %copy-done.16) | copy-start | bytes 6148
  176.4 5.4 %copy-start.15 = (pred[24,6]{1,0:T(8,128)(4,1)S(1)}, pred[24,6]{1,0:T(8,128)(4,1)}, u32[]{:S(2)}) copy-start(pred[24,6]{1,0:T(8,128)(4,1)} %copy-done.14) | copy-start | bytes 436
  187.3 0.7 copy-start.4
  188.0 12.5 %copy-start.11 = (pred[8,512]{1,0:T(8,128)(4,1)S(1)}, pred[8,512]{1,0:T(8,128)(4,1)}, u32[]{:S(2)}) copy-start(pred[8,512]{1,0:T(8,128)(4,1)} %copy-done.10) | copy-start | bytes 12292
  201.4 18.3 %all-to-all-start.4 = ((bf16[64,8,512]{2,0,1:T(8,128)(2,1)}), bf16[64,8,512]{2,0,1:T(8,128)(2,1)S(1)}, u32[]{:S(2)}, u32[]{:S(2)}) async-start(bf16[64,8,512]{2,0,1:T(8,128)(2,1)} %broadcast_select_fusion), calls=%async_computation.4 | async-start | bytes 1048576 | tf_op jit(solution)/shard_map/all_to_all | solution.py:71
  219.9 26.9 %copy-start.12 = (f32[1024]{0:T(1024)S(1)}, f32[1024]{0:T(1024)}, u32[]{:S(2)}) copy-start(f32[1024]{0:T(1024)} %convert_element_type.35) | copy-start | bytes 12292
  220.6 36.2 %copy-start.13 = (bf16[256,256]{1,0:T(8,128)(2,1)S(1)}, bf16[256,256]{1,0:T(8,128)(2,1)}, u32[]{:S(2)}) copy-start(bf16[256,256]{1,0:T(8,128)(2,1)} %param.17) | copy-start | bytes 393220
where the time goes:
time: 260 us; the launch traced here: 258 us
  local copies, waits for them, and re-layouts  101 us (39%)
  other arithmetic  62.5 us (24%)
  blocking collectives  48.6 us (19%)
  starting transfers between devices  22.1 us (8%)
  matrix products  12.7 us (5%)
  waiting for transfers between devices  9.74 us (4%)
    scatter-add x2, other arithmetic, combine(): incoming = jnp.zeros((feature_row_block, masters + 1), jnp.float32).at[:,...  52.4 us
    gather x4, local copies, waits for them, and re-layouts, serve(): return jnp.take(padded, wanted, axis=1)  24.9 us
    gather x4, local copies, waits for them, and re-layouts, combine(): outgoing = jnp.take(padded, send_index, axis=1)  24.9 us
    all_to_all x1, blocking collectives, on_device(): lax.all_to_all(serve(hidden_master), 'dom', split_axis=1, concat_axis=1,...  17.7 us
    all_gather x2, blocking collectives, mix(): lax.all_gather(inputs, 'feat', axis=0, tiled=True)  15.5 us
    all_gather x2, blocking collectives, mix(): lax.all_gather(neighbours, 'feat', axis=0, tiled=True)  15.4 us
    gather x3, local copies, waits for them, and re-layouts, aggregate_rows(): selected = jnp.take(tiled, column_tiles, axis=1)  13.8 us
    unnamed x48, local copies, waits for them, and re-layouts  13 us
  transfers between devices with their start and end apart: 4, of which 2 were waited for; matrix products, arithmetic and copies ran while one was open for 5% of the time, Pallas kernels for 0%

commit v1 on v0

v1 whole, which is shorter than its diff:
```python
import functools

import jax
import jax.numpy as jnp
from jax import lax
from jax.experimental import pallas as pl
from jax.experimental.pallas import tpu as pltpu
from jax.sharding import PartitionSpec as P

F32 = jnp.float32
BF16 = jnp.bfloat16
I32 = jnp.int32
LANES = 128
CHUNK = 256
GROUP = 8
VMEM = pl.BlockSpec(memory_space=pltpu.VMEM)
SMEM = pl.BlockSpec(memory_space=pltpu.SMEM)


def call(body, out_shape, operands, smem=(), scratch=(), flops=0, moved=0):
    return pl.pallas_call(
        body,
        out_shape=out_shape,
        in_specs=[SMEM if i in smem else VMEM for i in range(len(operands))],
        out_specs=jax.tree.map(lambda _: VMEM, out_shape),
        scratch_shapes=list(scratch),
        compiler_params=pltpu.CompilerParams(vmem_limit_bytes=24 << 20),
        cost_estimate=pl.CostEstimate(flops=flops, bytes_accessed=moved, transcendentals=0),
    )(*operands)


def dot(left, right, dims=(1, 0)):
    return lax.dot_general(
        left, right, (((dims[0],), (dims[1],)), ((), ())), preferred_element_type=F32
    )


def one_hot(index_row, depth):
    rows = lax.broadcasted_iota(I32, (depth, index_row.shape[1]), 0)
    return (rows == index_row).astype(F32).astype(BF16)


def keep(condition, values):
    return jnp.where(condition, values, jnp.zeros_like(values))


def transpose_masks(tile_mask):
    tiles, stored, side, _ = tile_mask.shape
    step = max(d for d in (1, 2, 3, 4) if tiles % d == 0)

    def body(mask, out):
        for i in range(step):
            for k in range(stored):
                block = mask[i, k].astype(F32).T
                out[i, k * side : (k + 1) * side, :] = block.astype(BF16)

    return pl.pallas_call(
        body,
        grid=(tiles // step,),
        in_specs=[pl.BlockSpec((step, stored, side, side), lambda i: (i, 0, 0, 0))],
        out_specs=pl.BlockSpec((step, stored * side, side), lambda i: (i, 0, 0)),
        out_shape=jax.ShapeDtypeStruct((tiles, stored * side, side), BF16),
        compiler_params=pltpu.CompilerParams(vmem_limit_bytes=24 << 20),
        cost_estimate=pl.CostEstimate(flops=0, bytes_accessed=tile_mask.size * 6, transcendentals=0),
    )(tile_mask)


def slot_rows_body(dom, reps, out):
    capacity = out.shape[1]
    part, slot, row = reps[0:1, :], reps[1:2, :], reps[2:3, :]
    parts = lax.broadcasted_iota(I32, (dom, part.shape[1]), 0)
    mine = parts == part
    high = keep(mine, jnp.broadcast_to(row // CHUNK, mine.shape)).astype(F32).astype(BF16)
    low = keep(mine, jnp.broadcast_to(row % CHUNK, mine.shape)).astype(F32).astype(BF16)
    slots = one_hot(slot, capacity)
    rows = dot(high, slots, (1, 1)) * CHUNK + dot(low, slots, (1, 1))
    out[...] = rows.astype(I32)


def pick_part(groups, part, n, products):
    def one(g, total):
        found = products(g)
        for k in range(GROUP):
            total = total + keep(part == g * GROUP + k, found[k])
        return total

    return one


def partial_body(dom, dense, cols, received, own, masks, reps, own_out, out, local, mirror):
    feats = own.shape[0]
    masters = own.shape[1]
    mirrors = reps.shape[1]
    depth = received.shape[2]
    capacity = out.shape[2]
    tiles = masks.shape[0]
    stored = masks.shape[1] // LANES
    head = masters // LANES
    for i in range(head):
        local[i] = own[:, i * LANES : (i + 1) * LANES]
    for n in range(0, mirrors, CHUNK):
        part = reps[0:1, n : n + CHUNK]
        places = one_hot(reps[2:3, n : n + CHUNK] if dense else reps[1:2, n : n + CHUNK], depth)

        def add_group(g, total):
            block = received[pl.ds(g * GROUP, GROUP)].reshape(GROUP * feats, depth)
            found = dot(block, places).reshape(GROUP, feats, CHUNK)
            for k in range(GROUP):
                total = total + keep(part == g * GROUP + k, found[k])
            return total

        zero = jnp.zeros((feats, CHUNK), F32)
        if dom == GROUP:
            values = add_group(0, zero)
        else:
            values = lax.fori_loop(0, dom // GROUP, add_group, zero)
        for i in range(CHUNK // LANES):
            local[head + n // LANES + i] = values[:, i * LANES : (i + 1) * LANES].astype(BF16)
    for i in range(tiles):
        chosen = jnp.concatenate([local[cols[k, i]] for k in range(stored)], axis=1)
        summed = dot(chosen, masks[i])
        if i < head:
            own_out[:, i * LANES : (i + 1) * LANES] = summed
        else:
            at = (i - head) * LANES
            mirror[:, at : at + LANES] = summed.astype(BF16)
    slots = one_hot(reps[1:2, :], capacity)
    values = mirror[...].astype(F32)
    part = reps[0:1, :]

    def send_group(g, carry):
        spread = jnp.concatenate(
            [keep(part == g * GROUP + k, values).astype(BF16) for k in range(GROUP)], axis=0
        )
        placed = dot(spread, slots, (1, 1)).astype(BF16)
        out[pl.ds(g * GROUP, GROUP)] = placed.reshape(GROUP, feats, capacity)
        return carry

    if dom == GROUP:
        send_group(0, 0)
    else:
        lax.fori_loop(0, dom // GROUP, send_group, 0)


def partial_sums(dom, dense, cols, received, own, masks, reps, capacity):
    feats, masters = own.shape
    mirrors = reps.shape[1]
    tiles = masks.shape[0]
    return call(
        functools.partial(partial_body, dom, dense),
        (
            jax.ShapeDtypeStruct((feats, masters), F32),
            jax.ShapeDtypeStruct((dom, feats, capacity), BF16),
        ),
        (cols, received, own, masks, reps),
        smem=(0,),
        scratch=(pltpu.VMEM((tiles, feats, LANES), BF16), pltpu.VMEM((feats, mirrors), BF16)),
        flops=2 * feats * masks.size,
        moved=2 * masks.size,
    )


def mean_body(dom, received, rows, own, degree, out):
    feats, masters = own.shape
    parts = masters // CHUNK

    def add(p, total):
        row = rows[pl.ds(p, 1), :]
        values = received[p].astype(F32)
        high = row // CHUNK
        spread = jnp.concatenate([keep(high == a, values).astype(BF16) for a in range(parts)], axis=0)
        return total + dot(spread, one_hot(row % CHUNK, CHUNK), (1, 1))

    total = jnp.zeros((parts * feats, CHUNK), F32)
    if dom == GROUP:
        for p in range(dom):
            total = add(p, total)
    else:
        total = lax.fori_loop(0, dom, add, total)
    for a in range(parts):
        at = slice(a * CHUNK, (a + 1) * CHUNK)
        whole = own[:, at] + total[a * feats : (a + 1) * feats]
        out[:, at] = (whole / degree[:, at].astype(F32)).astype(BF16)


def mean(dom, received, rows, own, degree):
    feats, masters = own.shape
    return call(
        functools.partial(mean_body, dom),
        jax.ShapeDtypeStruct((feats, masters), BF16),
        (received, rows, own, degree),
        flops=2 * received.size * masters,
        moved=received.size * 2,
    )


def serve_body(dom, self_t, neigh_t, inputs, means, rows, hidden_out, out):
    result = dot(self_t[...], inputs[...]) + dot(neigh_t[...], means[...])
    hidden = jnp.maximum(result, 0.0).astype(BF16)
    hidden_out[...] = hidden
    feats, masters = hidden.shape
    parts = masters // CHUNK
    folded = jnp.concatenate([hidden[:, a * CHUNK : (a + 1) * CHUNK] for a in range(parts)], axis=0)

    def one(p, carry):
        row = rows[pl.ds(p, 1), :]
        found = dot(folded, one_hot(row % CHUNK, CHUNK))
        high = row // CHUNK
        total = jnp.zeros((feats, row.shape[1]), F32)
        for a in range(parts):
            total = total + keep(high == a, found[a * feats : (a + 1) * feats])
        out[p] = total.astype(BF16)
        return carry

    if dom == GROUP:
        for p in range(dom):
            one(p, 0)
    else:
        lax.fori_loop(0, dom, one, 0)


def serve(dom, self_t, neigh_t, inputs, means, rows):
    feats = self_t.shape[0]
    masters = inputs.shape[1]
    capacity = rows.shape[1]
    return call(
        functools.partial(serve_body, dom),
        (
            jax.ShapeDtypeStruct((feats, masters), BF16),
            jax.ShapeDtypeStruct((dom, feats, capacity), BF16),
        ),
        (self_t, neigh_t, inputs, means, rows),
        flops=2 * feats * masters * dom * capacity,
        moved=2 * feats * dom * capacity,
    )


def self_body(self_one_t, neigh_one_t, self_two_t, inputs, means, out):
    result = dot(self_one_t[...], inputs[...]) + dot(neigh_one_t[...], means[...])
    hidden = jnp.maximum(result, 0.0).astype(BF16)
    out[...] = dot(self_two_t[...], hidden)


def embed_body(neigh_two_t, means, own, out):
    out[...] = (own[...] + dot(neigh_two_t[...], means[...])).astype(BF16)


def on_device(
    features, tile_mask, tile_cols, replicas, degree, self_one, neigh_one, self_two, neigh_two
):
    dom = lax.axis_size("dom")
    feat = lax.axis_size("feat")
    masters = features.shape[1]
    mirrors = replicas.shape[1]
    capacity = -(-(2 * mirrors // dom) // LANES) * LANES
    cols = tile_cols.T
    degree = degree.reshape(1, masters)

    def exchange(blocks):
        return lax.all_to_all(blocks, "dom", split_axis=0, concat_axis=0, tiled=True)

    def own_rows(weights):
        width = weights.shape[1] // feat
        start = lax.axis_index("feat") * width
        return lax.dynamic_slice_in_dim(weights, start, width, 1).T

    spread = exchange(jnp.broadcast_to(features[None], (dom,) + features.shape))
    slot_rows = call(
        functools.partial(slot_rows_body, dom),
        jax.ShapeDtypeStruct((dom, capacity), I32),
        (replicas,),
        flops=4 * dom * mirrors * capacity,
        moved=12 * mirrors,
    )
    rows = exchange(slot_rows)
    whole_in = lax.all_gather(features, "feat", axis=0, tiled=True)
    masks = transpose_masks(tile_mask)
    self_one_t, neigh_one_t = own_rows(self_one), own_rows(neigh_one)
    self_two_t, neigh_two_t = own_rows(self_two), own_rows(neigh_two)

    own_one, outgoing_one = partial_sums(
        dom, True, cols, spread, features, masks, replicas, capacity
    )
    mean_one = mean(dom, exchange(outgoing_one), rows, own_one, degree)
    whole_one = lax.all_gather(mean_one, "feat", axis=0, tiled=True)
    hidden, asked = serve(dom, self_one_t, neigh_one_t, whole_in, whole_one, rows)
    hidden_mirrors = exchange(asked)
    self_part = call(
        self_body,
        jax.ShapeDtypeStruct((self_two_t.shape[0], masters), F32),
        (self_one.T, neigh_one.T, self_two_t, whole_in, whole_one),
        flops=2 * masters * (2 * self_one.size + self_two_t.size),
        moved=masters * 1024,
    )
    own_two, outgoing_two = partial_sums(
        dom, False, cols, hidden_mirrors, hidden, masks, replicas, capacity
    )
    mean_two = mean(dom, exchange(outgoing_two), rows, own_two, degree)
    whole_two = lax.all_gather(mean_two, "feat", axis=0, tiled=True)
    return call(
        embed_body,
        jax.ShapeDtypeStruct((neigh_two_t.shape[0], masters), BF16),
        (neigh_two_t, whole_two, self_part),
        flops=2 * masters * neigh_two_t.size,
        moved=masters * 1024,
    )


def solution(mesh):
    return jax.shard_map(
        on_device,
        mesh=mesh,
        in_specs=(
            P("feat", "dom"),
            P("dom", None, None, None),
            P("dom", None),
            P(None, "dom"),
            P("dom"),
            P(),
            P(),
            P(),
            P(),
        ),
        out_specs=P("feat", "dom"),
        check_vma=False,
    )
```

time: 260 us -> 115 us (0.44)
  local copies, waits for them, and re-layouts: 101 us -> 11.9 us
  other arithmetic: 62.5 us -> 0 us
  Pallas kernels: 0 us -> 16.4 us
  waiting for transfers between devices: 9.74 us -> 24 us
  matrix products: 12.7 us -> 0 us
  blocking collectives: 48.6 us -> 40.4 us
    gather x13 -> x0, local copies, waits for them, and re-layouts: 75.9 us -> none  [the longest x4 24.9 us: serve(): return jnp.take(padded, wanted, axis=1)]
    scatter-add x2 -> x0, other arithmetic: 52.4 us -> none  [combine(): incoming = jnp.zeros((feature_row_block, masters + 1), jnp.float32).at[:,...]
    pallas_call x0 -> x9, Pallas kernels: none -> 16.4 us  [the longest x8 14.7 us: call(): pl.pallas_call(body, out_shape=out_shape, in_specs=[SMEM if i in smem els...]
    all_to_all x4, waiting for transfers between devices: 9.74 us -> 24 us  [exchange(): lax.all_to_all(blocks, 'dom', split_axis=0, concat_axis=0, tiled=True)]
    dot_general x6 -> x0, matrix products: 12.7 us -> none  [the longest x2 10.9 us: aggregate_rows(): jnp.einsum('fiku,ikvu->fiv', selected, masks_bf, preferred_element_type=j...]
    scatter x1 -> x0, local copies, waits for them, and re-layouts: 8.06 us -> none  [on_device(): send_index = jnp.full((slot_count,), mirrors, jnp.int32).at[position].set...]
    all_gather x4 -> x3, blocking collectives: 30.9 us -> 23.4 us  [the longest x1 8.45 us: on_device(): whole_two = lax.all_gather(mean_two, 'feat', axis=0, tiled=True)]
    select_n x9 -> x0, other arithmetic: 4.63 us -> none  [the longest x2 1.59 us: combine(): outgoing = jnp.take(padded, send_index, axis=1)]
  transfers between devices with their start and end apart: 4 -> 4, of which waited for: 2 -> 2; matrix products, arithmetic and copies ran while one was open for 5% -> 1% of each run, Pallas kernels for 0% -> 7%
where the time goes in v1:
time: 115 us; the launch traced here: 113 us
  blocking collectives  40.4 us (35%)
  waiting for transfers between devices  24 us (21%)
  starting transfers between devices  20.4 us (18%)
  Pallas kernels  16.4 us (14%)
  local copies, waits for them, and re-layouts  11.9 us (10%)
    all_to_all x4, waiting for transfers between devices, exchange(): lax.all_to_all(blocks, 'dom', split_axis=0, concat_axis=0, tiled=True)  24 us
    all_to_all x4, starting transfers between devices, exchange(): lax.all_to_all(blocks, 'dom', split_axis=0, concat_axis=0, tiled=True)  20.4 us
    all_to_all x1, blocking collectives, exchange(): lax.all_to_all(blocks, 'dom', split_axis=0, concat_axis=0, tiled=True)  17 us
    pallas_call x8, Pallas kernels, call(): pl.pallas_call(body, out_shape=out_shape, in_specs=[SMEM if i in smem els...  14.7 us
    unnamed x29, local copies, waits for them, and re-layouts  9.35 us
    all_gather x1, blocking collectives, on_device(): whole_two = lax.all_gather(mean_two, 'feat', axis=0, tiled=True)  8.45 us
    all_gather x1, blocking collectives, on_device(): whole_one = lax.all_gather(mean_one, 'feat', axis=0, tiled=True)  7.71 us
    all_gather x1, blocking collectives, on_device(): whole_in = lax.all_gather(features, 'feat', axis=0, tiled=True)  7.24 us
  transfers between devices with their start and end apart: 4, of which 2 were waited for; matrix products, arithmetic and copies ran while one was open for 1% of the time, Pallas kernels for 7%

profile of v1, /device:TPU:5, one launch (start us, length us, event | category | flops | bytes accessed | tf_op | source)
XLA Modules:
  0.0 113.2 jit_solution(4230919861187319469)
XLA Ops:
  0.0 0.0 copy-start.3
  0.0 0.0 copy-start.5
  0.0 0.0 copy-start.6
  0.0 1.8 %broadcast_in_dim.2 = bf16[8,32,1024]{2,1,0:T(8,128)(2,1)} broadcast(bf16[32,1024]{1,0:T(8,128)(2,1)} %own.1), dimensions={1,2} | broadcast | bytes 589824 | tf_op jit(solution)/shard_map/broadcast_in_dim | solution.py:267
  1.8 5.8 %all-to-all-start = ((bf16[8,32,1024]{2,1,0:T(8,128)(2,1)}), bf16[8,32,1024]{2,1,0:T(8,128)(2,1)S(1)}, u32[]{:S(2)}, u32[]{:S(2)}) async-start(bf16[8,32,1024]{2,1,0:T(8,128)(2,1)} %broadcast_in_dim.2), calls=%async_computation | async-start | bytes 1048576 | tf_op jit(solution)/shard_map/all_to_all | solution.py:260
  7.6 0.0 copy-start.4
  7.6 0.8 copy-done.4
  8.3 1.2 %shard_map.93 = s32[8,512]{1,0:T(8,128)S(1)} custom-call(s32[3,2048]{1,0:T(4,128)S(1)} %copy-done.4), custom_call_target="tpu_custom_call" | custom-call | flops 33554432 | bytes 24576 | tf_op jit(solution)/shard_map/pallas_call | solution.py:21
  9.5 0.6 copy.19
  10.2 11.1 %all-to-all-done.received = bf16[8,32,1024]{2,1,0:T(8,128)(2,1)S(1)} async-done(((bf16[8,32,1024]{2,1,0:T(8,128)(2,1)}), bf16[8,32,1024]{2,1,0:T(8,128)(2,1)S(1)}, u32[]{:S(2)}, u32[]{:S(2)}) %all-to-all-start) | async-done | bytes 524320 | tf_op jit(solution)/shard_map/all_to_all | solution.py:260
  21.3 4.6 %all-to-all-start.2 = ((s32[8,1,512]{2,1,0:T(1,128)}), s32[8,1,512]{2,1,0:T(1,128)S(1)}, u32[]{:S(2)}, u32[]{:S(2)}) async-start(s32[8,1,512]{2,1,0:T(1,128)} %copy.19), calls=%async_computation.2 | async-start | bytes 32768 | tf_op jit(solution)/shard_map/all_to_all | solution.py:260
  25.9 0.0 copy-start.2
  25.9 3.7 %copy-done.2 = s32[24,6,128,128]{3,2,1,0:T(8,128)S(1)} copy-done((s32[24,6,128,128]{3,2,1,0:T(8,128)S(1)}, s32[24,6,128,128]{3,2,1,0:T(8,128)}, u32[]{:S(2)}) %copy-start.2) | copy-done | bytes 9437208
  29.5 0.0 copy-start.8
  29.5 1.7 %shard_map.91.masks = bf16[24,768,128]{2,1,0:T(8,128)(2,1)S(1)} custom-call(s32[24,6,128,128]{3,2,1,0:T(8,128)S(1)} %copy-done.2), custom_call_target="tpu_custom_call" | custom-call | bytes 14155776 | tf_op jit(solution)/shard_map/pallas_call | solution.py:57
  31.3 0.0 copy-start.10
  31.3 0.0 copy-start.11
  31.3 0.0 copy-done.3
  31.3 0.0 copy-done.5
  31.3 0.0 copy-done.6
  31.3 4.4 %shard_map.92 = (f32[32,1024]{1,0:T(8,128)S(1)}, bf16[8,32,512]{2,1,0:T(8,128)(2,1)}) custom-call(s32[6,24]{1,0:T(8,128)S(1)} %bitcast.18, bf16[8,32,1024]{2,1,0:T(8,128)(2,1)S(1)} %all-to-all-done.received, bf16[32,1024]{1,0:T(8,128)(2,1)S(1)} %copy-done.3, bf16[24,768,128]{2,1,0:T(8,128)(2,1)S(1)} %shard_map.91.masks, s32[3,2048]{1,0:T(4,128)S(1)} %copy-done.5), custom_call_target="tpu_custom_call" | custom-call | flops 150994944 | bytes 4718592 | tf_op jit(solution)/shard_map/pallas_call | solution.py:21
  35.7 2.1 %copy-done = bf16[24,768,128]{2,1,0:T(8,128)(2,1)} copy-done((bf16[24,768,128]{2,1,0:T(8,128)(2,1)}, bf16[24,768,128]{2,1,0:T(8,128)(2,1)S(1)}, u32[]{:S(2)}) %copy-start) | copy-done | bytes 4718616
  37.8 0.0 all-to-all-done.2
  37.8 5.4 %all-to-all-start.1 = ((bf16[8,32,512]{2,1,0:T(8,128)(2,1)}), bf16[8,32,512]{2,1,0:T(8,128)(2,1)S(1)}, u32[]{:S(2)}, u32[]{:S(2)}) async-start(bf16[8,32,512]{2,1,0:T(8,128)(2,1)} %get-tuple-element.11), calls=%async_computation.1 | async-start | bytes 524288 | tf_op jit(solution)/shard_map/all_to_all | solution.py:260
  43.3 0.0 copy-done.8
  43.3 0.1 copy.17
  43.4 0.0 copy-done.9
  43.4 0.1 copy.18
  43.5 7.2 %all_gather.9.inputs = bf16[128,1024]{1,0:T(8,128)(2,1)S(1)} all-gather(bf16[32,1024]{1,0:T(8,128)(2,1)S(1)} %copy-done.3), channel_id=1, replica_groups=mesh['dom'=8,'feat'=4] {'feat'}, dimensions={0}, use_global_device_ids=true | all-gather | bytes 327680 | tf_op jit(solution)/shard_map/all_gather | solution.py:276
  50.8 0.0 all-to-all-done.1.received
  50.8 0.0 copy-done.7
  50.8 0.8 shard_map.94
  51.6 7.7 %all_gather.10.means = bf16[128,1024]{1,0:T(8,128)(2,1)S(1)} all-gather(bf16[32,1024]{1,0:T(8,128)(2,1)S(1)} %shard_map.94), channel_id=1, replica_groups=mesh['dom'=8,'feat'=4] {'feat'}, dimensions={0}, use_global_device_ids=true | all-gather | bytes 327680 | tf_op jit(solution)/shard_map/all_gather | solution.py:285
  59.3 1.3 %shard_map.95 = (bf16[64,1024]{1,0:T(8,128)(2,1)S(1)}, bf16[8,64,512]{2,1,0:T(8,128)(2,1)S(1)}) custom-call(bf16[64,128]{1,0:T(8,128)(2,1)S(1)} %get-tuple-element.18.self_t, bf16[64,128]{1,0:T(8,128)(2,1)S(1)} %get-tuple-element.17.neigh_t, bf16[128,1024]{1,0:T(8,128)(2,1)S(1)} %all_gather.9.inputs, bf16[128,1024]{1,0:T(8,128)(2,1)S(1)} %all_gather.10.means, ...), custom_call_target="tpu_custom_call" | custom-call | flops 536870912 | bytes 524288 | tf_op jit(solution)/shard_map/pallas_call | solution.py:21
  60.7 17.0 %all_to_all.31.received = bf16[8,64,512]{2,1,0:T(8,128)(2,1)S(1)} all-to-all(bf16[8,64,512]{2,1,0:T(8,128)(2,1)S(1)} %get-tuple-element.13), channel_id=1, replica_groups=mesh['dom'=8,'feat'=4] {'dom'}, dimensions={0} | all-to-all | bytes 1048576 | tf_op jit(solution)/shard_map/all_to_all | solution.py:260
  77.6 2.3 %copy-done.1 = bf16[24,768,128]{2,1,0:T(8,128)(2,1)S(1)} copy-done((bf16[24,768,128]{2,1,0:T(8,128)(2,1)S(1)}, bf16[24,768,128]{2,1,0:T(8,128)(2,1)}, u32[]{:S(2)}) %copy-start.1) | copy-done | bytes 4718616
  80.0 4.8 %shard_map.96 = (f32[64,1024]{1,0:T(8,128)S(1)}, bf16[8,64,512]{2,1,0:T(8,128)(2,1)}) custom-call(s32[6,24]{1,0:T(8,128)S(1)} %bitcast.19, bf16[8,64,512]{2,1,0:T(8,128)(2,1)S(1)} %all_to_all.31.received, bf16[64,1024]{1,0:T(8,128)(2,1)S(1)} %get-tuple-element.14.own, bf16[24,768,128]{2,1,0:T(8,128)(2,1)S(1)} %copy-done.1, s32[3,2048]{1,0:T(4,128)S(1)} %copy-done.5), custom_call_target="tpu_custom_call" | custom-call | flops 301989888 | bytes 4718592 | tf_op jit(solution)/shard_map/pallas_call | solution.py:21
  84.7 4.6 %all-to-all-start.4 = ((bf16[8,64,512]{2,1,0:T(8,128)(2,1)}), bf16[8,64,512]{2,1,0:T(8,128)(2,1)S(1)}, u32[]{:S(2)}, u32[]{:S(2)}) async-start(bf16[8,64,512]{2,1,0:T(8,128)(2,1)} %get-tuple-element.15), calls=%async_computation.4 | async-start | bytes 1048576 | tf_op jit(solution)/shard_map/all_to_all | solution.py:260
  89.4 0.0 copy-done.10
  89.4 0.0 copy-done.11
  89.4 0.1 constant_dynamic-slice_fusion
  89.5 0.1 copy.25
  89.6 0.1 copy.24
  89.7 0.6 shard_map.98.own
  90.2 12.8 %all-to-all-done.4.received = bf16[8,64,512]{2,1,0:T(8,128)(2,1)S(1)} async-done(((bf16[8,64,512]{2,1,0:T(8,128)(2,1)}), bf16[8,64,512]{2,1,0:T(8,128)(2,1)S(1)}, u32[]{:S(2)}, u32[]{:S(2)}) %all-to-all-start.4) | async-done | bytes 524320 | tf_op jit(solution)/shard_map/all_to_all | solution.py:260
  103.1 0.8 shard_map.97
  103.8 8.4 %all_gather.11.means = bf16[256,1024]{1,0:T(8,128)(2,1)S(1)} all-gather(bf16[64,1024]{1,0:T(8,128)(2,1)S(1)} %shard_map.97), channel_id=1, replica_groups=mesh['dom'=8,'feat'=4] {'feat'}, dimensions={0}, use_global_device_ids=true | all-gather | bytes 655360 | tf_op jit(solution)/shard_map/all_gather | solution.py:299
  112.3 0.9 shard_map.99
  (6 shorter events, 0.0 us)
Async XLA Ops:
  0.0 31.3 %copy-start.3 = (bf16[32,1024]{1,0:T(8,128)(2,1)S(1)}, bf16[32,1024]{1,0:T(8,128)(2,1)}, u32[]{:S(2)}) copy-start(bf16[32,1024]{1,0:T(8,128)(2,1)} %own.1) | copy-start | bytes 196612
  0.0 31.3 %copy-start.5 = (s32[3,2048]{1,0:T(4,128)S(1)}, s32[3,2048]{1,0:T(4,128)}, u32[]{:S(2)}) copy-start(s32[3,2048]{1,0:T(4,128)} %reps.5) | copy-start | bytes 73732
  0.0 31.3 %copy-start.6 = (s32[24,6]{0,1:T(8,128)S(1)}, s32[24,6]{0,1:T(8,128)}, u32[]{:S(2)}) copy-start(s32[24,6]{0,1:T(8,128)} %param.11) | copy-start | bytes 1732
  1.8 19.5 %all-to-all-start = ((bf16[8,32,1024]{2,1,0:T(8,128)(2,1)}), bf16[8,32,1024]{2,1,0:T(8,128)(2,1)S(1)}, u32[]{:S(2)}, u32[]{:S(2)}) async-start(bf16[8,32,1024]{2,1,0:T(8,128)(2,1)} %broadcast_in_dim.2), calls=%async_computation | async-start | bytes 1048576 | tf_op jit(solution)/shard_map/all_to_all | solution.py:260
  7.6 0.8 copy-start.4
  21.3 16.6 %all-to-all-start.2 = ((s32[8,1,512]{2,1,0:T(1,128)}), s32[8,1,512]{2,1,0:T(1,128)S(1)}, u32[]{:S(2)}, u32[]{:S(2)}) async-start(s32[8,1,512]{2,1,0:T(1,128)} %copy.19), calls=%async_computation.2 | async-start | bytes 32768 | tf_op jit(solution)/shard_map/all_to_all | solution.py:260
  25.9 3.7 %copy-start.2 = (s32[24,6,128,128]{3,2,1,0:T(8,128)S(1)}, s32[24,6,128,128]{3,2,1,0:T(8,128)}, u32[]{:S(2)}) copy-start(s32[24,6,128,128]{3,2,1,0:T(8,128)} %mask.1) | copy-start | bytes 28311556
  29.5 13.7 %copy-start.8 = (bf16[128,256]{1,0:T(8,128)(2,1)S(1)}, bf16[128,256]{1,0:T(8,128)(2,1)}, u32[]{:S(2)}) copy-start(bf16[128,256]{1,0:T(8,128)(2,1)} %param.14) | copy-start | bytes 196612
  29.5 13.9 %copy-start.9 = (bf16[128,256]{1,0:T(8,128)(2,1)S(1)}, bf16[128,256]{1,0:T(8,128)(2,1)}, u32[]{:S(2)}) copy-start(bf16[128,256]{1,0:T(8,128)(2,1)} %param.15) | copy-start | bytes 196612
  29.5 21.2 %copy-start.7 = (s32[1024]{0:T(1024)S(1)}, s32[1024]{0:T(1024)}, u32[]{:S(2)}) copy-start(s32[1024]{0:T(1024)} %param.13) | copy-start | bytes 12292
  31.3 58.1 %copy-start.10 = (bf16[256,256]{1,0:T(8,128)(2,1)S(1)}, bf16[256,256]{1,0:T(8,128)(2,1)}, u32[]{:S(2)}) copy-start(bf16[256,256]{1,0:T(8,128)(2,1)} %param.16) | copy-start | bytes 393220
  31.3 58.1 %copy-start.11 = (bf16[256,256]{1,0:T(8,128)(2,1)S(1)}, bf16[256,256]{1,0:T(8,128)(2,1)}, u32[]{:S(2)}) copy-start(bf16[256,256]{1,0:T(8,128)(2,1)} %param.17) | copy-start | bytes 393220
  35.7 2.1 %copy-start = (bf16[24,768,128]{2,1,0:T(8,128)(2,1)}, bf16[24,768,128]{2,1,0:T(8,128)(2,1)S(1)}, u32[]{:S(2)}) copy-start(bf16[24,768,128]{2,1,0:T(8,128)(2,1)S(1)} %shard_map.91.masks) | copy-start | bytes 14155780
  37.8 12.9 %all-to-all-start.1 = ((bf16[8,32,512]{2,1,0:T(8,128)(2,1)}), bf16[8,32,512]{2,1,0:T(8,128)(2,1)S(1)}, u32[]{:S(2)}, u32[]{:S(2)}) async-start(bf16[8,32,512]{2,1,0:T(8,128)(2,1)} %get-tuple-element.11), calls=%async_computation.1 | async-start | bytes 524288 | tf_op jit(solution)/shard_map/all_to_all | solution.py:260
  77.6 2.3 %copy-start.1 = (bf16[24,768,128]{2,1,0:T(8,128)(2,1)S(1)}, bf16[24,768,128]{2,1,0:T(8,128)(2,1)}, u32[]{:S(2)}) copy-start(bf16[24,768,128]{2,1,0:T(8,128)(2,1)} %copy-done) | copy-start | bytes 14155780
  84.7 18.3 %all-to-all-start.4 = ((bf16[8,64,512]{2,1,0:T(8,128)(2,1)}), bf16[8,64,512]{2,1,0:T(8,128)(2,1)S(1)}, u32[]{:S(2)}, u32[]{:S(2)}) async-start(bf16[8,64,512]{2,1,0:T(8,128)(2,1)} %get-tuple-element.15), calls=%async_computation.4 | async-start | bytes 1048576 | tf_op jit(solution)/shard_map/all_to_all | solution.py:260

commit v2 on v0

v2 whole, which is shorter than its diff:
```python
import functools

import jax
import jax.numpy as jnp
from jax import lax
from jax.experimental import pallas as pl
from jax.experimental.pallas import tpu as pltpu
from jax.sharding import PartitionSpec as P

F32 = jnp.float32
BF16 = jnp.bfloat16
I32 = jnp.int32
MASK = jnp.float8_e4m3fn
LANES = 128
SHIFT = 8
CHUNK = 1 << SHIFT
GROUP = 8
ORDER = (5, 2, 3, 7, 1, 0, 4, 6)
INDEX_ROWS = 16
VMEM = pl.BlockSpec(memory_space=pltpu.VMEM)
SMEM = pl.BlockSpec(memory_space=pltpu.SMEM)
HBM = pl.BlockSpec(memory_space=pltpu.HBM)
PIECES = 4
MASK_PIECES = 8
SPARE = 10


def call(body, out_shape, operands, smem=(), hbm=(), hbm_out=(), scratch=(), flops=0, moved=0, limit=20):
    def place(i):
        return SMEM if i in smem else HBM if i in hbm else VMEM

    return pl.pallas_call(
        body,
        out_shape=out_shape,
        in_specs=[place(i) for i in range(len(operands))],
        out_specs=(
            tuple(HBM if i in hbm_out else VMEM for i in range(len(out_shape)))
            if isinstance(out_shape, tuple)
            else VMEM
        ),
        scratch_shapes=list(scratch),
        compiler_params=pltpu.CompilerParams(vmem_limit_bytes=limit << 20),
        cost_estimate=pl.CostEstimate(flops=flops, bytes_accessed=moved, transcendentals=0),
    )(*operands)


def dot(left, right, dims=(1, 0)):
    return lax.dot_general(
        left, right, (((dims[0],), (dims[1],)), ((), ())), preferred_element_type=F32
    )


def one_hot(index_row, depth):
    side = min(depth, CHUNK)
    n = index_row.shape[1]
    rows = lax.broadcasted_iota(I32, (side, n), 0).astype(F32).astype(BF16)
    blocks = []
    for start in range(0, depth, side):
        here = (index_row >= start) & (index_row < start + side)
        spot = jnp.where(here, index_row - start, -1).astype(F32).astype(BF16)
        blocks.append(jnp.where(rows == spot, jnp.ones_like(rows), jnp.zeros_like(rows)))
    return blocks[0] if len(blocks) == 1 else jnp.concatenate(blocks, axis=0)


def keep(condition, values):
    return jnp.where(condition, values, jnp.zeros_like(values))


def loop(count, body, carry):
    if count <= GROUP:
        for i in range(count):
            carry = body(i, carry)
        return carry
    return lax.fori_loop(0, count, body, carry)


def masks_body(tile_mask, out, blocks, arrived):
    tiles, stored, side, _ = blocks.shape
    copies = fetch(tile_mask, blocks, arrived)
    step = tiles // len(copies)
    for i in range(tiles):
        if i % step == 0:
            copies[i // step].wait()
        for k in range(stored):
            block = blocks[i, k].astype(F32).astype(BF16)
            out[i, k * side : (k + 1) * side, :] = block.T


def transpose_masks(tile_mask):
    tiles, stored, side, _ = tile_mask.shape
    return call(
        masks_body,
        jax.ShapeDtypeStruct((tiles, stored * side, side), BF16),
        (tile_mask,),
        hbm=(0,),
        limit=47,
        scratch=(
            pltpu.VMEM(tile_mask.shape, I32),
            pltpu.SemaphoreType.DMA((MASK_PIECES,)),
        ),
        moved=6 * tile_mask.size,
    )


def index_rows(part, row, slot_places, names):
    blocks = slot_places.shape[0] // LANES
    name = lax.broadcasted_iota(I32, (len(names), 1), 0)
    for k, q in enumerate(names):
        name = jnp.where(lax.broadcasted_iota(I32, (len(names), 1), 0) == k, q, name)
    mine = jnp.broadcast_to(name, (len(names), part.shape[1])) == part
    digits = [keep(mine, jnp.broadcast_to(d, mine.shape)) for d in (row >> SHIFT, row & (CHUNK - 1))]
    digits = jnp.concatenate(digits, axis=0).astype(F32).astype(BF16)
    found = dot(digits, slot_places, (1, 1))
    out = []
    for k in range(len(names)):
        pieces = [
            found[at : at + 1, b * LANES : (b + 1) * LANES]
            for at in (k, len(names) + k)
            for b in range(blocks)
        ]
        pieces.append(jnp.zeros((INDEX_ROWS - len(pieces), LANES), F32))
        out.append(jnp.concatenate(pieces, axis=0).astype(BF16))
    return out


def pick(blocks, names, spots, part, feats):
    found = dot(jnp.concatenate(blocks, axis=0), spots)
    total = jnp.zeros((feats, spots.shape[1]), F32)
    for k, name in enumerate(names):
        total = total + keep(part == name, found[k * feats : (k + 1) * feats])
    return total


def pick_all(order, received, spots, part, feats):
    dom = received.shape[0]
    if dom == GROUP:
        return pick([received[k] for k in range(dom)], order, spots, part, feats)

    def add_group(g, total):
        blocks = [received[g * GROUP + k] for k in range(GROUP)]
        return total + pick(blocks, range(GROUP), spots, part - g * GROUP, feats)

    return lax.fori_loop(0, dom // GROUP, add_group, jnp.zeros((feats, spots.shape[1]), F32))


def fetch(source, target, arrived):
    pieces = arrived.shape[0]
    step = target.shape[0] // pieces
    copies = []
    for i in range(pieces):
        at = pl.ds(i * step, step)
        copies.append(pltpu.make_async_copy(source.at[at], target.at[at], arrived.at[i]))
        copies[-1].start()
    return copies


def aggregate(cols, local, masks, head, own_out, mirror, narrow=None):
    stored = masks.shape[1] // LANES
    for i in range(masks.shape[0]):
        chosen = jnp.concatenate([local[cols[k, i]] for k in range(stored)], axis=1)
        row = masks[i]
        if narrow is not None:
            narrow[i] = row.astype(MASK)
        summed = dot(chosen, row.astype(BF16))
        if i < head:
            own_out[:, i * LANES : (i + 1) * LANES] = summed
        else:
            at = (i - head) * LANES
            mirror[:, at : at + LANES] = summed.astype(BF16)


def send(order, mirror, reps, out, with_index):
    feats = mirror.shape[0]
    dom = out.shape[0]
    rows = out.shape[1] // feats * feats
    blocks = rows // feats
    part, slot, row = reps[0:1, :], reps[1:2, :], reps[2:3, :]
    slot_places = one_hot(slot, blocks * LANES)
    values = mirror[...]

    def group(first, names, part):
        spread = jnp.concatenate([keep(part == name, values) for name in names], axis=0)
        placed = dot(spread, slot_places, (1, 1)).astype(BF16)
        for k in range(GROUP):
            for b in range(blocks):
                block = placed[k * feats : (k + 1) * feats, b * LANES : (b + 1) * LANES]
                out[first + k, b * feats : (b + 1) * feats, :] = block
        if with_index:
            for k, index in enumerate(index_rows(part, row, slot_places, names)):
                out[first + k, rows:, :] = index

    if dom == GROUP:
        group(0, order, part)
    else:

        def one(g, carry):
            group(g * GROUP, range(GROUP), part - g * GROUP)
            return carry

        lax.fori_loop(0, dom // GROUP, one, 0)


def first_body(order, cols, own, masks, reps, *refs):
    received = refs[:-8]
    own_out, all_out, out, kept, local, mirror, narrow, written = refs[-8:]
    feats, masters = own.shape
    head = masters // LANES
    for i in range(head):
        local[i] = own[:, i * LANES : (i + 1) * LANES]
    for n in range(0, reps.shape[1], CHUNK):
        at = slice(n, n + CHUNK)
        spots = one_hot(reps[2:3, at], masters)
        part = reps[0:1, at]
        if len(received) == 1:
            values = pick_all(order, received[0], spots, part, feats)
        else:
            part = part ^ lax.axis_index("dom")
            blocks = [ref[...] for ref in received]
            values = pick(blocks, range(1, len(blocks) + 1), spots, part, feats)
        values = values.astype(BF16)
        all_out[:, at] = values
        for i in range(CHUNK // LANES):
            local[head + n // LANES + i] = values[:, i * LANES : (i + 1) * LANES]
    aggregate(cols, local, masks, head, own_out, mirror, narrow)
    copy = pltpu.make_async_copy(narrow, kept.at[pl.ds(0, masks.shape[0])], written)
    copy.start()
    send(order, mirror, reps, out, True)
    copy.wait()


def first_sums(order, cols, received, own, masks, reps, capacity):
    feats, masters = own.shape
    mirrors = reps.shape[1]
    rows = capacity // LANES * feats + INDEX_ROWS
    tiles = masks.shape[0]
    return call(
        functools.partial(first_body, order),
        (
            jax.ShapeDtypeStruct((feats, masters), F32),
            jax.ShapeDtypeStruct((feats, mirrors), BF16),
            jax.ShapeDtypeStruct((len(order), rows, LANES), BF16),
            jax.ShapeDtypeStruct((SPARE * tiles,) + masks.shape[1:], MASK),
        ),
        (cols, own, masks, reps) + received,
        smem=(0,),
        hbm_out=(3,),
        limit=44,
        scratch=(
            pltpu.VMEM((tiles, feats, LANES), BF16),
            pltpu.VMEM((feats, mirrors), BF16),
            pltpu.VMEM(masks.shape, MASK),
            pltpu.SemaphoreType.DMA,
        ),
        flops=2 * feats * masks.size,
        moved=2 * masks.size,
    )


def message(received, p, feats, blocks):
    return jnp.concatenate([received[p, b * feats : (b + 1) * feats, :] for b in range(blocks)], axis=1)


def add_mirrors(dom, received, high, low, feats, blocks, masters):
    parts = masters // CHUNK

    def add(p, total):
        values = message(received, p, feats, blocks)
        spread = jnp.concatenate([keep(high(p) == a, values) for a in range(parts)], axis=0)
        return total + dot(spread, one_hot(low(p), CHUNK), (1, 1))

    return loop(dom, add, jnp.zeros((parts * feats, CHUNK), F32))


def divide(total, own, degree, out):
    feats, masters = own.shape
    for a in range(masters // CHUNK):
        at = slice(a * CHUNK, (a + 1) * CHUNK)
        whole = own[:, at] + total[a * feats : (a + 1) * feats]
        out[:, at] = (whole / degree[:, at].astype(F32)).astype(BF16)


def first_mean_body(received, features, own, degree, out, asked, rows_out, mean):
    feats, masters = own.shape
    dom, capacity = rows_out.shape
    blocks = capacity // LANES
    parts = masters // CHUNK

    def rows(p, carry):
        coded = received[p, blocks * feats :, :].astype(F32).astype(I32)
        high = jnp.concatenate([coded[b : b + 1] for b in range(blocks)], axis=1)
        low = jnp.concatenate([coded[blocks + b : blocks + b + 1] for b in range(blocks)], axis=1)
        rows_out[pl.ds(p, 1), :] = high * CHUNK + low
        return carry

    loop(dom, rows, 0)

    def high(p):
        return rows_out[pl.ds(p, 1), :] >> SHIFT

    def low(p):
        return rows_out[pl.ds(p, 1), :] & (CHUNK - 1)

    total = add_mirrors(dom, received, high, low, feats, blocks, masters)
    divide(total, own, degree, mean)
    folded = jnp.concatenate([mean[:, a * CHUNK : (a + 1) * CHUNK] for a in range(parts)], axis=0)

    def one(p, carry):
        found = dot(folded, one_hot(low(p), CHUNK))
        chosen = jnp.zeros((feats, capacity), F32)
        for a in range(parts):
            chosen = chosen + keep(high(p) == a, found[a * feats : (a + 1) * feats])
        asked[p] = chosen.astype(BF16)
        return carry

    loop(dom, one, 0)
    out[:feats] = features[...]
    out[feats:] = mean[...]


def first_mean(dom, received, features, own, degree, capacity):
    feats, masters = own.shape
    return call(
        first_mean_body,
        (
            jax.ShapeDtypeStruct((2 * feats, masters), BF16),
            jax.ShapeDtypeStruct((dom, feats, capacity), BF16),
            jax.ShapeDtypeStruct((dom, capacity), I32),
        ),
        (received, features, own, degree),
        scratch=(pltpu.VMEM((feats, masters), BF16),),
        flops=2 * received.size * masters,
        moved=received.size * 2,
    )


def collect_body(order, received, reps, masks_hbm, out, masks, arrived):
    copies = fetch(masks_hbm, masks, arrived)
    feats = out.shape[0]
    for n in range(0, reps.shape[1], CHUNK):
        at = slice(n, n + CHUNK)
        spots = one_hot(reps[1:2, at], received.shape[2])
        out[:, at] = pick_all(order, received, spots, reps[0:1, at], feats).astype(BF16)
    for copy in copies:
        copy.wait()


def hidden_body(weights_t, own_t, self_own_t, self_two_own, inputs, mirrors, own_out, mirror_out, self_out):
    own_out[...] = jnp.maximum(dot(own_t[...], inputs[...]), 0.0).astype(BF16)
    mirror_out[...] = dot(self_own_t[...], mirrors[...])
    hidden = jnp.maximum(dot(weights_t[...], inputs[...]), 0.0).astype(BF16)
    self_out[...] = dot(self_two_own[...], hidden)


def second_body(order, cols, means, mirror_self, neigh_t, own, masks, reps, own_out, out, local, mirror):
    feats, masters = own.shape
    head = masters // LANES
    for i in range(head):
        local[i] = own[:, i * LANES : (i + 1) * LANES]
    for n in range(0, reps.shape[1], CHUNK):
        at = slice(n, n + CHUNK)
        result = mirror_self[:, at] + dot(neigh_t[...], means[:, at])
        values = jnp.maximum(result, 0.0).astype(BF16)
        for i in range(CHUNK // LANES):
            local[head + n // LANES + i] = values[:, i * LANES : (i + 1) * LANES]
    aggregate(cols, local, masks, head, own_out, mirror)
    send(order, mirror, reps, out, False)


def second_sums(order, cols, means, mirror_self, neigh_t, own, masks, reps, capacity):
    feats, masters = own.shape
    mirrors = reps.shape[1]
    rows = capacity // LANES * feats
    return call(
        functools.partial(second_body, order),
        (
            jax.ShapeDtypeStruct((feats, masters), F32),
            jax.ShapeDtypeStruct((len(order), rows, LANES), BF16),
        ),
        (cols, means, mirror_self, neigh_t, own, masks, reps),
        smem=(0,),
        scratch=(
            pltpu.VMEM((masks.shape[0], feats, LANES), BF16),
            pltpu.VMEM((feats, mirrors), BF16),
        ),
        flops=2 * feats * masks.size,
        moved=masks.size,
    )


def second_mean_body(received, rows, own, degree, out):
    feats, masters = own.shape
    dom, capacity = rows.shape

    def high(p):
        return rows[pl.ds(p, 1), :] >> SHIFT

    def low(p):
        return rows[pl.ds(p, 1), :] & (CHUNK - 1)

    total = add_mirrors(dom, received, high, low, feats, capacity // LANES, masters)
    divide(total, own, degree, out)


def embed_body(neigh_t, means, own, out):
    out[...] = (own[...] + dot(neigh_t[...], means[...])).astype(BF16)


def on_device(
    features, tile_mask, tile_cols, replicas, degree, self_one, neigh_one, self_two, neigh_two
):
    dom = lax.axis_size("dom")
    feat = lax.axis_size("feat")
    feats, masters = features.shape
    mirrors = replicas.shape[1]
    hidden_feats = self_one.shape[1] // feat
    capacity = -(-(2 * mirrors // dom) // LANES) * LANES
    cols = tile_cols.T
    degree = degree.reshape(1, masters)

    order = ORDER if dom == len(ORDER) else tuple(range(dom))

    def exchange(blocks):
        return lax.all_to_all(
            blocks, "dom", split_axis=0, concat_axis=0, tiled=True, axis_index_groups=[list(order)]
        )

    def gather(rows):
        return lax.all_gather(rows, "feat", axis=0, tiled=True)

    def own_rows(weights):
        width = weights.shape[1] // feat
        start = lax.axis_index("feat") * width
        return lax.dynamic_slice_in_dim(weights, start, width, 1).T

    def spread(columns):
        if dom != GROUP:
            return (exchange(jnp.broadcast_to(columns[None], (dom,) + columns.shape)),)
        half = dom // 2
        others = list(range(1, half))

        def swap(values, k):
            return lax.ppermute(values, "dom", [(i, i ^ k) for i in range(dom)])

        far = swap(columns, half)
        near = [swap(columns, k) for k in others]
        return (*near, far, *[swap(far, k) for k in others])

    both = jnp.concatenate(
        [self_one.reshape(feat, feats, -1), neigh_one.reshape(feat, feats, -1)], axis=1
    ).reshape(2 * feat * feats, -1)
    self_one_own, neigh_one_own, both_own = own_rows(self_one), own_rows(neigh_one), own_rows(both)
    self_two_own, neigh_two_own = own_rows(self_two), own_rows(neigh_two)

    received = spread(features)
    masks = transpose_masks(tile_mask)
    own_one, mirror_in, outgoing, kept_masks = first_sums(
        order, cols, received, features, masks, replicas, capacity
    )
    sums, mirror_in = lax.optimization_barrier((exchange(outgoing), gather(mirror_in)))
    own_both, asked, rows = first_mean(dom, sums, features, own_one, degree, capacity)
    slots = exchange(asked)
    hidden, mirror_self, self_part = call(
        hidden_body,
        (
            jax.ShapeDtypeStruct((hidden_feats, masters), BF16),
            jax.ShapeDtypeStruct((hidden_feats, mirrors), F32),
            jax.ShapeDtypeStruct((self_two_own.shape[0], masters), F32),
        ),
        (both.T, both_own, self_one_own, self_two_own, gather(own_both), mirror_in),
        flops=2 * masters * (4 * self_one.size + self_two_own.size),
        moved=masters * 1024,
    )
    mirror_mean, near_masks = call(
        functools.partial(collect_body, order),
        (
            jax.ShapeDtypeStruct((feats, mirrors), BF16),
            jax.ShapeDtypeStruct(masks.shape, MASK),
        ),
        (slots, replicas, kept_masks),
        hbm=(2,),
        limit=44,
        scratch=(pltpu.SemaphoreType.DMA((PIECES,)),),
        flops=2 * slots.size * mirrors,
        moved=2 * slots.size,
    )
    own_two, outgoing = second_sums(
        order, cols, gather(mirror_mean), mirror_self, neigh_one_own, hidden, near_masks, replicas, capacity
    )
    mean_two = call(
        second_mean_body,
        jax.ShapeDtypeStruct((hidden_feats, masters), BF16),
        (exchange(outgoing), rows, own_two, degree),
        flops=2 * hidden_feats * dom * capacity * masters,
        moved=2 * hidden_feats * dom * capacity,
    )
    return call(
        embed_body,
        jax.ShapeDtypeStruct((neigh_two_own.shape[0], masters), BF16),
        (neigh_two_own, gather(mean_two), self_part),
        flops=2 * masters * neigh_two_own.size,
        moved=masters * 1024,
    )


def solution(mesh):
    return jax.shard_map(
        on_device,
        mesh=mesh,
        in_specs=(
            P("feat", "dom"),
            P("dom", None, None, None),
            P("dom", None),
            P(None, "dom"),
            P("dom"),
            P(),
            P(),
            P(),
            P(),
        ),
        out_specs=P("feat", "dom"),
        check_vma=False,
    )
```

time: 260 us -> 86.6 us (0.33)
  local copies, waits for them, and re-layouts: 101 us -> 0.71 us
  other arithmetic: 62.5 us -> 0.01 us
  Pallas kernels: 0 us -> 18.3 us
  blocking collectives: 48.6 us -> 31.5 us
  matrix products: 12.7 us -> 0 us
    gather x13 -> x0, local copies, waits for them, and re-layouts: 75.9 us -> none  [the longest x4 24.9 us: serve(): return jnp.take(padded, wanted, axis=1)]
    scatter-add x2 -> x0, other arithmetic: 52.4 us -> none  [combine(): incoming = jnp.zeros((feature_row_block, masters + 1), jnp.float32).at[:,...]
    pallas_call x0 -> x8, Pallas kernels: none -> 18.3 us  [call(): pl.pallas_call(body, out_shape=out_shape, in_specs=[place(i) for i in ran...]
    all_to_all x1 -> x0, blocking collectives: 17.7 us -> none  [on_device(): lax.all_to_all(serve(hidden_master), 'dom', split_axis=1, concat_axis=1,...]
    dot_general x6 -> x0, matrix products: 12.7 us -> none  [the longest x2 10.9 us: aggregate_rows(): jnp.einsum('fiku,ikvu->fiv', selected, masks_bf, preferred_element_type=j...]
    unnamed x48 -> x20, local copies, waits for them, and re-layouts: 13 us -> 0.39 us
    scatter x1 -> x0, local copies, waits for them, and re-layouts: 8.06 us -> none  [on_device(): send_index = jnp.full((slot_count,), mirrors, jnp.int32).at[position].set...]
    ppermute x0 -> x7, starting transfers between devices: none -> 7.67 us  [swap(): return lax.ppermute(values, 'dom', [(i, i ^ k) for i in range(dom)])]
  transfers between devices with their start and end apart: 4 -> 10, of which waited for: 2 -> 1; matrix products, arithmetic and copies ran while one was open for 5% -> 1% of each run, Pallas kernels for 0% -> 5%
where the time goes in v2:
time: 86.6 us; the launch traced here: 86.1 us
  blocking collectives  31.5 us (36%)
  starting transfers between devices  23.3 us (27%)
  Pallas kernels  18.3 us (21%)
  waiting for transfers between devices  12 us (14%)
    all_gather x4, blocking collectives, gather(): return lax.all_gather(rows, 'feat', axis=0, tiled=True)  31.5 us
    pallas_call x8, Pallas kernels, call(): pl.pallas_call(body, out_shape=out_shape, in_specs=[place(i) for i in ran...  18.3 us
    all_to_all x3, starting transfers between devices, exchange(): lax.all_to_all(blocks, 'dom', split_axis=0, concat_axis=0, tiled=True, ax...  15.7 us
    all_to_all x3, waiting for transfers between devices, exchange(): lax.all_to_all(blocks, 'dom', split_axis=0, concat_axis=0, tiled=True, ax...  12 us
    ppermute x7, starting transfers between devices, swap(): return lax.ppermute(values, 'dom', [(i, i ^ k) for i in range(dom)])  7.67 us
  transfers between devices with their start and end apart: 10, of which 1 were waited for; matrix products, arithmetic and copies ran while one was open for 1% of the time, Pallas kernels for 5%

profile of v2, /device:TPU:5, one launch (start us, length us, event | category | flops | bytes accessed | tf_op | source)
XLA Modules:
  0.0 86.1 jit_solution(17639409142765882848)
XLA Ops:
  0.0 0.0 copy-start.5
  0.0 0.0 copy-start.4
  0.0 0.0 copy-start.3
  0.0 0.0 copy-start.6
  0.0 0.0 copy-start.7
  0.1 2.4 %collective-permute-start.3 = (bf16[32,1024]{1,0:T(8,128)(2,1)}, bf16[32,1024]{1,0:T(8,128)(2,1)S(1)}, u32[]{:S(2)}, u32[]{:S(2)}) collective-permute-start(bf16[32,1024]{1,0:T(8,128)(2,1)} %features.1), channel_id=1, source_target_pairs={{0,16},{4,20},{8,24},{12,28},{16,0},{20,4},{24,8},{28,12},{1,17},{... | collective-permute-start | bytes 196616 | tf_op jit(solution)/shard_map/ppermute | solution.py:442
  2.4 0.2 collective-permute-start
  2.7 1.3 %collective-permute-start.1 = (bf16[32,1024]{1,0:T(8,128)(2,1)}, bf16[32,1024]{1,0:T(8,128)(2,1)S(1)}, u32[]{:S(2)}, u32[]{:S(2)}) collective-permute-start(bf16[32,1024]{1,0:T(8,128)(2,1)} %features.1), channel_id=1, source_target_pairs={{0,8},{4,12},{8,0},{12,4},{16,24},{20,28},{24,16},{28,20},{1,9},{5... | collective-permute-start | bytes 196616 | tf_op jit(solution)/shard_map/ppermute | solution.py:442
  4.0 1.1 %collective-permute-start.2 = (bf16[32,1024]{1,0:T(8,128)(2,1)}, bf16[32,1024]{1,0:T(8,128)(2,1)S(1)}, u32[]{:S(2)}, u32[]{:S(2)}) collective-permute-start(bf16[32,1024]{1,0:T(8,128)(2,1)} %features.1), channel_id=1, source_target_pairs={{0,12},{4,8},{8,4},{12,0},{16,28},{20,24},{24,20},{28,16},{1,13},{... | collective-permute-start | bytes 196616 | tf_op jit(solution)/shard_map/ppermute | solution.py:442
  5.1 0.0 collective-permute-done.3.refs_3_
  5.1 0.2 collective-permute-start.4
  5.3 1.6 %collective-permute-start.5 = (bf16[32,1024]{1,0:T(8,128)(2,1)S(1)}, bf16[32,1024]{1,0:T(8,128)(2,1)S(1)}, u32[]{:S(2)}, u32[]{:S(2)}) collective-permute-start(bf16[32,1024]{1,0:T(8,128)(2,1)S(1)} %collective-permute-done.3.refs_3_), channel_id=1, source_target_pairs={{0,8},{4,12},{8,0},{12,4},{16,24},{20,28},{24,16},{28,20},{1,9},{5... | collective-permute-start | bytes 196616 | tf_op jit(solution)/shard_map/ppermute | solution.py:442
  6.9 0.0 collective-permute-done.refs_0_
  6.9 0.9 collective-permute-start.6
  7.7 4.0 %shard_map.91.masks = bf16[24,768,128]{2,1,0:T(8,128)(2,1)S(1)} custom-call(s32[24,6,128,128]{3,2,1,0:T(8,128)} %tile_mask.1), custom_call_target="tpu_custom_call" | custom-call | bytes 14155776 | tf_op jit(solution)/shard_map/pallas_call | solution.py:32
  11.7 0.0 collective-permute-done.1.refs_1_
  11.7 0.0 collective-permute-done.2.refs_2_
  11.8 0.0 collective-permute-done.4.refs_4_
  11.8 0.0 collective-permute-done.5.refs_5_
  11.8 0.0 collective-permute-done.6.refs_6_
  11.8 0.0 copy-done.1
  11.8 0.0 copy-done.2
  11.8 4.5 %shard_map.92 = (f32[32,1024]{1,0:T(8,128)S(1)}, bf16[32,2048]{1,0:T(8,128)(2,1)S(1)}, bf16[8,144,128]{2,1,0:T(8,128)(2,1)}, f8e4m3fn[240,768,128]{2,1,0:T(32,128)(4,1)}) custom-call(s32[6,24]{1,0:T(8,128)S(1)} %bitcast.17, bf16[32,1024]{1,0:T(8,128)(2,1)S(1)} %copy-done.1, bf16[24,768,128]{2,1,0:T(8,128)(2,1)S(1)} %shard_map.91.masks, ...), custom_call_target="tpu_custom_call" | custom-call | flops 150994944 | bytes 4718592 | tf_op jit(solution)/shard_map/pallas_call | solution.py:32
  16.4 6.6 %all-to-all-start = ((bf16[8,144,128]{2,1,0:T(8,128)(2,1)}), bf16[8,144,128]{2,1,0:T(8,128)(2,1)S(1)}, u32[]{:S(2)}, u32[]{:S(2)}) async-start(bf16[8,144,128]{2,1,0:T(8,128)(2,1)} %get-tuple-element.21), calls=%async_computation | async-start | bytes 589824 | tf_op jit(solution)/shard_map/all_to_all | solution.py:423
  23.0 0.0 copy-done.5
  23.0 8.9 %all_gather.12.mirrors = bf16[128,2048]{1,0:T(8,128)(2,1)S(1)} all-gather(bf16[32,2048]{1,0:T(8,128)(2,1)S(1)} %get-tuple-element.22), channel_id=1, replica_groups=mesh['dom'=8,'feat'=4] {'feat'}, dimensions={0}, use_global_device_ids=true | all-gather | bytes 655360 | tf_op jit(solution)/shard_map/all_gather | solution.py:428
  31.9 0.0 all-to-all-done.received
  31.9 2.4 %shard_map.93 = (bf16[64,1024]{1,0:T(8,128)(2,1)S(1)}, bf16[8,32,512]{2,1,0:T(8,128)(2,1)}, s32[8,512]{1,0:T(8,128)S(1)}) custom-call(bf16[8,144,128]{2,1,0:T(8,128)(2,1)S(1)} %all-to-all-done.received, bf16[32,1024]{1,0:T(8,128)(2,1)S(1)} %copy-done.1, f32[32,1024]{1,0:T(8,128)S(1)} %get-tuple-element.24.own, s32[1,1024]{1,0:T(1,128)S(1)} %bitcast.19), custom_call_target="tpu_custom_call" | custom-call | flops 301989888 | bytes 294912 | tf_op jit(solution)/shard_map/pallas_call | solution.py:32
  34.3 4.5 %all-to-all-start.1 = ((bf16[8,32,512]{2,1,0:T(8,128)(2,1)}), bf16[8,32,512]{2,1,0:T(8,128)(2,1)S(1)}, u32[]{:S(2)}, u32[]{:S(2)}) async-start(bf16[8,32,512]{2,1,0:T(8,128)(2,1)} %get-tuple-element.25), calls=%async_computation.1 | async-start | bytes 524288 | tf_op jit(solution)/shard_map/all_to_all | solution.py:423
  38.8 0.0 copy-done.6
  38.9 0.1 constant_dynamic-slice_fusion.1
  39.0 0.1 copy.17
  39.1 0.1 copy.24
  39.2 0.1 constant_dynamic-slice_fusion
  39.3 0.1 copy.23
  39.4 0.1 copy.25
  39.5 7.3 %all_gather.14.inputs = bf16[256,1024]{1,0:T(8,128)(2,1)S(1)} all-gather(bf16[64,1024]{1,0:T(8,128)(2,1)S(1)} %get-tuple-element.28), channel_id=1, replica_groups=mesh['dom'=8,'feat'=4] {'feat'}, dimensions={0}, use_global_device_ids=true | all-gather | bytes 655360 | tf_op jit(solution)/shard_map/all_gather | solution.py:428
  46.8 0.6 shard_map.95
  47.4 0.0 all-to-all-done.1.received
  47.4 1.6 %shard_map.94 = (bf16[32,2048]{1,0:T(8,128)(2,1)S(1)}, f8e4m3fn[24,768,128]{2,1,0:T(32,128)(4,1)S(1)}) custom-call(bf16[8,32,512]{2,1,0:T(8,128)(2,1)S(1)} %all-to-all-done.1.received, s32[3,2048]{1,0:T(4,128)S(1)} %copy-done, f8e4m3fn[240,768,128]{2,1,0:T(32,128)(4,1)} %get-tuple-element.26.masks_hbm), custom_call_target="tpu_custom_call" | custom-call | flops 536870912 | bytes 262144 | tf_op jit(solution)/shard_map/pallas_call | solution.py:32
  49.1 7.3 %all_gather.13.means = bf16[128,2048]{1,0:T(8,128)(2,1)S(1)} all-gather(bf16[32,2048]{1,0:T(8,128)(2,1)S(1)} %get-tuple-element.27), channel_id=1, replica_groups=mesh['dom'=8,'feat'=4] {'feat'}, dimensions={0}, use_global_device_ids=true | all-gather | bytes 655360 | tf_op jit(solution)/shard_map/all_gather | solution.py:428
  56.4 3.6 %shard_map.96 = (f32[64,1024]{1,0:T(8,128)S(1)}, bf16[8,256,128]{2,1,0:T(8,128)(2,1)}) custom-call(s32[6,24]{1,0:T(8,128)S(1)} %bitcast.18, bf16[128,2048]{1,0:T(8,128)(2,1)S(1)} %all_gather.13.means, f32[64,2048]{1,0:T(8,128)S(1)} %get-tuple-element.30.mirror_self, bf16[64,128]{1,0:T(8,128)(2,1)S(1)} %bitcast.15, ...), custom_call_target="tpu_custom_call" | custom-call | flops 301989888 | bytes 2359296 | tf_op jit(solution)/shard_map/pallas_call | solution.py:32
  59.9 4.5 %all-to-all-start.2 = ((bf16[8,256,128]{2,1,0:T(8,128)(2,1)}), bf16[8,256,128]{2,1,0:T(8,128)(2,1)S(1)}, u32[]{:S(2)}, u32[]{:S(2)}) async-start(bf16[8,256,128]{2,1,0:T(8,128)(2,1)} %get-tuple-element.33), calls=%async_computation.2 | async-start | bytes 1048576 | tf_op jit(solution)/shard_map/all_to_all | solution.py:423
  64.5 0.1 copy.22
  64.5 12.0 %all-to-all-done.2.received = bf16[8,256,128]{2,1,0:T(8,128)(2,1)S(1)} async-done(((bf16[8,256,128]{2,1,0:T(8,128)(2,1)}), bf16[8,256,128]{2,1,0:T(8,128)(2,1)S(1)}, u32[]{:S(2)}, u32[]{:S(2)}) %all-to-all-start.2) | async-done | bytes 524320 | tf_op jit(solution)/shard_map/all_to_all | solution.py:423
  76.6 0.8 shard_map.97
  77.3 7.9 %all_gather.15.means = bf16[256,1024]{1,0:T(8,128)(2,1)S(1)} all-gather(bf16[64,1024]{1,0:T(8,128)(2,1)S(1)} %shard_map.97), channel_id=1, replica_groups=mesh['dom'=8,'feat'=4] {'feat'}, dimensions={0}, use_global_device_ids=true | all-gather | bytes 655360 | tf_op jit(solution)/shard_map/all_gather | solution.py:428
  85.3 0.9 %shard_map.98 = bf16[64,1024]{1,0:T(8,128)(2,1)} custom-call(bf16[64,256]{1,0:T(8,128)(2,1)S(1)} %bitcast.14, bf16[256,1024]{1,0:T(8,128)(2,1)S(1)} %all_gather.15.means, f32[64,1024]{1,0:T(8,128)S(1)} %get-tuple-element.36.own), custom_call_target="tpu_custom_call" | custom-call | flops 33554432 | bytes 1048576 | tf_op jit(solution)/shard_map/pallas_call | solution.py:32
  (9 shorter events, 0.0 us)
Async XLA Ops:
  0.0 11.8 %copy-start.1 = (bf16[32,1024]{1,0:T(8,128)(2,1)S(1)}, bf16[32,1024]{1,0:T(8,128)(2,1)}, u32[]{:S(2)}) copy-start(bf16[32,1024]{1,0:T(8,128)(2,1)} %features.1) | copy-start | bytes 196612
  0.0 11.8 %copy-start.2 = (s32[24,6]{0,1:T(8,128)S(1)}, s32[24,6]{0,1:T(8,128)}, u32[]{:S(2)}) copy-start(s32[24,6]{0,1:T(8,128)} %param.11) | copy-start | bytes 1732
  0.0 11.8 %copy-start = (s32[3,2048]{1,0:T(4,128)S(1)}, s32[3,2048]{1,0:T(4,128)}, u32[]{:S(2)}) copy-start(s32[3,2048]{1,0:T(4,128)} %reps.5) | copy-start | bytes 73732
  0.0 23.0 %copy-start.5 = (bf16[128,256]{1,0:T(8,128)(2,1)S(1)}, bf16[128,256]{1,0:T(8,128)(2,1)}, u32[]{:S(2)}) copy-start(bf16[128,256]{1,0:T(8,128)(2,1)} %param.14) | copy-start | bytes 196612
  0.0 23.0 %copy-start.4 = (bf16[128,256]{1,0:T(8,128)(2,1)S(1)}, bf16[128,256]{1,0:T(8,128)(2,1)}, u32[]{:S(2)}) copy-start(bf16[128,256]{1,0:T(8,128)(2,1)} %param.15) | copy-start | bytes 196612
  0.0 31.9 %copy-start.3 = (s32[1024]{0:T(1024)S(1)}, s32[1024]{0:T(1024)}, u32[]{:S(2)}) copy-start(s32[1024]{0:T(1024)} %param.13) | copy-start | bytes 12292
  0.0 38.8 %copy-start.6 = (bf16[256,256]{1,0:T(8,128)(2,1)S(1)}, bf16[256,256]{1,0:T(8,128)(2,1)}, u32[]{:S(2)}) copy-start(bf16[256,256]{1,0:T(8,128)(2,1)} %param.16) | copy-start | bytes 393220
  0.0 38.8 %copy-start.7 = (bf16[256,256]{1,0:T(8,128)(2,1)S(1)}, bf16[256,256]{1,0:T(8,128)(2,1)}, u32[]{:S(2)}) copy-start(bf16[256,256]{1,0:T(8,128)(2,1)} %param.17) | copy-start | bytes 393220
  0.1 5.0 %collective-permute-start.3 = (bf16[32,1024]{1,0:T(8,128)(2,1)}, bf16[32,1024]{1,0:T(8,128)(2,1)S(1)}, u32[]{:S(2)}, u32[]{:S(2)}) collective-permute-start(bf16[32,1024]{1,0:T(8,128)(2,1)} %features.1), channel_id=1, source_target_pairs={{0,16},{4,20},{8,24},{12,28},{16,0},{20,4},{24,8},{28,12},{1,17},{... | collective-permute-start | bytes 196616 | tf_op jit(solution)/shard_map/ppermute | solution.py:442
  2.4 4.5 %collective-permute-start = (bf16[32,1024]{1,0:T(8,128)(2,1)}, bf16[32,1024]{1,0:T(8,128)(2,1)S(1)}, u32[]{:S(2)}, u32[]{:S(2)}) collective-permute-start(bf16[32,1024]{1,0:T(8,128)(2,1)} %features.1), channel_id=1, source_target_pairs={{0,4},{4,0},{8,12},{12,8},{16,20},{20,16},{24,28},{28,24},{1,5},{5... | collective-permute-start | bytes 196616 | tf_op jit(solution)/shard_map/ppermute | solution.py:442
  2.7 9.1 %collective-permute-start.1 = (bf16[32,1024]{1,0:T(8,128)(2,1)}, bf16[32,1024]{1,0:T(8,128)(2,1)S(1)}, u32[]{:S(2)}, u32[]{:S(2)}) collective-permute-start(bf16[32,1024]{1,0:T(8,128)(2,1)} %features.1), channel_id=1, source_target_pairs={{0,8},{4,12},{8,0},{12,4},{16,24},{20,28},{24,16},{28,20},{1,9},{5... | collective-permute-start | bytes 196616 | tf_op jit(solution)/shard_map/ppermute | solution.py:442
  4.0 7.8 %collective-permute-start.2 = (bf16[32,1024]{1,0:T(8,128)(2,1)}, bf16[32,1024]{1,0:T(8,128)(2,1)S(1)}, u32[]{:S(2)}, u32[]{:S(2)}) collective-permute-start(bf16[32,1024]{1,0:T(8,128)(2,1)} %features.1), channel_id=1, source_target_pairs={{0,12},{4,8},{8,4},{12,0},{16,28},{20,24},{24,20},{28,16},{1,13},{... | collective-permute-start | bytes 196616 | tf_op jit(solution)/shard_map/ppermute | solution.py:442
  5.1 6.7 %collective-permute-start.4 = (bf16[32,1024]{1,0:T(8,128)(2,1)S(1)}, bf16[32,1024]{1,0:T(8,128)(2,1)S(1)}, u32[]{:S(2)}, u32[]{:S(2)}) collective-permute-start(bf16[32,1024]{1,0:T(8,128)(2,1)S(1)} %collective-permute-done.3.refs_3_), channel_id=1, source_target_pairs={{0,4},{4,0},{8,12},{12,8},{16,20},{20,16},{24,28},{28,24},{1,5},{5... | collective-permute-start | bytes 196616 | tf_op jit(solution)/shard_map/ppermute | solution.py:442
  5.3 6.5 %collective-permute-start.5 = (bf16[32,1024]{1,0:T(8,128)(2,1)S(1)}, bf16[32,1024]{1,0:T(8,128)(2,1)S(1)}, u32[]{:S(2)}, u32[]{:S(2)}) collective-permute-start(bf16[32,1024]{1,0:T(8,128)(2,1)S(1)} %collective-permute-done.3.refs_3_), channel_id=1, source_target_pairs={{0,8},{4,12},{8,0},{12,4},{16,24},{20,28},{24,16},{28,20},{1,9},{5... | collective-permute-start | bytes 196616 | tf_op jit(solution)/shard_map/ppermute | solution.py:442
  6.9 4.9 %collective-permute-start.6 = (bf16[32,1024]{1,0:T(8,128)(2,1)S(1)}, bf16[32,1024]{1,0:T(8,128)(2,1)S(1)}, u32[]{:S(2)}, u32[]{:S(2)}) collective-permute-start(bf16[32,1024]{1,0:T(8,128)(2,1)S(1)} %collective-permute-done.3.refs_3_), channel_id=1, source_target_pairs={{0,12},{4,8},{8,4},{12,0},{16,28},{20,24},{24,20},{28,16},{1,13},{... | collective-permute-start | bytes 196616 | tf_op jit(solution)/shard_map/ppermute | solution.py:442
  16.4 15.6 %all-to-all-start = ((bf16[8,144,128]{2,1,0:T(8,128)(2,1)}), bf16[8,144,128]{2,1,0:T(8,128)(2,1)S(1)}, u32[]{:S(2)}, u32[]{:S(2)}) async-start(bf16[8,144,128]{2,1,0:T(8,128)(2,1)} %get-tuple-element.21), calls=%async_computation | async-start | bytes 589824 | tf_op jit(solution)/shard_map/all_to_all | solution.py:423
  34.3 13.1 %all-to-all-start.1 = ((bf16[8,32,512]{2,1,0:T(8,128)(2,1)}), bf16[8,32,512]{2,1,0:T(8,128)(2,1)S(1)}, u32[]{:S(2)}, u32[]{:S(2)}) async-start(bf16[8,32,512]{2,1,0:T(8,128)(2,1)} %get-tuple-element.25), calls=%async_computation.1 | async-start | bytes 524288 | tf_op jit(solution)/shard_map/all_to_all | solution.py:423
  59.9 16.6 %all-to-all-start.2 = ((bf16[8,256,128]{2,1,0:T(8,128)(2,1)}), bf16[8,256,128]{2,1,0:T(8,128)(2,1)S(1)}, u32[]{:S(2)}, u32[]{:S(2)}) async-start(bf16[8,256,128]{2,1,0:T(8,128)(2,1)} %get-tuple-element.33), calls=%async_computation.2 | async-start | bytes 1048576 | tf_op jit(solution)/shard_map/all_to_all | solution.py:423

commit v3 on v2

--- a/solution.py
+++ b/solution.py
@@ -15,7 +15,7 @@
 SHIFT = 8
 CHUNK = 1 << SHIFT
 GROUP = 8
-ORDER = (5, 2, 3, 7, 1, 0, 4, 6)
+ORDER = (4, 7, 2, 6, 1, 0, 5, 3)
 INDEX_ROWS = 16
 VMEM = pl.BlockSpec(memory_space=pltpu.VMEM)
 SMEM = pl.BlockSpec(memory_space=pltpu.SMEM)
@@ -333,32 +333,88 @@
     )
 
 
-def collect_body(order, received, reps, masks_hbm, out, masks, arrived):
-    copies = fetch(masks_hbm, masks, arrived)
+def collect_body(order, received, reps, out):
     feats = out.shape[0]
     for n in range(0, reps.shape[1], CHUNK):
         at = slice(n, n + CHUNK)
         spots = one_hot(reps[1:2, at], received.shape[2])
         out[:, at] = pick_all(order, received, spots, reps[0:1, at], feats).astype(BF16)
-    for copy in copies:
+
+
+def bring_body(masks_hbm, masks, arrived):
+    for copy in fetch(masks_hbm, masks, arrived):
         copy.wait()
 
 
-def hidden_body(weights_t, own_t, self_own_t, self_two_own, inputs, mirrors, own_out, mirror_out, self_out):
-    own_out[...] = jnp.maximum(dot(own_t[...], inputs[...]), 0.0).astype(BF16)
-    mirror_out[...] = dot(self_own_t[...], mirrors[...])
-    hidden = jnp.maximum(dot(weights_t[...], inputs[...]), 0.0).astype(BF16)
+def weights_body(feat, me, self_one, neigh_one, self_two, neigh_two, both_out, both_own, mirror_own, self_own, neigh_own):
+    rows_one = self_one.shape[0] // feat
+    rows_two = neigh_two.shape[0] // feat
+    wide_one = self_one.shape[1] // feat
+    wide_two = neigh_two.shape[1] // feat
+
+    def turned(pieces):
+        return jnp.concatenate([piece.astype(F32) for piece in pieces], axis=0).T.astype(BF16)
+
+    def fill(f):
+        def block(weight, rows, k):
+            return weight[(f ^ k) * rows : ((f ^ k) + 1) * rows, :]
+
+        def own(values, wide):
+            return values[f * wide : (f + 1) * wide]
+
+        ones = [[block(w, rows_one, k) for w in (self_one, neigh_one)] for k in range(feat)]
+        both = turned([piece for pair in ones for piece in pair])
+        both_out[...] = both
+        both_own[...] = own(both, wide_one)
+        mirror_own[...] = own(turned([pair[i] for i in range(2) for pair in ones]), wide_one)
+        self_own[...] = own(turned([self_two[...]]), wide_two)
+        neigh_own[...] = own(turned([block(neigh_two, rows_two, k) for k in range(feat)]), wide_two)
+
+    for f in range(feat):
+        pl.when(me[0] == f)(functools.partial(fill, f))
+
+
+def turn_weights(feat, me, self_one, neigh_one, self_two, neigh_two):
+    wide_one = self_one.shape[1] // feat
+    wide_two = neigh_two.shape[1] // feat
+    depth = 2 * self_one.shape[0]
+    shapes = [
+        (self_one.shape[1], depth),
+        (wide_one, depth),
+        (wide_one, depth),
+        (wide_two, self_two.shape[0]),
+        (wide_two, neigh_two.shape[0]),
+    ]
+    return call(
+        functools.partial(weights_body, feat),
+        tuple(jax.ShapeDtypeStruct(shape, BF16) for shape in shapes),
+        (me.reshape(1), self_one, neigh_one, self_two, neigh_two),
+        smem=(0,),
+        moved=2 * sum(a * b for a, b in shapes),
+    )
+
+
+def stack(refs, at=slice(None)):
+    return jnp.concatenate([ref[:, at] for ref in refs], axis=0)
+
+
+def hidden_body(feat, both_t, both_own, self_two_own, *refs):
+    own_out, self_out = refs[feat:]
+    values = stack(refs[:feat])
+    own_out[...] = jnp.maximum(dot(both_own[...], values), 0.0).astype(BF16)
+    hidden = jnp.maximum(dot(both_t[...], values), 0.0).astype(BF16)
     self_out[...] = dot(self_two_own[...], hidden)
 
 
-def second_body(order, cols, means, mirror_self, neigh_t, own, masks, reps, own_out, out, local, mirror):
+def second_body(feat, order, cols, mirror_own, own, masks, reps, *refs):
+    rows = refs[: 2 * feat]
+    own_out, out, local, mirror = refs[2 * feat :]
     feats, masters = own.shape
     head = masters // LANES
     for i in range(head):
         local[i] = own[:, i * LANES : (i + 1) * LANES]
     for n in range(0, reps.shape[1], CHUNK):
-        at = slice(n, n + CHUNK)
-        result = mirror_self[:, at] + dot(neigh_t[...], means[:, at])
+        result = dot(mirror_own[...], stack(rows, slice(n, n + CHUNK)))
         values = jnp.maximum(result, 0.0).astype(BF16)
         for i in range(CHUNK // LANES):
             local[head + n // LANES + i] = values[:, i * LANES : (i + 1) * LANES]
@@ -366,17 +422,17 @@
     send(order, mirror, reps, out, False)
 
 
-def second_sums(order, cols, means, mirror_self, neigh_t, own, masks, reps, capacity):
+def second_sums(order, cols, inputs, means, mirror_own, own, masks, reps, capacity):
     feats, masters = own.shape
     mirrors = reps.shape[1]
     rows = capacity // LANES * feats
     return call(
-        functools.partial(second_body, order),
+        functools.partial(second_body, len(means), order),
         (
             jax.ShapeDtypeStruct((feats, masters), F32),
             jax.ShapeDtypeStruct((len(order), rows, LANES), BF16),
         ),
-        (cols, means, mirror_self, neigh_t, own, masks, reps),
+        (cols, mirror_own, own, masks, reps) + inputs + means,
         smem=(0,),
         scratch=(
             pltpu.VMEM((masks.shape[0], feats, LANES), BF16),
@@ -401,8 +457,19 @@
     divide(total, own, degree, out)
 
 
-def embed_body(neigh_t, means, own, out):
-    out[...] = (own[...] + dot(neigh_t[...], means[...])).astype(BF16)
+def embed_body(count, neigh_t, total, *refs):
+    out = refs[count]
+    out[...] = (total[...] + dot(neigh_t[...], stack(refs[:count]))).astype(out.dtype)
+
+
+def embed(neigh_t, total, blocks, dtype):
+    return call(
+        functools.partial(embed_body, len(blocks)),
+        jax.ShapeDtypeStruct(total.shape, dtype),
+        (neigh_t, total) + blocks,
+        flops=2 * total.size * neigh_t.shape[1],
+        moved=10 * total.size,
+    )
 
 
 def on_device(
@@ -424,13 +491,20 @@
             blocks, "dom", split_axis=0, concat_axis=0, tiled=True, axis_index_groups=[list(order)]
         )
 
-    def gather(rows):
-        return lax.all_gather(rows, "feat", axis=0, tiled=True)
-
-    def own_rows(weights):
-        width = weights.shape[1] // feat
-        start = lax.axis_index("feat") * width
-        return lax.dynamic_slice_in_dim(weights, start, width, 1).T
+    me = lax.axis_index("feat")
+
+    def swap(values, k):
+        return lax.ppermute(values, "feat", [(i, i ^ k) for i in range(feat)])
+
+    def gather(blocks, stop=feat):
+        blocks = list(blocks)
+        for k in range(len(blocks), stop):
+            low = k & -k
+            blocks.append(swap(blocks[k ^ low], low))
+        return tuple(blocks)
+
+    last = feat - 1
+    together = lax.optimization_barrier
 
     def spread(columns):
         if dom != GROUP:
@@ -445,46 +519,53 @@
         near = [swap(columns, k) for k in others]
         return (*near, far, *[swap(far, k) for k in others])
 
-    both = jnp.concatenate(
-        [self_one.reshape(feat, feats, -1), neigh_one.reshape(feat, feats, -1)], axis=1
-    ).reshape(2 * feat * feats, -1)
-    self_one_own, neigh_one_own, both_own = own_rows(self_one), own_rows(neigh_one), own_rows(both)
-    self_two_own, neigh_two_own = own_rows(self_two), own_rows(neigh_two)
-
     received = spread(features)
     masks = transpose_masks(tile_mask)
     own_one, mirror_in, outgoing, kept_masks = first_sums(
         order, cols, received, features, masks, replicas, capacity
     )
-    sums, mirror_in = lax.optimization_barrier((exchange(outgoing), gather(mirror_in)))
+    sums = exchange(outgoing)
     own_both, asked, rows = first_mean(dom, sums, features, own_one, degree, capacity)
+    own_both, weights = together((own_both, (self_one, neigh_one, self_two, neigh_two)))
     slots = exchange(asked)
-    hidden, mirror_self, self_part = call(
-        hidden_body,
+    inputs = gather((own_both,))
+    both_t, both_own, mirror_own, self_two_own, neigh_two_own = turn_weights(feat, me, *weights)
+    slots, both_t, both_own, mirror_own, self_two_own, neigh_two_own = together(
+        (slots, both_t, both_own, mirror_own, self_two_own, neigh_two_own)
+    )
+    mirror_mean = call(
+        functools.partial(collect_body, order),
+        jax.ShapeDtypeStruct((feats, mirrors), BF16),
+        (slots, replicas),
+        flops=2 * slots.size * mirrors,
+        moved=2 * slots.size,
+    )
+    mirror_mean, kept_masks = together((mirror_mean, kept_masks))
+    means = gather((mirror_mean,), last)
+    near_masks = call(
+        bring_body,
+        jax.ShapeDtypeStruct(masks.shape, MASK),
+        (kept_masks,),
+        hbm=(0,),
+        limit=44,
+        scratch=(pltpu.SemaphoreType.DMA((PIECES,)),),
+        moved=2 * masks.size,
+    )
+    hidden, self_part = call(
+        functools.partial(hidden_body, feat),
         (
             jax.ShapeDtypeStruct((hidden_feats, masters), BF16),
-            jax.ShapeDtypeStruct((hidden_feats, mirrors), F32),
             jax.ShapeDtypeStruct((self_two_own.shape[0], masters), F32),
         ),
-        (both.T, both_own, self_one_own, self_two_own, gather(own_both), mirror_in),
+        (both_t, both_own, self_two_own) + inputs,
         flops=2 * masters * (4 * self_one.size + self_two_own.size),
         moved=masters * 1024,
     )
-    mirror_mean, near_masks = call(
-        functools.partial(collect_body, order),
-        (
-            jax.ShapeDtypeStruct((feats, mirrors), BF16),
-            jax.ShapeDtypeStruct(masks.shape, MASK),
-        ),
-        (slots, replicas, kept_masks),
-        hbm=(2,),
-        limit=44,
-        scratch=(pltpu.SemaphoreType.DMA((PIECES,)),),
-        flops=2 * slots.size * mirrors,
-        moved=2 * slots.size,
+    means, near_masks, hidden, self_part, neigh_two_own = together(
+        (means, near_masks, hidden, self_part, neigh_two_own)
     )
     own_two, outgoing = second_sums(
-        order, cols, gather(mirror_mean), mirror_self, neigh_one_own, hidden, near_masks, replicas, capacity
+        order, cols, gather((mirror_in,)), gather(means), mirror_own, hidden, near_masks, replicas, capacity
     )
     mean_two = call(
         second_mean_body,
@@ -493,13 +574,12 @@
         flops=2 * hidden_feats * dom * capacity * masters,
         moved=2 * hidden_feats * dom * capacity,
     )
-    return call(
-        embed_body,
-        jax.ShapeDtypeStruct((neigh_two_own.shape[0], masters), BF16),
-        (neigh_two_own, gather(mean_two), self_part),
-        flops=2 * masters * neigh_two_own.size,
-        moved=masters * 1024,
-    )
+    blocks = gather((mean_two,))
+    total = self_part
+    for start, stop in ((0, 2), (2, 3), (3, 4)):
+        weights = neigh_two_own[:, start * hidden_feats : stop * hidden_feats]
+        total = embed(weights, total, blocks[start:stop], BF16 if stop == feat else F32)
+    return total
 
 
 def solution(mesh):

time: 86.6 us -> 81.4 us (0.940); the launches traced: 86.1 us -> 79.9 us
  waiting for transfers between devices: 12 us -> 2.96 us
  starting transfers between devices: 23.3 us -> 30.6 us
  blocking collectives: 31.5 us -> 27.9 us
    all_gather x4 -> x0, blocking collectives: 31.5 us -> none  [gather(): return lax.all_gather(rows, 'feat', axis=0, tiled=True)]
    all_to_all x0 -> x2, blocking collectives: none -> 27.9 us  [exchange(): lax.all_to_all(blocks, 'dom', split_axis=0, concat_axis=0, tiled=True, ax...]
    ppermute x0 -> x12, starting transfers between devices: none -> 17.5 us  [swap(): return lax.ppermute(values, 'feat', [(i, i ^ k) for i in range(feat)])]
    all_to_all x3 -> x1, waiting for transfers between devices: 12 us -> 0.01 us  [exchange(): lax.all_to_all(blocks, 'dom', split_axis=0, concat_axis=0, tiled=True, ax...]
    all_to_all x3 -> x1, starting transfers between devices: 15.7 us -> 5.47 us  [exchange(): lax.all_to_all(blocks, 'dom', split_axis=0, concat_axis=0, tiled=True, ax...]
    ppermute x0 -> x12, waiting for transfers between devices: none -> 2.94 us  [swap(): return lax.ppermute(values, 'feat', [(i, i ^ k) for i in range(feat)])]
    pallas_call x8 -> x12, Pallas kernels: 18.3 us -> 18 us  [call(): pl.pallas_call(body, out_shape=out_shape, in_specs=[place(i) for i in ran...]
  transfers between devices with their start and end apart: 10 -> 20, of which waited for: 1 -> 4; matrix products, arithmetic and copies ran while one was open for 1% -> 0% of each run, Pallas kernels for 5% -> 9%
where the time goes in v3:
time: 81.4 us; the launch traced here: 79.9 us
  starting transfers between devices  30.6 us (38%)
  blocking collectives  27.9 us (34%)
  Pallas kernels  18 us (22%)
  waiting for transfers between devices  2.96 us (4%)
    all_to_all x2, blocking collectives, exchange(): lax.all_to_all(blocks, 'dom', split_axis=0, concat_axis=0, tiled=True, ax...  27.9 us
    pallas_call x12, Pallas kernels, call(): pl.pallas_call(body, out_shape=out_shape, in_specs=[place(i) for i in ran...  18 us
    ppermute x12, starting transfers between devices, swap(): return lax.ppermute(values, 'feat', [(i, i ^ k) for i in range(feat)])  17.5 us
    ppermute x7, starting transfers between devices, swap(): return lax.ppermute(values, 'dom', [(i, i ^ k) for i in range(dom)])  7.67 us
    all_to_all x1, starting transfers between devices, exchange(): lax.all_to_all(blocks, 'dom', split_axis=0, concat_axis=0, tiled=True, ax...  5.47 us
    ppermute x12, waiting for transfers between devices, swap(): return lax.ppermute(values, 'feat', [(i, i ^ k) for i in range(feat)])  2.94 us
  transfers between devices with their start and end apart: 20, of which 4 were waited for; matrix products, arithmetic and copies ran while one was open for 0% of the time, Pallas kernels for 9%

profile of v3, /device:TPU:5, one launch (start us, length us, event | category | flops | bytes accessed | tf_op | source)
XLA Modules:
  0.0 79.9 jit_solution(11894368795192714936)
XLA Ops:
  0.1 2.4 %collective-permute-start.3 = (bf16[32,1024]{1,0:T(8,128)(2,1)}, bf16[32,1024]{1,0:T(8,128)(2,1)S(1)}, u32[]{:S(2)}, u32[]{:S(2)}) collective-permute-start(bf16[32,1024]{1,0:T(8,128)(2,1)} %features.1), channel_id=1, source_target_pairs={{0,16},{4,20},{8,24},{12,28},{16,0},{20,4},{24,8},{28,12},{1,17},{... | collective-permute-start | bytes 196616 | tf_op jit(solution)/shard_map/ppermute | solution.py:516
  2.4 0.2 collective-permute-start
  2.7 1.3 %collective-permute-start.1 = (bf16[32,1024]{1,0:T(8,128)(2,1)}, bf16[32,1024]{1,0:T(8,128)(2,1)S(1)}, u32[]{:S(2)}, u32[]{:S(2)}) collective-permute-start(bf16[32,1024]{1,0:T(8,128)(2,1)} %features.1), channel_id=1, source_target_pairs={{0,8},{4,12},{8,0},{12,4},{16,24},{20,28},{24,16},{28,20},{1,9},{5... | collective-permute-start | bytes 196616 | tf_op jit(solution)/shard_map/ppermute | solution.py:516
  4.0 1.1 %collective-permute-start.2 = (bf16[32,1024]{1,0:T(8,128)(2,1)}, bf16[32,1024]{1,0:T(8,128)(2,1)S(1)}, u32[]{:S(2)}, u32[]{:S(2)}) collective-permute-start(bf16[32,1024]{1,0:T(8,128)(2,1)} %features.1), channel_id=1, source_target_pairs={{0,12},{4,8},{8,4},{12,0},{16,28},{20,24},{24,20},{28,16},{1,13},{... | collective-permute-start | bytes 196616 | tf_op jit(solution)/shard_map/ppermute | solution.py:516
  5.1 0.2 collective-permute-start.4
  5.3 1.6 %collective-permute-start.5 = (bf16[32,1024]{1,0:T(8,128)(2,1)S(1)}, bf16[32,1024]{1,0:T(8,128)(2,1)S(1)}, u32[]{:S(2)}, u32[]{:S(2)}) collective-permute-start(bf16[32,1024]{1,0:T(8,128)(2,1)S(1)} %collective-permute-done.3.refs_3_), channel_id=1, source_target_pairs={{0,8},{4,12},{8,0},{12,4},{16,24},{20,28},{24,16},{28,20},{1,9},{5... | collective-permute-start | bytes 196616 | tf_op jit(solution)/shard_map/ppermute | solution.py:516
  6.9 0.0 collective-permute-done.refs_0_
  6.9 0.9 %collective-permute-start.6 = (bf16[32,1024]{1,0:T(8,128)(2,1)S(1)}, bf16[32,1024]{1,0:T(8,128)(2,1)S(1)}, u32[]{:S(2)}, u32[]{:S(2)}) collective-permute-start(bf16[32,1024]{1,0:T(8,128)(2,1)S(1)} %collective-permute-done.3.refs_3_), channel_id=1, source_target_pairs={{0,12},{4,8},{8,4},{12,0},{16,28},{20,24},{24,20},{28,16},{1,13},{... | collective-permute-start | bytes 196616 | tf_op jit(solution)/shard_map/ppermute | solution.py:516
  7.7 4.0 %shard_map.91.masks = bf16[24,768,128]{2,1,0:T(8,128)(2,1)S(1)} custom-call(s32[24,6,128,128]{3,2,1,0:T(8,128)} %tile_mask.1), custom_call_target="tpu_custom_call" | custom-call | bytes 14155776 | tf_op jit(solution)/shard_map/pallas_call | solution.py:32
  11.7 0.0 collective-permute-done.1.refs_1_
  11.8 0.0 collective-permute-done.4.refs_4_
  11.8 0.0 collective-permute-done.5.refs_5_
  11.8 3.8 %shard_map.92 = (f32[32,1024]{1,0:T(8,128)S(1)}, bf16[32,2048]{1,0:T(8,128)(2,1)S(1)}, bf16[8,144,128]{2,1,0:T(8,128)(2,1)S(1)}, f8e4m3fn[240,768,128]{2,1,0:T(32,128)(4,1)}) custom-call(s32[6,24]{1,0:T(8,128)S(1)} %bitcast.3, bf16[32,1024]{1,0:T(8,128)(2,1)S(1)} %copy-done.3, bf16[24,768,128]{2,1,0:T(8,128)(2,1)S(1)} %shard_map.91.masks, ...), custom_call_target="tpu_custom_call" | custom-call | flops 150994944 | bytes 4718592 | tf_op jit(solution)/shard_map/pallas_call | solution.py:32
  15.7 11.3 %all_to_all.15.received = bf16[8,144,128]{2,1,0:T(8,128)(2,1)S(1)} all-to-all(bf16[8,144,128]{2,1,0:T(8,128)(2,1)S(1)} %get-tuple-element.41), channel_id=1, replica_groups={{16,28,8,24,4,0,20,12},{17,29,9,25,5,1,21,13},{18,30,10,26,6,2,22,14},{..., dimensions={0} | all-to-all | bytes 589824 | tf_op jit(solution)/shard_map/all_to_all | solution.py:490
  27.0 2.4 %shard_map.93 = (bf16[64,1024]{1,0:T(8,128)(2,1)S(1)}, bf16[8,32,512]{2,1,0:T(8,128)(2,1)}, s32[8,512]{1,0:T(8,128)S(1)}) custom-call(bf16[8,144,128]{2,1,0:T(8,128)(2,1)S(1)} %all_to_all.15.received, bf16[32,1024]{1,0:T(8,128)(2,1)S(1)} %copy-done.3, f32[32,1024]{1,0:T(8,128)S(1)} %get-tuple-element.42.own, s32[1,1024]{1,0:T(1,128)S(1)} %bitcast.5), custom_call_target="tpu_custom_call" | custom-call | flops 301989888 | bytes 294912 | tf_op jit(solution)/shard_map/pallas_call | solution.py:32
  29.4 5.5 %all-to-all-start.1 = ((bf16[8,32,512]{2,1,0:T(8,128)(2,1)}), bf16[8,32,512]{2,1,0:T(8,128)(2,1)S(1)}, u32[]{:S(2)}, u32[]{:S(2)}) async-start(bf16[8,32,512]{2,1,0:T(8,128)(2,1)} %get-tuple-element.43), calls=%async_computation.1 | async-start | bytes 524288 | tf_op jit(solution)/shard_map/all_to_all | solution.py:490
  34.8 1.2 %collective-permute-start.10 = (bf16[64,1024]{1,0:T(8,128)(2,1)S(1)}, bf16[64,1024]{1,0:T(8,128)(2,1)S(1)}, u32[]{:S(2)}, u32[]{:S(2)}) collective-permute-start(bf16[64,1024]{1,0:T(8,128)(2,1)S(1)} %get-tuple-element.61.refs_0_), channel_id=1, source_target_pairs={{0,2},{1,3},{2,0},{3,1},{4,6},{5,7},{6,4},{7,5},{8,10},{9,11},{10,... | collective-permute-start | bytes 393224 | tf_op jit(solution)/shard_map/ppermute | solution.py:497
  36.0 0.3 collective-permute-start.13
  36.3 4.5 %collective-permute-start.9 = (bf16[64,1024]{1,0:T(8,128)(2,1)S(1)}, bf16[64,1024]{1,0:T(8,128)(2,1)S(1)}, u32[]{:S(2)}, u32[]{:S(2)}) collective-permute-start(bf16[64,1024]{1,0:T(8,128)(2,1)S(1)} %get-tuple-element.61.refs_0_), channel_id=1, source_target_pairs={{0,1},{1,0},{2,3},{3,2},{4,5},{5,4},{6,7},{7,6},{8,9},{9,8},{10,11... | collective-permute-start | bytes 393224 | tf_op jit(solution)/shard_map/ppermute | solution.py:497
  40.9 0.2 shard_map.94
  41.1 2.7 %collective-permute-start.11 = (bf16[64,1024]{1,0:T(8,128)(2,1)S(1)}, bf16[64,1024]{1,0:T(8,128)(2,1)S(1)}, u32[]{:S(2)}, u32[]{:S(2)}) collective-permute-start(bf16[64,1024]{1,0:T(8,128)(2,1)S(1)} %collective-permute-done.10.refs_2_), channel_id=1, source_target_pairs={{0,1},{1,0},{2,3},{3,2},{4,5},{5,4},{6,7},{7,6},{8,9},{9,8},{10,11... | collective-permute-start | bytes 393224 | tf_op jit(solution)/shard_map/ppermute | solution.py:497
  43.8 0.0 all-to-all-done.1.received
  43.8 0.7 shard_map.95.refs_4_
  44.5 0.1 collective-permute-start.7
  44.6 1.3 %collective-permute-start.8 = (bf16[32,2048]{1,0:T(8,128)(2,1)S(1)}, bf16[32,2048]{1,0:T(8,128)(2,1)S(1)}, u32[]{:S(2)}, u32[]{:S(2)}) collective-permute-start(bf16[32,2048]{1,0:T(8,128)(2,1)S(1)} %shard_map.95.refs_4_), channel_id=1, source_target_pairs={{0,2},{1,3},{2,0},{3,1},{4,6},{5,7},{6,4},{7,5},{8,10},{9,11},{10,... | collective-permute-start | bytes 393224 | tf_op jit(solution)/shard_map/ppermute | solution.py:497
  45.9 1.6 %shard_map.96.masks = f8e4m3fn[24,768,128]{2,1,0:T(32,128)(4,1)S(1)} custom-call(f8e4m3fn[240,768,128]{2,1,0:T(32,128)(4,1)} %get-tuple-element.57.masks_hbm), custom_call_target="tpu_custom_call" | custom-call | bytes 4718592 | tf_op jit(solution)/shard_map/pallas_call | solution.py:32
  47.5 0.0 collective-permute-done.13.refs_2_
  47.5 0.8 collective-permute-start.12
  48.3 0.0 collective-permute-done.9.refs_1_
  48.3 0.1 collective-permute-start.14
  48.4 0.5 shard_map.97
  49.0 0.4 collective-permute-done.8.refs_6_
  49.3 1.3 %collective-permute-start.15 = (bf16[32,2048]{1,0:T(8,128)(2,1)S(1)}, bf16[32,2048]{1,0:T(8,128)(2,1)S(1)}, u32[]{:S(2)}, u32[]{:S(2)}) collective-permute-start(bf16[32,2048]{1,0:T(8,128)(2,1)S(1)} %collective-permute-done.8.refs_6_), channel_id=1, source_target_pairs={{0,1},{1,0},{2,3},{3,2},{4,5},{5,4},{6,7},{7,6},{8,9},{9,8},{10,11... | collective-permute-start | bytes 393224 | tf_op jit(solution)/shard_map/ppermute | solution.py:497
  50.6 0.0 collective-permute-done.12.refs_1_
  50.6 1.0 %collective-permute-done.15.refs_7_ = bf16[32,2048]{1,0:T(8,128)(2,1)S(1)} collective-permute-done((bf16[32,2048]{1,0:T(8,128)(2,1)S(1)}, bf16[32,2048]{1,0:T(8,128)(2,1)S(1)}, u32[]{:S(2)}, u32[]{:S(2)}) %collective-permute-start.15) | collective-permute-done | bytes 131104 | tf_op jit(solution)/shard_map/ppermute | solution.py:497
  51.6 2.8 %shard_map.98 = (f32[64,1024]{1,0:T(8,128)S(1)}, bf16[8,256,128]{2,1,0:T(8,128)(2,1)S(1)}) custom-call(s32[6,24]{1,0:T(8,128)S(1)} %bitcast.4, bf16[64,256]{1,0:T(8,128)(2,1)S(1)} %get-tuple-element.67.mirror_own, bf16[64,1024]{1,0:T(8,128)(2,1)S(1)} %get-tuple-element.68.own, f8e4m3fn[24,768,128]{2,1,0:T(32,128)(4,1)S(1)} %shard_map.96.masks, ...), custom_call_target="tpu_custom_call" | custom-call | flops 301989888 | bytes 2359296 | tf_op jit(solution)/shard_map/pallas_call | solution.py:32
  54.4 16.6 %all_to_all.16.received = bf16[8,256,128]{2,1,0:T(8,128)(2,1)S(1)} all-to-all(bf16[8,256,128]{2,1,0:T(8,128)(2,1)S(1)} %get-tuple-element.74), channel_id=1, replica_groups={{16,28,8,24,4,0,20,12},{17,29,9,25,5,1,21,13},{18,30,10,26,6,2,22,14},{..., dimensions={0} | all-to-all | bytes 1048576 | tf_op jit(solution)/shard_map/all_to_all | solution.py:490
  71.0 0.8 shard_map.99.refs_0_
  71.7 1.3 %collective-permute-start.17 = (bf16[64,1024]{1,0:T(8,128)(2,1)S(1)}, bf16[64,1024]{1,0:T(8,128)(2,1)S(1)}, u32[]{:S(2)}, u32[]{:S(2)}) collective-permute-start(bf16[64,1024]{1,0:T(8,128)(2,1)S(1)} %shard_map.99.refs_0_), channel_id=1, source_target_pairs={{0,2},{1,3},{2,0},{3,1},{4,6},{5,7},{6,4},{7,5},{8,10},{9,11},{10,... | collective-permute-start | bytes 393224 | tf_op jit(solution)/shard_map/ppermute | solution.py:497
  73.0 1.6 %collective-permute-start.16 = (bf16[64,1024]{1,0:T(8,128)(2,1)S(1)}, bf16[64,1024]{1,0:T(8,128)(2,1)S(1)}, u32[]{:S(2)}, u32[]{:S(2)}) collective-permute-start(bf16[64,1024]{1,0:T(8,128)(2,1)S(1)} %shard_map.99.refs_0_), channel_id=1, source_target_pairs={{0,1},{1,0},{2,3},{3,2},{4,5},{5,4},{6,7},{7,6},{8,9},{9,8},{10,11... | collective-permute-start | bytes 393224 | tf_op jit(solution)/shard_map/ppermute | solution.py:497
  74.6 1.0 %collective-permute-done.17.refs_0_ = bf16[64,1024]{1,0:T(8,128)(2,1)S(1)} collective-permute-done((bf16[64,1024]{1,0:T(8,128)(2,1)S(1)}, bf16[64,1024]{1,0:T(8,128)(2,1)S(1)}, u32[]{:S(2)}, u32[]{:S(2)}) %collective-permute-start.17) | collective-permute-done | bytes 131104 | tf_op jit(solution)/shard_map/ppermute | solution.py:497
  75.6 2.4 %collective-permute-start.18 = (bf16[64,1024]{1,0:T(8,128)(2,1)S(1)}, bf16[64,1024]{1,0:T(8,128)(2,1)S(1)}, u32[]{:S(2)}, u32[]{:S(2)}) collective-permute-start(bf16[64,1024]{1,0:T(8,128)(2,1)S(1)} %collective-permute-done.17.refs_0_), channel_id=1, source_target_pairs={{0,1},{1,0},{2,3},{3,2},{4,5},{5,4},{6,7},{7,6},{8,9},{9,8},{10,11... | collective-permute-start | bytes 393224 | tf_op jit(solution)/shard_map/ppermute | solution.py:497
  78.1 0.1 fusion
  78.1 0.0 collective-permute-done.16.refs_1_
  78.1 0.2 shard_map.100.total
  78.3 0.2 shard_map.101.total
  78.5 0.6 collective-permute-done.18.refs_0_
  79.0 0.8 %shard_map.102 = bf16[64,1024]{1,0:T(8,128)(2,1)} custom-call(bf16[64,64]{1,0:T(8,128)(2,1)S(1)} %get-tuple-element.78.neigh_t, f32[64,1024]{1,0:T(8,128)S(1)} %shard_map.101.total, bf16[64,1024]{1,0:T(8,128)(2,1)S(1)} %collective-permute-done.18.refs_0_), custom_call_target="tpu_custom_call" | custom-call | flops 8388608 | bytes 655360 | tf_op jit(solution)/shard_map/pallas_call | solution.py:32
  (24 shorter events, 0.1 us)
Async XLA Ops:
  0.0 11.8 %copy-start.3 = (bf16[32,1024]{1,0:T(8,128)(2,1)S(1)}, bf16[32,1024]{1,0:T(8,128)(2,1)}, u32[]{:S(2)}) copy-start(bf16[32,1024]{1,0:T(8,128)(2,1)} %features.1) | copy-start | bytes 196612
  0.0 11.8 %copy-start.6 = (s32[24,6]{0,1:T(8,128)S(1)}, s32[24,6]{0,1:T(8,128)}, u32[]{:S(2)}) copy-start(s32[24,6]{0,1:T(8,128)} %param.11) | copy-start | bytes 1732
  0.0 11.8 %copy-start = (s32[3,2048]{1,0:T(4,128)S(1)}, s32[3,2048]{1,0:T(4,128)}, u32[]{:S(2)}) copy-start(s32[3,2048]{1,0:T(4,128)} %reps.5) | copy-start | bytes 73732
  0.0 27.0 %copy-start.7 = (s32[1024]{0:T(1024)S(1)}, s32[1024]{0:T(1024)}, u32[]{:S(2)}) copy-start(s32[1024]{0:T(1024)} %param.13) | copy-start | bytes 12292
  0.0 40.8 %copy-start.4 = (bf16[128,256]{1,0:T(8,128)(2,1)S(1)}, bf16[128,256]{1,0:T(8,128)(2,1)}, u32[]{:S(2)}) copy-start(bf16[128,256]{1,0:T(8,128)(2,1)} %self_one) | copy-start | bytes 196612
  0.0 40.8 %copy-start.5 = (bf16[128,256]{1,0:T(8,128)(2,1)S(1)}, bf16[128,256]{1,0:T(8,128)(2,1)}, u32[]{:S(2)}) copy-start(bf16[128,256]{1,0:T(8,128)(2,1)} %neigh_one) | copy-start | bytes 196612
  0.0 40.8 %copy-start.1 = (bf16[256,256]{1,0:T(8,128)(2,1)S(1)}, bf16[256,256]{1,0:T(8,128)(2,1)}, u32[]{:S(2)}) copy-start(bf16[256,256]{1,0:T(8,128)(2,1)} %self_two) | copy-start | bytes 393220
  0.0 40.8 %copy-start.2 = (bf16[256,256]{1,0:T(8,128)(2,1)S(1)}, bf16[256,256]{1,0:T(8,128)(2,1)}, u32[]{:S(2)}) copy-start(bf16[256,256]{1,0:T(8,128)(2,1)} %neigh_two) | copy-start | bytes 393220
  0.1 5.0 %collective-permute-start.3 = (bf16[32,1024]{1,0:T(8,128)(2,1)}, bf16[32,1024]{1,0:T(8,128)(2,1)S(1)}, u32[]{:S(2)}, u32[]{:S(2)}) collective-permute-start(bf16[32,1024]{1,0:T(8,128)(2,1)} %features.1), channel_id=1, source_target_pairs={{0,16},{4,20},{8,24},{12,28},{16,0},{20,4},{24,8},{28,12},{1,17},{... | collective-permute-start | bytes 196616 | tf_op jit(solution)/shard_map/ppermute | solution.py:516
  2.4 4.5 %collective-permute-start = (bf16[32,1024]{1,0:T(8,128)(2,1)}, bf16[32,1024]{1,0:T(8,128)(2,1)S(1)}, u32[]{:S(2)}, u32[]{:S(2)}) collective-permute-start(bf16[32,1024]{1,0:T(8,128)(2,1)} %features.1), channel_id=1, source_target_pairs={{0,4},{4,0},{8,12},{12,8},{16,20},{20,16},{24,28},{28,24},{1,5},{5... | collective-permute-start | bytes 196616 | tf_op jit(solution)/shard_map/ppermute | solution.py:516
  2.7 9.1 %collective-permute-start.1 = (bf16[32,1024]{1,0:T(8,128)(2,1)}, bf16[32,1024]{1,0:T(8,128)(2,1)S(1)}, u32[]{:S(2)}, u32[]{:S(2)}) collective-permute-start(bf16[32,1024]{1,0:T(8,128)(2,1)} %features.1), channel_id=1, source_target_pairs={{0,8},{4,12},{8,0},{12,4},{16,24},{20,28},{24,16},{28,20},{1,9},{5... | collective-permute-start | bytes 196616 | tf_op jit(solution)/shard_map/ppermute | solution.py:516
  4.0 7.8 %collective-permute-start.2 = (bf16[32,1024]{1,0:T(8,128)(2,1)}, bf16[32,1024]{1,0:T(8,128)(2,1)S(1)}, u32[]{:S(2)}, u32[]{:S(2)}) collective-permute-start(bf16[32,1024]{1,0:T(8,128)(2,1)} %features.1), channel_id=1, source_target_pairs={{0,12},{4,8},{8,4},{12,0},{16,28},{20,24},{24,20},{28,16},{1,13},{... | collective-permute-start | bytes 196616 | tf_op jit(solution)/shard_map/ppermute | solution.py:516
  5.1 6.7 %collective-permute-start.4 = (bf16[32,1024]{1,0:T(8,128)(2,1)S(1)}, bf16[32,1024]{1,0:T(8,128)(2,1)S(1)}, u32[]{:S(2)}, u32[]{:S(2)}) collective-permute-start(bf16[32,1024]{1,0:T(8,128)(2,1)S(1)} %collective-permute-done.3.refs_3_), channel_id=1, source_target_pairs={{0,4},{4,0},{8,12},{12,8},{16,20},{20,16},{24,28},{28,24},{1,5},{5... | collective-permute-start | bytes 196616 | tf_op jit(solution)/shard_map/ppermute | solution.py:516
  5.3 6.5 %collective-permute-start.5 = (bf16[32,1024]{1,0:T(8,128)(2,1)S(1)}, bf16[32,1024]{1,0:T(8,128)(2,1)S(1)}, u32[]{:S(2)}, u32[]{:S(2)}) collective-permute-start(bf16[32,1024]{1,0:T(8,128)(2,1)S(1)} %collective-permute-done.3.refs_3_), channel_id=1, source_target_pairs={{0,8},{4,12},{8,0},{12,4},{16,24},{20,28},{24,16},{28,20},{1,9},{5... | collective-permute-start | bytes 196616 | tf_op jit(solution)/shard_map/ppermute | solution.py:516
  6.9 4.9 %collective-permute-start.6 = (bf16[32,1024]{1,0:T(8,128)(2,1)S(1)}, bf16[32,1024]{1,0:T(8,128)(2,1)S(1)}, u32[]{:S(2)}, u32[]{:S(2)}) collective-permute-start(bf16[32,1024]{1,0:T(8,128)(2,1)S(1)} %collective-permute-done.3.refs_3_), channel_id=1, source_target_pairs={{0,12},{4,8},{8,4},{12,0},{16,28},{20,24},{24,20},{28,16},{1,13},{... | collective-permute-start | bytes 196616 | tf_op jit(solution)/shard_map/ppermute | solution.py:516
  29.4 14.4 %all-to-all-start.1 = ((bf16[8,32,512]{2,1,0:T(8,128)(2,1)}), bf16[8,32,512]{2,1,0:T(8,128)(2,1)S(1)}, u32[]{:S(2)}, u32[]{:S(2)}) async-start(bf16[8,32,512]{2,1,0:T(8,128)(2,1)} %get-tuple-element.43), calls=%async_computation.1 | async-start | bytes 524288 | tf_op jit(solution)/shard_map/all_to_all | solution.py:490
  34.8 6.2 %collective-permute-start.10 = (bf16[64,1024]{1,0:T(8,128)(2,1)S(1)}, bf16[64,1024]{1,0:T(8,128)(2,1)S(1)}, u32[]{:S(2)}, u32[]{:S(2)}) collective-permute-start(bf16[64,1024]{1,0:T(8,128)(2,1)S(1)} %get-tuple-element.61.refs_0_), channel_id=1, source_target_pairs={{0,2},{1,3},{2,0},{3,1},{4,6},{5,7},{6,4},{7,5},{8,10},{9,11},{10,... | collective-permute-start | bytes 393224 | tf_op jit(solution)/shard_map/ppermute | solution.py:497
  36.0 11.5 %collective-permute-start.13 = (bf16[32,2048]{1,0:T(8,128)(2,1)S(1)}, bf16[32,2048]{1,0:T(8,128)(2,1)S(1)}, u32[]{:S(2)}, u32[]{:S(2)}) collective-permute-start(bf16[32,2048]{1,0:T(8,128)(2,1)S(1)} %get-tuple-element.70.refs_0_), channel_id=1, source_target_pairs={{0,2},{1,3},{2,0},{3,1},{4,6},{5,7},{6,4},{7,5},{8,10},{9,11},{10,... | collective-permute-start | bytes 393224 | tf_op jit(solution)/shard_map/ppermute | solution.py:497
  36.3 12.0 %collective-permute-start.9 = (bf16[64,1024]{1,0:T(8,128)(2,1)S(1)}, bf16[64,1024]{1,0:T(8,128)(2,1)S(1)}, u32[]{:S(2)}, u32[]{:S(2)}) collective-permute-start(bf16[64,1024]{1,0:T(8,128)(2,1)S(1)} %get-tuple-element.61.refs_0_), channel_id=1, source_target_pairs={{0,1},{1,0},{2,3},{3,2},{4,5},{5,4},{6,7},{7,6},{8,9},{9,8},{10,11... | collective-permute-start | bytes 393224 | tf_op jit(solution)/shard_map/ppermute | solution.py:497
  41.1 7.3 %collective-permute-start.11 = (bf16[64,1024]{1,0:T(8,128)(2,1)S(1)}, bf16[64,1024]{1,0:T(8,128)(2,1)S(1)}, u32[]{:S(2)}, u32[]{:S(2)}) collective-permute-start(bf16[64,1024]{1,0:T(8,128)(2,1)S(1)} %collective-permute-done.10.refs_2_), channel_id=1, source_target_pairs={{0,1},{1,0},{2,3},{3,2},{4,5},{5,4},{6,7},{7,6},{8,9},{9,8},{10,11... | collective-permute-start | bytes 393224 | tf_op jit(solution)/shard_map/ppermute | solution.py:497
  44.5 4.4 %collective-permute-start.7 = (bf16[32,2048]{1,0:T(8,128)(2,1)S(1)}, bf16[32,2048]{1,0:T(8,128)(2,1)S(1)}, u32[]{:S(2)}, u32[]{:S(2)}) collective-permute-start(bf16[32,2048]{1,0:T(8,128)(2,1)S(1)} %shard_map.95.refs_4_), channel_id=1, source_target_pairs={{0,1},{1,0},{2,3},{3,2},{4,5},{5,4},{6,7},{7,6},{8,9},{9,8},{10,11... | collective-permute-start | bytes 393224 | tf_op jit(solution)/shard_map/ppermute | solution.py:497
  44.6 4.7 %collective-permute-start.8 = (bf16[32,2048]{1,0:T(8,128)(2,1)S(1)}, bf16[32,2048]{1,0:T(8,128)(2,1)S(1)}, u32[]{:S(2)}, u32[]{:S(2)}) collective-permute-start(bf16[32,2048]{1,0:T(8,128)(2,1)S(1)} %shard_map.95.refs_4_), channel_id=1, source_target_pairs={{0,2},{1,3},{2,0},{3,1},{4,6},{5,7},{6,4},{7,5},{8,10},{9,11},{10,... | collective-permute-start | bytes 393224 | tf_op jit(solution)/shard_map/ppermute | solution.py:497
  47.5 3.1 %collective-permute-start.12 = (bf16[32,2048]{1,0:T(8,128)(2,1)S(1)}, bf16[32,2048]{1,0:T(8,128)(2,1)S(1)}, u32[]{:S(2)}, u32[]{:S(2)}) collective-permute-start(bf16[32,2048]{1,0:T(8,128)(2,1)S(1)} %get-tuple-element.70.refs_0_), channel_id=1, source_target_pairs={{0,1},{1,0},{2,3},{3,2},{4,5},{5,4},{6,7},{7,6},{8,9},{9,8},{10,11... | collective-permute-start | bytes 393224 | tf_op jit(solution)/shard_map/ppermute | solution.py:497
  48.3 2.3 %collective-permute-start.14 = (bf16[32,2048]{1,0:T(8,128)(2,1)S(1)}, bf16[32,2048]{1,0:T(8,128)(2,1)S(1)}, u32[]{:S(2)}, u32[]{:S(2)}) collective-permute-start(bf16[32,2048]{1,0:T(8,128)(2,1)S(1)} %collective-permute-done.13.refs_2_), channel_id=1, source_target_pairs={{0,1},{1,0},{2,3},{3,2},{4,5},{5,4},{6,7},{7,6},{8,9},{9,8},{10,11... | collective-permute-start | bytes 393224 | tf_op jit(solution)/shard_map/ppermute | solution.py:497
  49.3 2.3 %collective-permute-start.15 = (bf16[32,2048]{1,0:T(8,128)(2,1)S(1)}, bf16[32,2048]{1,0:T(8,128)(2,1)S(1)}, u32[]{:S(2)}, u32[]{:S(2)}) collective-permute-start(bf16[32,2048]{1,0:T(8,128)(2,1)S(1)} %collective-permute-done.8.refs_6_), channel_id=1, source_target_pairs={{0,1},{1,0},{2,3},{3,2},{4,5},{5,4},{6,7},{7,6},{8,9},{9,8},{10,11... | collective-permute-start | bytes 393224 | tf_op jit(solution)/shard_map/ppermute | solution.py:497
  71.7 3.9 %collective-permute-start.17 = (bf16[64,1024]{1,0:T(8,128)(2,1)S(1)}, bf16[64,1024]{1,0:T(8,128)(2,1)S(1)}, u32[]{:S(2)}, u32[]{:S(2)}) collective-permute-start(bf16[64,1024]{1,0:T(8,128)(2,1)S(1)} %shard_map.99.refs_0_), channel_id=1, source_target_pairs={{0,2},{1,3},{2,0},{3,1},{4,6},{5,7},{6,4},{7,5},{8,10},{9,11},{10,... | collective-permute-start | bytes 393224 | tf_op jit(solution)/shard_map/ppermute | solution.py:497
  73.0 5.1 %collective-permute-start.16 = (bf16[64,1024]{1,0:T(8,128)(2,1)S(1)}, bf16[64,1024]{1,0:T(8,128)(2,1)S(1)}, u32[]{:S(2)}, u32[]{:S(2)}) collective-permute-start(bf16[64,1024]{1,0:T(8,128)(2,1)S(1)} %shard_map.99.refs_0_), channel_id=1, source_target_pairs={{0,1},{1,0},{2,3},{3,2},{4,5},{5,4},{6,7},{7,6},{8,9},{9,8},{10,11... | collective-permute-start | bytes 393224 | tf_op jit(solution)/shard_map/ppermute | solution.py:497
  75.6 3.4 %collective-permute-start.18 = (bf16[64,1024]{1,0:T(8,128)(2,1)S(1)}, bf16[64,1024]{1,0:T(8,128)(2,1)S(1)}, u32[]{:S(2)}, u32[]{:S(2)}) collective-permute-start(bf16[64,1024]{1,0:T(8,128)(2,1)S(1)} %collective-permute-done.17.refs_0_), channel_id=1, source_target_pairs={{0,1},{1,0},{2,3},{3,2},{4,5},{5,4},{6,7},{7,6},{8,9},{9,8},{10,11... | collective-permute-start | bytes 393224 | tf_op jit(solution)/shard_map/ppermute | solution.py:497

commit v4 on v3

--- a/solution.py
+++ b/solution.py
@@ -15,14 +15,12 @@
 SHIFT = 8
 CHUNK = 1 << SHIFT
 GROUP = 8
-ORDER = (4, 7, 2, 6, 1, 0, 5, 3)
+ORDER = (5, 2, 3, 7, 1, 0, 4, 6)
 INDEX_ROWS = 16
 VMEM = pl.BlockSpec(memory_space=pltpu.VMEM)
 SMEM = pl.BlockSpec(memory_space=pltpu.SMEM)
 HBM = pl.BlockSpec(memory_space=pltpu.HBM)
-PIECES = 4
 MASK_PIECES = 8
-SPARE = 10
 
 
 def call(body, out_shape, operands, smem=(), hbm=(), hbm_out=(), scratch=(), flops=0, moved=0, limit=20):
@@ -76,7 +74,7 @@
 
 def masks_body(tile_mask, out, blocks, arrived):
     tiles, stored, side, _ = blocks.shape
-    copies = fetch(tile_mask, blocks, arrived)
+    copies = transfer(tile_mask, blocks, tiles, arrived)
     step = tiles // len(copies)
     for i in range(tiles):
         if i % step == 0:
@@ -102,25 +100,22 @@
     )
 
 
-def index_rows(part, row, slot_places, names):
-    blocks = slot_places.shape[0] // LANES
-    name = lax.broadcasted_iota(I32, (len(names), 1), 0)
+def index_rows(part, slot, row, names, blocks):
+    lane_shift = LANES.bit_length() - 1
+    shape = (len(names) * INDEX_ROWS, part.shape[1])
+    at = lax.broadcasted_iota(I32, (shape[0], 1), 0)
+    place = at % INDEX_ROWS
+    name = jnp.zeros_like(at)
     for k, q in enumerate(names):
-        name = jnp.where(lax.broadcasted_iota(I32, (len(names), 1), 0) == k, q, name)
-    mine = jnp.broadcast_to(name, (len(names), part.shape[1])) == part
-    digits = [keep(mine, jnp.broadcast_to(d, mine.shape)) for d in (row >> SHIFT, row & (CHUNK - 1))]
-    digits = jnp.concatenate(digits, axis=0).astype(F32).astype(BF16)
-    found = dot(digits, slot_places, (1, 1))
-    out = []
-    for k in range(len(names)):
-        pieces = [
-            found[at : at + 1, b * LANES : (b + 1) * LANES]
-            for at in (k, len(names) + k)
-            for b in range(blocks)
-        ]
-        pieces.append(jnp.zeros((INDEX_ROWS - len(pieces), LANES), F32))
-        out.append(jnp.concatenate(pieces, axis=0).astype(BF16))
-    return out
+        name = jnp.where(at // INDEX_ROWS == k, q, name)
+    wanted = jnp.where(place < 2 * blocks, name * blocks + place % blocks, -1)
+    here = jnp.broadcast_to(wanted, shape) == part * blocks + (slot >> lane_shift)
+    digits = jnp.where(
+        jnp.broadcast_to(place < blocks, shape),
+        jnp.broadcast_to((row >> SHIFT).astype(F32), shape),
+        jnp.broadcast_to((row & (CHUNK - 1)).astype(F32), shape),
+    )
+    return dot(keep(here, digits).astype(BF16), one_hot(slot & (LANES - 1), LANES), (1, 1)).astype(BF16)
 
 
 def pick(blocks, names, spots, part, feats):
@@ -143,13 +138,12 @@
     return lax.fori_loop(0, dom // GROUP, add_group, jnp.zeros((feats, spots.shape[1]), F32))
 
 
-def fetch(source, target, arrived):
-    pieces = arrived.shape[0]
-    step = target.shape[0] // pieces
+def transfer(source, target, rows, done):
+    step = rows // done.shape[0]
     copies = []
-    for i in range(pieces):
+    for i in range(done.shape[0]):
         at = pl.ds(i * step, step)
-        copies.append(pltpu.make_async_copy(source.at[at], target.at[at], arrived.at[i]))
+        copies.append(pltpu.make_async_copy(source.at[at], target.at[at], done.at[i]))
         copies[-1].start()
     return copies
 
@@ -186,8 +180,9 @@
                 block = placed[k * feats : (k + 1) * feats, b * LANES : (b + 1) * LANES]
                 out[first + k, b * feats : (b + 1) * feats, :] = block
         if with_index:
-            for k, index in enumerate(index_rows(part, row, slot_places, names)):
-                out[first + k, rows:, :] = index
+            index = index_rows(part, slot, row, names, blocks)
+            for k in range(GROUP):
+                out[first + k, rows:, :] = index[k * INDEX_ROWS : (k + 1) * INDEX_ROWS]
 
     if dom == GROUP:
         group(0, order, part)
@@ -201,8 +196,8 @@
 
 
 def first_body(order, cols, own, masks, reps, *refs):
-    received = refs[:-8]
-    own_out, all_out, out, kept, local, mirror, narrow, written = refs[-8:]
+    received = refs[:-6]
+    own_out, all_out, out, narrow, local, mirror = refs[-6:]
     feats, masters = own.shape
     head = masters // LANES
     for i in range(head):
@@ -222,10 +217,7 @@
         for i in range(CHUNK // LANES):
             local[head + n // LANES + i] = values[:, i * LANES : (i + 1) * LANES]
     aggregate(cols, local, masks, head, own_out, mirror, narrow)
-    copy = pltpu.make_async_copy(narrow, kept.at[pl.ds(0, masks.shape[0])], written)
-    copy.start()
     send(order, mirror, reps, out, True)
-    copy.wait()
 
 
 def first_sums(order, cols, received, own, masks, reps, capacity):
@@ -239,17 +231,13 @@
             jax.ShapeDtypeStruct((feats, masters), F32),
             jax.ShapeDtypeStruct((feats, mirrors), BF16),
             jax.ShapeDtypeStruct((len(order), rows, LANES), BF16),
-            jax.ShapeDtypeStruct((SPARE * tiles,) + masks.shape[1:], MASK),
+            jax.ShapeDtypeStruct(masks.shape, MASK),
         ),
         (cols, own, masks, reps) + received,
         smem=(0,),
-        hbm_out=(3,),
-        limit=44,
         scratch=(
             pltpu.VMEM((tiles, feats, LANES), BF16),
             pltpu.VMEM((feats, mirrors), BF16),
-            pltpu.VMEM(masks.shape, MASK),
-            pltpu.SemaphoreType.DMA,
         ),
         flops=2 * feats * masks.size,
         moved=2 * masks.size,
@@ -279,7 +267,7 @@
         out[:, at] = (whole / degree[:, at].astype(F32)).astype(BF16)
 
 
-def first_mean_body(received, features, own, degree, out, asked, rows_out, mean):
+def first_mean_body(received, features, mirror_in, own, degree, out, asked_hbm, rows_out, mean, asked, left):
     feats, masters = own.shape
     dom, capacity = rows_out.shape
     blocks = capacity // LANES
@@ -304,7 +292,7 @@
     divide(total, own, degree, mean)
     folded = jnp.concatenate([mean[:, a * CHUNK : (a + 1) * CHUNK] for a in range(parts)], axis=0)
 
-    def one(p, carry):
+    def serve(p, carry):
         found = dot(folded, one_hot(low(p), CHUNK))
         chosen = jnp.zeros((feats, capacity), F32)
         for a in range(parts):
@@ -312,22 +300,43 @@
         asked[p] = chosen.astype(BF16)
         return carry
 
-    loop(dom, one, 0)
+    def one(p, carry):
+        serve(p, carry)
+        copies[p].start()
+        return carry
+
+    if dom == GROUP:
+        copies = [pltpu.make_async_copy(asked.at[p], asked_hbm.at[p], left.at[p]) for p in range(dom)]
+        loop(dom, one, 0)
+    else:
+        copies = [pltpu.make_async_copy(asked, asked_hbm, left.at[0])]
+        lax.fori_loop(0, dom, serve, 0)
+        copies[0].start()
     out[:feats] = features[...]
-    out[feats:] = mean[...]
-
-
-def first_mean(dom, received, features, own, degree, capacity):
-    feats, masters = own.shape
+    out[feats : 2 * feats] = mean[...]
+    for n in range(mirror_in.shape[1] // masters):
+        out[(2 + n) * feats : (3 + n) * feats] = mirror_in[:, n * masters : (n + 1) * masters]
+    for copy in copies:
+        copy.wait()
+
+
+def first_mean(dom, received, features, mirror_in, own, degree, capacity):
+    feats, masters = own.shape
+    rows = (2 + mirror_in.shape[1] // masters) * feats
     return call(
         first_mean_body,
         (
-            jax.ShapeDtypeStruct((2 * feats, masters), BF16),
+            jax.ShapeDtypeStruct((rows, masters), BF16),
             jax.ShapeDtypeStruct((dom, feats, capacity), BF16),
             jax.ShapeDtypeStruct((dom, capacity), I32),
         ),
-        (received, features, own, degree),
-        scratch=(pltpu.VMEM((feats, masters), BF16),),
+        (received, features, mirror_in, own, degree),
+        hbm_out=(1,),
+        scratch=(
+            pltpu.VMEM((feats, masters), BF16),
+            pltpu.VMEM((dom, feats, capacity), BF16),
+            pltpu.SemaphoreType.DMA((dom if dom == GROUP else 1,)),
+        ),
         flops=2 * received.size * masters,
         moved=received.size * 2,
     )
@@ -341,16 +350,11 @@
         out[:, at] = pick_all(order, received, spots, reps[0:1, at], feats).astype(BF16)
 
 
-def bring_body(masks_hbm, masks, arrived):
-    for copy in fetch(masks_hbm, masks, arrived):
-        copy.wait()
-
-
-def weights_body(feat, me, self_one, neigh_one, self_two, neigh_two, both_out, both_own, mirror_own, self_own, neigh_own):
+def weights_body(feat, me, self_one, neigh_one, self_two, neigh_two, out):
     rows_one = self_one.shape[0] // feat
     rows_two = neigh_two.shape[0] // feat
-    wide_one = self_one.shape[1] // feat
-    wide_two = neigh_two.shape[1] // feat
+    hidden = self_one.shape[1]
+    wide = hidden // feat
 
     def turned(pieces):
         return jnp.concatenate([piece.astype(F32) for piece in pieces], axis=0).T.astype(BF16)
@@ -359,38 +363,33 @@
         def block(weight, rows, k):
             return weight[(f ^ k) * rows : ((f ^ k) + 1) * rows, :]
 
-        def own(values, wide):
+        def own(values):
             return values[f * wide : (f + 1) * wide]
 
         ones = [[block(w, rows_one, k) for w in (self_one, neigh_one)] for k in range(feat)]
         both = turned([piece for pair in ones for piece in pair])
-        both_out[...] = both
-        both_own[...] = own(both, wide_one)
-        mirror_own[...] = own(turned([pair[i] for i in range(2) for pair in ones]), wide_one)
-        self_own[...] = own(turned([self_two[...]]), wide_two)
-        neigh_own[...] = own(turned([block(neigh_two, rows_two, k) for k in range(feat)]), wide_two)
+        parts = [
+            both,
+            own(both),
+            own(turned([pair[i] for i in range(2) for pair in ones])),
+            own(turned([self_two[...]])),
+            own(turned([block(neigh_two, rows_two, k) for k in range(feat)])),
+        ]
+        out[...] = jnp.concatenate(parts, axis=0)
 
     for f in range(feat):
         pl.when(me[0] == f)(functools.partial(fill, f))
 
 
 def turn_weights(feat, me, self_one, neigh_one, self_two, neigh_two):
-    wide_one = self_one.shape[1] // feat
-    wide_two = neigh_two.shape[1] // feat
-    depth = 2 * self_one.shape[0]
-    shapes = [
-        (self_one.shape[1], depth),
-        (wide_one, depth),
-        (wide_one, depth),
-        (wide_two, self_two.shape[0]),
-        (wide_two, neigh_two.shape[0]),
-    ]
+    hidden = self_one.shape[1]
+    shape = (hidden + 4 * (hidden // feat), 2 * self_one.shape[0])
     return call(
         functools.partial(weights_body, feat),
-        tuple(jax.ShapeDtypeStruct(shape, BF16) for shape in shapes),
+        jax.ShapeDtypeStruct(shape, BF16),
         (me.reshape(1), self_one, neigh_one, self_two, neigh_two),
         smem=(0,),
-        moved=2 * sum(a * b for a, b in shapes),
+        moved=2 * shape[0] * shape[1],
     )
 
 
@@ -398,23 +397,32 @@
     return jnp.concatenate([ref[:, at] for ref in refs], axis=0)
 
 
-def hidden_body(feat, both_t, both_own, self_two_own, *refs):
-    own_out, self_out = refs[feat:]
-    values = stack(refs[:feat])
-    own_out[...] = jnp.maximum(dot(both_own[...], values), 0.0).astype(BF16)
-    hidden = jnp.maximum(dot(both_t[...], values), 0.0).astype(BF16)
-    self_out[...] = dot(self_two_own[...], hidden)
+def hidden_body(feat, weights, *refs):
+    own_out, self_out, mirror_own, neigh_own = refs[feat:]
+    wide = own_out.shape[0]
+    whole = feat * wide
+    depth = weights.shape[1] // feat
+    values = jnp.concatenate([ref[:depth] for ref in refs[:feat]], axis=0)
+    own_out[...] = jnp.maximum(dot(weights[whole : whole + wide], values), 0.0).astype(BF16)
+    hidden = jnp.maximum(dot(weights[:whole], values), 0.0).astype(BF16)
+    self_out[...] = dot(weights[whole + 2 * wide : whole + 3 * wide], hidden)
+    mirror_own[...] = weights[whole + wide : whole + 2 * wide]
+    neigh_own[...] = weights[whole + 3 * wide : whole + 4 * wide]
 
 
 def second_body(feat, order, cols, mirror_own, own, masks, reps, *refs):
-    rows = refs[: 2 * feat]
+    packs, means = refs[:feat], refs[feat : 2 * feat]
     own_out, out, local, mirror = refs[2 * feat :]
     feats, masters = own.shape
     head = masters // LANES
     for i in range(head):
         local[i] = own[:, i * LANES : (i + 1) * LANES]
     for n in range(0, reps.shape[1], CHUNK):
-        result = dot(mirror_own[...], stack(rows, slice(n, n + CHUNK)))
+        block, start = n // masters, n % masters
+        depth = means[0].shape[0]
+        rows = [ref[(2 + block) * depth : (3 + block) * depth, start : start + CHUNK] for ref in packs]
+        rows += [ref[:, n : n + CHUNK] for ref in means]
+        result = dot(mirror_own[...], jnp.concatenate(rows, axis=0))
         values = jnp.maximum(result, 0.0).astype(BF16)
         for i in range(CHUNK // LANES):
             local[head + n // LANES + i] = values[:, i * LANES : (i + 1) * LANES]
@@ -521,18 +529,16 @@
 
     received = spread(features)
     masks = transpose_masks(tile_mask)
-    own_one, mirror_in, outgoing, kept_masks = first_sums(
+    own_one, mirror_in, outgoing, narrow = first_sums(
         order, cols, received, features, masks, replicas, capacity
     )
     sums = exchange(outgoing)
-    own_both, asked, rows = first_mean(dom, sums, features, own_one, degree, capacity)
-    own_both, weights = together((own_both, (self_one, neigh_one, self_two, neigh_two)))
+    pack, asked, rows = first_mean(dom, sums, features, mirror_in, own_one, degree, capacity)
+    pack, weights = together((pack, (self_one, neigh_one, self_two, neigh_two)))
     slots = exchange(asked)
-    inputs = gather((own_both,))
-    both_t, both_own, mirror_own, self_two_own, neigh_two_own = turn_weights(feat, me, *weights)
-    slots, both_t, both_own, mirror_own, self_two_own, neigh_two_own = together(
-        (slots, both_t, both_own, mirror_own, self_two_own, neigh_two_own)
-    )
+    across = swap(pack, 2)
+    weights = turn_weights(feat, me, *weights)
+    slots, weights = together((slots, weights))
     mirror_mean = call(
         functools.partial(collect_body, order),
         jax.ShapeDtypeStruct((feats, mirrors), BF16),
@@ -540,32 +546,26 @@
         flops=2 * slots.size * mirrors,
         moved=2 * slots.size,
     )
-    mirror_mean, kept_masks = together((mirror_mean, kept_masks))
     means = gather((mirror_mean,), last)
-    near_masks = call(
-        bring_body,
-        jax.ShapeDtypeStruct(masks.shape, MASK),
-        (kept_masks,),
-        hbm=(0,),
-        limit=44,
-        scratch=(pltpu.SemaphoreType.DMA((PIECES,)),),
-        moved=2 * masks.size,
-    )
-    hidden, self_part = call(
+    mirror_mean, pack, across = together((mirror_mean, pack, across))
+    packs = (pack, swap(pack, 1), across, swap(across, 1))
+    hidden, self_part, mirror_own, neigh_two_own = call(
         functools.partial(hidden_body, feat),
         (
             jax.ShapeDtypeStruct((hidden_feats, masters), BF16),
-            jax.ShapeDtypeStruct((self_two_own.shape[0], masters), F32),
-        ),
-        (both_t, both_own, self_two_own) + inputs,
-        flops=2 * masters * (4 * self_one.size + self_two_own.size),
+            jax.ShapeDtypeStruct((hidden_feats, masters), F32),
+            jax.ShapeDtypeStruct((hidden_feats, weights.shape[1]), BF16),
+            jax.ShapeDtypeStruct((hidden_feats, weights.shape[1]), BF16),
+        ),
+        (weights,) + packs,
+        flops=2 * masters * weights.size,
         moved=masters * 1024,
     )
-    means, near_masks, hidden, self_part, neigh_two_own = together(
-        (means, near_masks, hidden, self_part, neigh_two_own)
+    means, hidden, self_part, mirror_own, neigh_two_own = together(
+        (means, hidden, self_part, mirror_own, neigh_two_own)
     )
     own_two, outgoing = second_sums(
-        order, cols, gather((mirror_in,)), gather(means), mirror_own, hidden, near_masks, replicas, capacity
+        order, cols, packs, gather(means), mirror_own, hidden, narrow, replicas, capacity
     )
     mean_two = call(
         second_mean_body,
@@ -576,7 +576,7 @@
     )
     blocks = gather((mean_two,))
     total = self_part
-    for start, stop in ((0, 2), (2, 3), (3, 4)):
+    for start, stop in ((0, 3), (3, 4)):
         weights = neigh_two_own[:, start * hidden_feats : stop * hidden_feats]
         total = embed(weights, total, blocks[start:stop], BF16 if stop == feat else F32)
     return total

time: 81.4 us -> 80.6 us (level)
  waiting for transfers between devices: 2.96 us -> 6.25 us
  starting transfers between devices: 30.6 us -> 27.8 us
  local copies, waits for them, and re-layouts: 0.11 us -> 2.75 us
  Pallas kernels: 18 us -> 15.6 us
    unnamed x16, local copies, waits for them, and re-layouts: 0.03 us -> 2.67 us
    pallas_call x12 -> x10, Pallas kernels: 18 us -> 15.6 us  [call(): pl.pallas_call(body, out_shape=out_shape, in_specs=[place(i) for i in ran...]
    ppermute x12 -> x9, waiting for transfers between devices: 2.94 us -> 5.17 us  [swap(): return lax.ppermute(values, 'feat', [(i, i ^ k) for i in range(feat)])]
    ppermute x12 -> x9, starting transfers between devices: 17.5 us -> 15.7 us  [swap(): return lax.ppermute(values, 'feat', [(i, i ^ k) for i in range(feat)])]
    all_to_all x1, waiting for transfers between devices: 0.01 us -> 1.06 us  [exchange(): lax.all_to_all(blocks, 'dom', split_axis=0, concat_axis=0, tiled=True, ax...]
    all_to_all x1, starting transfers between devices: 5.47 us -> 4.47 us  [exchange(): lax.all_to_all(blocks, 'dom', split_axis=0, concat_axis=0, tiled=True, ax...]
    all_to_all x2, blocking collectives: 27.9 us -> 27.1 us  [exchange(): lax.all_to_all(blocks, 'dom', split_axis=0, concat_axis=0, tiled=True, ax...]
  transfers between devices with their start and end apart: 20 -> 17, of which waited for: 4 -> 5; matrix products, arithmetic and copies ran while one was open for 0% -> 0% of each run, Pallas kernels for 9% -> 7%
where the time goes in v4:
time: 80.6 us; the launch traced here: 79.7 us
  starting transfers between devices  27.8 us (34%)
  blocking collectives  27.1 us (34%)
  Pallas kernels  15.6 us (19%)
  waiting for transfers between devices  6.25 us (8%)
  local copies, waits for them, and re-layouts  2.75 us (3%)
    all_to_all x2, blocking collectives, exchange(): lax.all_to_all(blocks, 'dom', split_axis=0, concat_axis=0, tiled=True, ax...  27.1 us
    ppermute x9, starting transfers between devices, swap(): return lax.ppermute(values, 'feat', [(i, i ^ k) for i in range(feat)])  15.7 us
    pallas_call x10, Pallas kernels, call(): pl.pallas_call(body, out_shape=out_shape, in_specs=[place(i) for i in ran...  15.6 us
    ppermute x7, starting transfers between devices, swap(): return lax.ppermute(values, 'dom', [(i, i ^ k) for i in range(dom)])  7.67 us
    ppermute x9, waiting for transfers between devices, swap(): return lax.ppermute(values, 'feat', [(i, i ^ k) for i in range(feat)])  5.17 us
    all_to_all x1, starting transfers between devices, exchange(): lax.all_to_all(blocks, 'dom', split_axis=0, concat_axis=0, tiled=True, ax...  4.47 us
    unnamed x16, local copies, waits for them, and re-layouts  2.67 us
  transfers between devices with their start and end apart: 17, of which 5 were waited for; matrix products, arithmetic and copies ran while one was open for 0% of the time, Pallas kernels for 7%

profile of v4, /device:TPU:5, one launch (start us, length us, event | category | flops | bytes accessed | tf_op | source)
XLA Modules:
  0.0 79.7 jit_solution(5438818970790262149)
XLA Ops:
  0.0 2.4 %collective-permute-start.3 = (bf16[32,1024]{1,0:T(8,128)(2,1)}, bf16[32,1024]{1,0:T(8,128)(2,1)S(1)}, u32[]{:S(2)}, u32[]{:S(2)}) collective-permute-start(bf16[32,1024]{1,0:T(8,128)(2,1)} %features.1), channel_id=1, source_target_pairs={{0,16},{4,20},{8,24},{12,28},{16,0},{20,4},{24,8},{28,12},{1,17},{... | collective-permute-start | bytes 196616 | tf_op jit(solution)/shard_map/ppermute | solution.py:524
  2.4 0.2 collective-permute-start
  2.6 1.3 %collective-permute-start.1 = (bf16[32,1024]{1,0:T(8,128)(2,1)}, bf16[32,1024]{1,0:T(8,128)(2,1)S(1)}, u32[]{:S(2)}, u32[]{:S(2)}) collective-permute-start(bf16[32,1024]{1,0:T(8,128)(2,1)} %features.1), channel_id=1, source_target_pairs={{0,8},{4,12},{8,0},{12,4},{16,24},{20,28},{24,16},{28,20},{1,9},{5... | collective-permute-start | bytes 196616 | tf_op jit(solution)/shard_map/ppermute | solution.py:524
  3.9 1.1 %collective-permute-start.2 = (bf16[32,1024]{1,0:T(8,128)(2,1)}, bf16[32,1024]{1,0:T(8,128)(2,1)S(1)}, u32[]{:S(2)}, u32[]{:S(2)}) collective-permute-start(bf16[32,1024]{1,0:T(8,128)(2,1)} %features.1), channel_id=1, source_target_pairs={{0,12},{4,8},{8,4},{12,0},{16,28},{20,24},{24,20},{28,16},{1,13},{... | collective-permute-start | bytes 196616 | tf_op jit(solution)/shard_map/ppermute | solution.py:524
  5.0 0.0 collective-permute-done.3.refs_3_
  5.0 0.2 collective-permute-start.4
  5.3 1.6 %collective-permute-start.5 = (bf16[32,1024]{1,0:T(8,128)(2,1)S(1)}, bf16[32,1024]{1,0:T(8,128)(2,1)S(1)}, u32[]{:S(2)}, u32[]{:S(2)}) collective-permute-start(bf16[32,1024]{1,0:T(8,128)(2,1)S(1)} %collective-permute-done.3.refs_3_), channel_id=1, source_target_pairs={{0,8},{4,12},{8,0},{12,4},{16,24},{20,28},{24,16},{28,20},{1,9},{5... | collective-permute-start | bytes 196616 | tf_op jit(solution)/shard_map/ppermute | solution.py:524
  6.8 0.0 collective-permute-done.refs_0_
  6.8 0.9 %collective-permute-start.6 = (bf16[32,1024]{1,0:T(8,128)(2,1)S(1)}, bf16[32,1024]{1,0:T(8,128)(2,1)S(1)}, u32[]{:S(2)}, u32[]{:S(2)}) collective-permute-start(bf16[32,1024]{1,0:T(8,128)(2,1)S(1)} %collective-permute-done.3.refs_3_), channel_id=1, source_target_pairs={{0,12},{4,8},{8,4},{12,0},{16,28},{20,24},{24,20},{28,16},{1,13},{... | collective-permute-start | bytes 196616 | tf_op jit(solution)/shard_map/ppermute | solution.py:524
  7.7 4.0 %shard_map.91.masks = bf16[24,768,128]{2,1,0:T(8,128)(2,1)S(1)} custom-call(s32[24,6,128,128]{3,2,1,0:T(8,128)} %tile_mask.1), custom_call_target="tpu_custom_call" | custom-call | bytes 14155776 | tf_op jit(solution)/shard_map/pallas_call | solution.py:30
  11.7 0.0 copy-start.7
  11.7 0.0 copy-start.4
  11.7 0.0 collective-permute-done.1.refs_1_
  11.7 0.0 collective-permute-done.2.refs_2_
  11.7 0.0 collective-permute-done.5.refs_5_
  11.8 0.0 collective-permute-done.6.refs_6_
  11.8 3.3 %shard_map.92 = (f32[32,1024]{1,0:T(8,128)S(1)}, bf16[32,2048]{1,0:T(8,128)(2,1)S(1)}, bf16[8,144,128]{2,1,0:T(8,128)(2,1)S(1)}, f8e4m3fn[24,768,128]{2,1,0:T(32,128)(4,1)S(1)}) custom-call(s32[6,24]{1,0:T(8,128)S(1)} %bitcast.5, bf16[32,1024]{1,0:T(8,128)(2,1)S(1)} %copy-done.3, bf16[24,768,128]{2,1,0:T(8,128)(2,1)S(1)} %shard_map.91.masks, ...), custom_call_target="tpu_custom_call" | custom-call | flops 150994944 | bytes 4718592 | tf_op jit(solution)/shard_map/pallas_call | solution.py:30
  15.1 11.4 %all_to_all.15.received = bf16[8,144,128]{2,1,0:T(8,128)(2,1)S(1)} all-to-all(bf16[8,144,128]{2,1,0:T(8,128)(2,1)S(1)} %get-tuple-element.34), channel_id=1, replica_groups={{20,8,12,28,4,0,16,24},{21,9,13,29,5,1,17,25},{22,10,14,30,6,2,18,26},{..., dimensions={0} | all-to-all | bytes 589824 | tf_op jit(solution)/shard_map/all_to_all | solution.py:498
  26.5 2.3 %shard_map.93 = (bf16[128,1024]{1,0:T(8,128)(2,1)S(1)}, bf16[8,32,512]{2,1,0:T(8,128)(2,1)}, s32[8,512]{1,0:T(8,128)S(1)}) custom-call(bf16[8,144,128]{2,1,0:T(8,128)(2,1)S(1)} %all_to_all.15.received, bf16[32,1024]{1,0:T(8,128)(2,1)S(1)} %copy-done.3, bf16[32,2048]{1,0:T(8,128)(2,1)S(1)} %get-tuple-element.35.mirror_in, ...), custom_call_target="tpu_custom_call" | custom-call | flops 301989888 | bytes 294912 | tf_op jit(solution)/shard_map/pallas_call | solution.py:30
  28.8 4.5 %all-to-all-start.1 = ((bf16[8,32,512]{2,1,0:T(8,128)(2,1)}), bf16[8,32,512]{2,1,0:T(8,128)(2,1)S(1)}, u32[]{:S(2)}, u32[]{:S(2)}) async-start(bf16[8,32,512]{2,1,0:T(8,128)(2,1)} %get-tuple-element.37), calls=%async_computation.1 | async-start | bytes 524288 | tf_op jit(solution)/shard_map/all_to_all | solution.py:498
  33.3 1.2 %collective-permute-start.9 = (bf16[128,1024]{1,0:T(8,128)(2,1)S(1)}, bf16[128,1024]{1,0:T(8,128)(2,1)S(1)}, u32[]{:S(2)}, u32[]{:S(2)}) collective-permute-start(bf16[128,1024]{1,0:T(8,128)(2,1)S(1)} %get-tuple-element.46.refs_0_), channel_id=1, source_target_pairs={{0,2},{1,3},{2,0},{3,1},{4,6},{5,7},{6,4},{7,5},{8,10},{9,11},{10,... | collective-permute-start | bytes 786440 | tf_op jit(solution)/shard_map/ppermute | solution.py:505
  34.5 0.9 %copy-done.1 = bf16[256,256]{1,0:T(8,128)(2,1)S(1)} copy-done((bf16[256,256]{1,0:T(8,128)(2,1)S(1)}, bf16[256,256]{1,0:T(8,128)(2,1)}, u32[]{:S(2)}) %copy-start.1) | copy-done | bytes 131096
  35.4 0.9 %copy-done.2 = bf16[256,256]{1,0:T(8,128)(2,1)S(1)} copy-done((bf16[256,256]{1,0:T(8,128)(2,1)S(1)}, bf16[256,256]{1,0:T(8,128)(2,1)}, u32[]{:S(2)}) %copy-start.2) | copy-done | bytes 131096
  36.3 0.8 %copy-done.5 = bf16[128,256]{1,0:T(8,128)(2,1)S(1)} copy-done((bf16[128,256]{1,0:T(8,128)(2,1)S(1)}, bf16[128,256]{1,0:T(8,128)(2,1)}, u32[]{:S(2)}) %copy-start.5) | copy-done | bytes 65560
  37.1 0.2 shard_map.94.weights
  37.3 1.1 %all-to-all-done.1.received = bf16[8,32,512]{2,1,0:T(8,128)(2,1)S(1)} async-done(((bf16[8,32,512]{2,1,0:T(8,128)(2,1)}), bf16[8,32,512]{2,1,0:T(8,128)(2,1)S(1)}, u32[]{:S(2)}, u32[]{:S(2)}) %all-to-all-start.1) | async-done | bytes 262176 | tf_op jit(solution)/shard_map/all_to_all | solution.py:498
  38.4 0.7 shard_map.95.refs_4_
  39.1 4.9 %collective-permute-start.10 = (bf16[128,1024]{1,0:T(8,128)(2,1)S(1)}, bf16[128,1024]{1,0:T(8,128)(2,1)S(1)}, u32[]{:S(2)}, u32[]{:S(2)}) collective-permute-start(bf16[128,1024]{1,0:T(8,128)(2,1)S(1)} %get-tuple-element.46.refs_0_), channel_id=1, source_target_pairs={{0,1},{1,0},{2,3},{3,2},{4,5},{5,4},{6,7},{7,6},{8,9},{9,8},{10,11... | collective-permute-start | bytes 786440 | tf_op jit(solution)/shard_map/ppermute | solution.py:505
  44.0 0.1 collective-permute-start.11
  44.1 0.4 collective-permute-start.7
  44.5 1.2 %collective-permute-start.8 = (bf16[32,2048]{1,0:T(8,128)(2,1)S(1)}, bf16[32,2048]{1,0:T(8,128)(2,1)S(1)}, u32[]{:S(2)}, u32[]{:S(2)}) collective-permute-start(bf16[32,2048]{1,0:T(8,128)(2,1)S(1)} %shard_map.95.refs_4_), channel_id=1, source_target_pairs={{0,2},{1,3},{2,0},{3,1},{4,6},{5,7},{6,4},{7,5},{8,10},{9,11},{10,... | collective-permute-start | bytes 393224 | tf_op jit(solution)/shard_map/ppermute | solution.py:505
  45.8 0.0 collective-permute-done.10.refs_1_
  45.8 0.0 collective-permute-done.11.refs_3_
  45.8 0.5 shard_map.96
  46.3 3.3 %collective-permute-done.8.refs_6_ = bf16[32,2048]{1,0:T(8,128)(2,1)S(1)} collective-permute-done((bf16[32,2048]{1,0:T(8,128)(2,1)S(1)}, bf16[32,2048]{1,0:T(8,128)(2,1)S(1)}, u32[]{:S(2)}, u32[]{:S(2)}) %collective-permute-start.8) | collective-permute-done | bytes 131104 | tf_op jit(solution)/shard_map/ppermute | solution.py:505
  49.6 0.8 %collective-permute-start.12 = (bf16[32,2048]{1,0:T(8,128)(2,1)S(1)}, bf16[32,2048]{1,0:T(8,128)(2,1)S(1)}, u32[]{:S(2)}, u32[]{:S(2)}) collective-permute-start(bf16[32,2048]{1,0:T(8,128)(2,1)S(1)} %collective-permute-done.8.refs_6_), channel_id=1, source_target_pairs={{0,1},{1,0},{2,3},{3,2},{4,5},{5,4},{6,7},{7,6},{8,9},{9,8},{10,11... | collective-permute-start | bytes 393224 | tf_op jit(solution)/shard_map/ppermute | solution.py:505
  50.5 1.0 %collective-permute-done.12.refs_7_ = bf16[32,2048]{1,0:T(8,128)(2,1)S(1)} collective-permute-done((bf16[32,2048]{1,0:T(8,128)(2,1)S(1)}, bf16[32,2048]{1,0:T(8,128)(2,1)S(1)}, u32[]{:S(2)}, u32[]{:S(2)}) %collective-permute-start.12) | collective-permute-done | bytes 131104 | tf_op jit(solution)/shard_map/ppermute | solution.py:505
  51.4 2.8 %shard_map.97 = (f32[64,1024]{1,0:T(8,128)S(1)}, bf16[8,256,128]{2,1,0:T(8,128)(2,1)S(1)}) custom-call(s32[6,24]{1,0:T(8,128)S(1)} %bitcast.6, bf16[64,256]{1,0:T(8,128)(2,1)S(1)} %get-tuple-element.54.mirror_own, bf16[64,1024]{1,0:T(8,128)(2,1)S(1)} %get-tuple-element.55.own, f8e4m3fn[24,768,128]{2,1,0:T(32,128)(4,1)S(1)} %get-tuple-element.56.masks, ...), custom_call_target="tpu_custom_call" | custom-call | flops 301989888 | bytes 2359296 | tf_op jit(solution)/shard_map/pallas_call | solution.py:30
  54.3 15.7 %all_to_all.16.received = bf16[8,256,128]{2,1,0:T(8,128)(2,1)S(1)} all-to-all(bf16[8,256,128]{2,1,0:T(8,128)(2,1)S(1)} %get-tuple-element.60), channel_id=1, replica_groups={{20,8,12,28,4,0,16,24},{21,9,13,29,5,1,17,25},{22,10,14,30,6,2,18,26},{..., dimensions={0} | all-to-all | bytes 1048576 | tf_op jit(solution)/shard_map/all_to_all | solution.py:498
  69.9 0.7 shard_map.98.refs_0_
  70.7 1.3 %collective-permute-start.14 = (bf16[64,1024]{1,0:T(8,128)(2,1)S(1)}, bf16[64,1024]{1,0:T(8,128)(2,1)S(1)}, u32[]{:S(2)}, u32[]{:S(2)}) collective-permute-start(bf16[64,1024]{1,0:T(8,128)(2,1)S(1)} %shard_map.98.refs_0_), channel_id=1, source_target_pairs={{0,2},{1,3},{2,0},{3,1},{4,6},{5,7},{6,4},{7,5},{8,10},{9,11},{10,... | collective-permute-start | bytes 393224 | tf_op jit(solution)/shard_map/ppermute | solution.py:505
  72.0 2.4 %collective-permute-start.13 = (bf16[64,1024]{1,0:T(8,128)(2,1)S(1)}, bf16[64,1024]{1,0:T(8,128)(2,1)S(1)}, u32[]{:S(2)}, u32[]{:S(2)}) collective-permute-start(bf16[64,1024]{1,0:T(8,128)(2,1)S(1)} %shard_map.98.refs_0_), channel_id=1, source_target_pairs={{0,1},{1,0},{2,3},{3,2},{4,5},{5,4},{6,7},{7,6},{8,9},{9,8},{10,11... | collective-permute-start | bytes 393224 | tf_op jit(solution)/shard_map/ppermute | solution.py:505
  74.4 0.2 collective-permute-done.14.refs_2_
  74.6 3.3 %collective-permute-start.15 = (bf16[64,1024]{1,0:T(8,128)(2,1)S(1)}, bf16[64,1024]{1,0:T(8,128)(2,1)S(1)}, u32[]{:S(2)}, u32[]{:S(2)}) collective-permute-start(bf16[64,1024]{1,0:T(8,128)(2,1)S(1)} %collective-permute-done.14.refs_2_), channel_id=1, source_target_pairs={{0,1},{1,0},{2,3},{3,2},{4,5},{5,4},{6,7},{7,6},{8,9},{9,8},{10,11... | collective-permute-start | bytes 393224 | tf_op jit(solution)/shard_map/ppermute | solution.py:505
  77.9 0.1 slice.6.neigh_t
  78.0 0.2 shard_map.99.total
  78.2 0.7 collective-permute-done.15.refs_0_
  78.9 0.8 %shard_map.100 = bf16[64,1024]{1,0:T(8,128)(2,1)} custom-call(bf16[64,64]{1,0:T(8,128)(2,1)S(1)} %slice.6.neigh_t, f32[64,1024]{1,0:T(8,128)S(1)} %shard_map.99.total, bf16[64,1024]{1,0:T(8,128)(2,1)S(1)} %collective-permute-done.15.refs_0_), custom_call_target="tpu_custom_call" | custom-call | flops 8388608 | bytes 655360 | tf_op jit(solution)/shard_map/pallas_call | solution.py:30
  (15 shorter events, 0.0 us)
Async XLA Ops:
  0.0 11.8 %copy-start.3 = (bf16[32,1024]{1,0:T(8,128)(2,1)S(1)}, bf16[32,1024]{1,0:T(8,128)(2,1)}, u32[]{:S(2)}) copy-start(bf16[32,1024]{1,0:T(8,128)(2,1)} %features.1) | copy-start | bytes 196612
  0.0 11.8 %copy-start.6 = (s32[24,6]{0,1:T(8,128)S(1)}, s32[24,6]{0,1:T(8,128)}, u32[]{:S(2)}) copy-start(s32[24,6]{0,1:T(8,128)} %param.11) | copy-start | bytes 1732
  0.0 11.8 %copy-start = (s32[3,2048]{1,0:T(4,128)S(1)}, s32[3,2048]{1,0:T(4,128)}, u32[]{:S(2)}) copy-start(s32[3,2048]{1,0:T(4,128)} %reps.5) | copy-start | bytes 73732
  0.0 5.0 %collective-permute-start.3 = (bf16[32,1024]{1,0:T(8,128)(2,1)}, bf16[32,1024]{1,0:T(8,128)(2,1)S(1)}, u32[]{:S(2)}, u32[]{:S(2)}) collective-permute-start(bf16[32,1024]{1,0:T(8,128)(2,1)} %features.1), channel_id=1, source_target_pairs={{0,16},{4,20},{8,24},{12,28},{16,0},{20,4},{24,8},{28,12},{1,17},{... | collective-permute-start | bytes 196616 | tf_op jit(solution)/shard_map/ppermute | solution.py:524
  2.4 4.5 %collective-permute-start = (bf16[32,1024]{1,0:T(8,128)(2,1)}, bf16[32,1024]{1,0:T(8,128)(2,1)S(1)}, u32[]{:S(2)}, u32[]{:S(2)}) collective-permute-start(bf16[32,1024]{1,0:T(8,128)(2,1)} %features.1), channel_id=1, source_target_pairs={{0,4},{4,0},{8,12},{12,8},{16,20},{20,16},{24,28},{28,24},{1,5},{5... | collective-permute-start | bytes 196616 | tf_op jit(solution)/shard_map/ppermute | solution.py:524
  2.6 9.1 %collective-permute-start.1 = (bf16[32,1024]{1,0:T(8,128)(2,1)}, bf16[32,1024]{1,0:T(8,128)(2,1)S(1)}, u32[]{:S(2)}, u32[]{:S(2)}) collective-permute-start(bf16[32,1024]{1,0:T(8,128)(2,1)} %features.1), channel_id=1, source_target_pairs={{0,8},{4,12},{8,0},{12,4},{16,24},{20,28},{24,16},{28,20},{1,9},{5... | collective-permute-start | bytes 196616 | tf_op jit(solution)/shard_map/ppermute | solution.py:524
  3.9 7.8 %collective-permute-start.2 = (bf16[32,1024]{1,0:T(8,128)(2,1)}, bf16[32,1024]{1,0:T(8,128)(2,1)S(1)}, u32[]{:S(2)}, u32[]{:S(2)}) collective-permute-start(bf16[32,1024]{1,0:T(8,128)(2,1)} %features.1), channel_id=1, source_target_pairs={{0,12},{4,8},{8,4},{12,0},{16,28},{20,24},{24,20},{28,16},{1,13},{... | collective-permute-start | bytes 196616 | tf_op jit(solution)/shard_map/ppermute | solution.py:524
  5.0 6.7 %collective-permute-start.4 = (bf16[32,1024]{1,0:T(8,128)(2,1)S(1)}, bf16[32,1024]{1,0:T(8,128)(2,1)S(1)}, u32[]{:S(2)}, u32[]{:S(2)}) collective-permute-start(bf16[32,1024]{1,0:T(8,128)(2,1)S(1)} %collective-permute-done.3.refs_3_), channel_id=1, source_target_pairs={{0,4},{4,0},{8,12},{12,8},{16,20},{20,16},{24,28},{28,24},{1,5},{5... | collective-permute-start | bytes 196616 | tf_op jit(solution)/shard_map/ppermute | solution.py:524
  5.3 6.5 %collective-permute-start.5 = (bf16[32,1024]{1,0:T(8,128)(2,1)S(1)}, bf16[32,1024]{1,0:T(8,128)(2,1)S(1)}, u32[]{:S(2)}, u32[]{:S(2)}) collective-permute-start(bf16[32,1024]{1,0:T(8,128)(2,1)S(1)} %collective-permute-done.3.refs_3_), channel_id=1, source_target_pairs={{0,8},{4,12},{8,0},{12,4},{16,24},{20,28},{24,16},{28,20},{1,9},{5... | collective-permute-start | bytes 196616 | tf_op jit(solution)/shard_map/ppermute | solution.py:524
  6.8 4.9 %collective-permute-start.6 = (bf16[32,1024]{1,0:T(8,128)(2,1)S(1)}, bf16[32,1024]{1,0:T(8,128)(2,1)S(1)}, u32[]{:S(2)}, u32[]{:S(2)}) collective-permute-start(bf16[32,1024]{1,0:T(8,128)(2,1)S(1)} %collective-permute-done.3.refs_3_), channel_id=1, source_target_pairs={{0,12},{4,8},{8,4},{12,0},{16,28},{20,24},{24,20},{28,16},{1,13},{... | collective-permute-start | bytes 196616 | tf_op jit(solution)/shard_map/ppermute | solution.py:524
  11.7 14.8 %copy-start.7 = (s32[1024]{0:T(1024)S(1)}, s32[1024]{0:T(1024)}, u32[]{:S(2)}) copy-start(s32[1024]{0:T(1024)} %param.13) | copy-start | bytes 12292
  11.7 22.8 %copy-start.4 = (bf16[128,256]{1,0:T(8,128)(2,1)S(1)}, bf16[128,256]{1,0:T(8,128)(2,1)}, u32[]{:S(2)}) copy-start(bf16[128,256]{1,0:T(8,128)(2,1)} %self_one) | copy-start | bytes 196612
  28.8 9.6 %all-to-all-start.1 = ((bf16[8,32,512]{2,1,0:T(8,128)(2,1)}), bf16[8,32,512]{2,1,0:T(8,128)(2,1)S(1)}, u32[]{:S(2)}, u32[]{:S(2)}) async-start(bf16[8,32,512]{2,1,0:T(8,128)(2,1)} %get-tuple-element.37), calls=%async_computation.1 | async-start | bytes 524288 | tf_op jit(solution)/shard_map/all_to_all | solution.py:498
  33.3 5.8 %collective-permute-start.9 = (bf16[128,1024]{1,0:T(8,128)(2,1)S(1)}, bf16[128,1024]{1,0:T(8,128)(2,1)S(1)}, u32[]{:S(2)}, u32[]{:S(2)}) collective-permute-start(bf16[128,1024]{1,0:T(8,128)(2,1)S(1)} %get-tuple-element.46.refs_0_), channel_id=1, source_target_pairs={{0,2},{1,3},{2,0},{3,1},{4,6},{5,7},{6,4},{7,5},{8,10},{9,11},{10,... | collective-permute-start | bytes 786440 | tf_op jit(solution)/shard_map/ppermute | solution.py:505
  34.5 0.9 %copy-start.1 = (bf16[256,256]{1,0:T(8,128)(2,1)S(1)}, bf16[256,256]{1,0:T(8,128)(2,1)}, u32[]{:S(2)}) copy-start(bf16[256,256]{1,0:T(8,128)(2,1)} %self_two) | copy-start | bytes 393220
  35.4 0.9 %copy-start.2 = (bf16[256,256]{1,0:T(8,128)(2,1)S(1)}, bf16[256,256]{1,0:T(8,128)(2,1)}, u32[]{:S(2)}) copy-start(bf16[256,256]{1,0:T(8,128)(2,1)} %neigh_two) | copy-start | bytes 393220
  36.3 0.8 %copy-start.5 = (bf16[128,256]{1,0:T(8,128)(2,1)S(1)}, bf16[128,256]{1,0:T(8,128)(2,1)}, u32[]{:S(2)}) copy-start(bf16[128,256]{1,0:T(8,128)(2,1)} %neigh_one) | copy-start | bytes 196612
  39.1 6.6 %collective-permute-start.10 = (bf16[128,1024]{1,0:T(8,128)(2,1)S(1)}, bf16[128,1024]{1,0:T(8,128)(2,1)S(1)}, u32[]{:S(2)}, u32[]{:S(2)}) collective-permute-start(bf16[128,1024]{1,0:T(8,128)(2,1)S(1)} %get-tuple-element.46.refs_0_), channel_id=1, source_target_pairs={{0,1},{1,0},{2,3},{3,2},{4,5},{5,4},{6,7},{7,6},{8,9},{9,8},{10,11... | collective-permute-start | bytes 786440 | tf_op jit(solution)/shard_map/ppermute | solution.py:505
  44.0 1.7 %collective-permute-start.11 = (bf16[128,1024]{1,0:T(8,128)(2,1)S(1)}, bf16[128,1024]{1,0:T(8,128)(2,1)S(1)}, u32[]{:S(2)}, u32[]{:S(2)}) collective-permute-start(bf16[128,1024]{1,0:T(8,128)(2,1)S(1)} %collective-permute-done.9.refs_2_), channel_id=1, source_target_pairs={{0,1},{1,0},{2,3},{3,2},{4,5},{5,4},{6,7},{7,6},{8,9},{9,8},{10,11... | collective-permute-start | bytes 786440 | tf_op jit(solution)/shard_map/ppermute | solution.py:505
  44.1 2.2 %collective-permute-start.7 = (bf16[32,2048]{1,0:T(8,128)(2,1)S(1)}, bf16[32,2048]{1,0:T(8,128)(2,1)S(1)}, u32[]{:S(2)}, u32[]{:S(2)}) collective-permute-start(bf16[32,2048]{1,0:T(8,128)(2,1)S(1)} %shard_map.95.refs_4_), channel_id=1, source_target_pairs={{0,1},{1,0},{2,3},{3,2},{4,5},{5,4},{6,7},{7,6},{8,9},{9,8},{10,11... | collective-permute-start | bytes 393224 | tf_op jit(solution)/shard_map/ppermute | solution.py:505
  44.5 5.1 %collective-permute-start.8 = (bf16[32,2048]{1,0:T(8,128)(2,1)S(1)}, bf16[32,2048]{1,0:T(8,128)(2,1)S(1)}, u32[]{:S(2)}, u32[]{:S(2)}) collective-permute-start(bf16[32,2048]{1,0:T(8,128)(2,1)S(1)} %shard_map.95.refs_4_), channel_id=1, source_target_pairs={{0,2},{1,3},{2,0},{3,1},{4,6},{5,7},{6,4},{7,5},{8,10},{9,11},{10,... | collective-permute-start | bytes 393224 | tf_op jit(solution)/shard_map/ppermute | solution.py:505
  49.6 1.8 %collective-permute-start.12 = (bf16[32,2048]{1,0:T(8,128)(2,1)S(1)}, bf16[32,2048]{1,0:T(8,128)(2,1)S(1)}, u32[]{:S(2)}, u32[]{:S(2)}) collective-permute-start(bf16[32,2048]{1,0:T(8,128)(2,1)S(1)} %collective-permute-done.8.refs_6_), channel_id=1, source_target_pairs={{0,1},{1,0},{2,3},{3,2},{4,5},{5,4},{6,7},{7,6},{8,9},{9,8},{10,11... | collective-permute-start | bytes 393224 | tf_op jit(solution)/shard_map/ppermute | solution.py:505
  70.7 3.9 %collective-permute-start.14 = (bf16[64,1024]{1,0:T(8,128)(2,1)S(1)}, bf16[64,1024]{1,0:T(8,128)(2,1)S(1)}, u32[]{:S(2)}, u32[]{:S(2)}) collective-permute-start(bf16[64,1024]{1,0:T(8,128)(2,1)S(1)} %shard_map.98.refs_0_), channel_id=1, source_target_pairs={{0,2},{1,3},{2,0},{3,1},{4,6},{5,7},{6,4},{7,5},{8,10},{9,11},{10,... | collective-permute-start | bytes 393224 | tf_op jit(solution)/shard_map/ppermute | solution.py:505
  72.0 6.0 %collective-permute-start.13 = (bf16[64,1024]{1,0:T(8,128)(2,1)S(1)}, bf16[64,1024]{1,0:T(8,128)(2,1)S(1)}, u32[]{:S(2)}, u32[]{:S(2)}) collective-permute-start(bf16[64,1024]{1,0:T(8,128)(2,1)S(1)} %shard_map.98.refs_0_), channel_id=1, source_target_pairs={{0,1},{1,0},{2,3},{3,2},{4,5},{5,4},{6,7},{7,6},{8,9},{9,8},{10,11... | collective-permute-start | bytes 393224 | tf_op jit(solution)/shard_map/ppermute | solution.py:505
  74.6 4.3 %collective-permute-start.15 = (bf16[64,1024]{1,0:T(8,128)(2,1)S(1)}, bf16[64,1024]{1,0:T(8,128)(2,1)S(1)}, u32[]{:S(2)}, u32[]{:S(2)}) collective-permute-start(bf16[64,1024]{1,0:T(8,128)(2,1)S(1)} %collective-permute-done.14.refs_2_), channel_id=1, source_target_pairs={{0,1},{1,0},{2,3},{3,2},{4,5},{5,4},{6,7},{7,6},{8,9},{9,8},{10,11... | collective-permute-start | bytes 393224 | tf_op jit(solution)/shard_map/ppermute | solution.py:505

commit v5 on v3

--- a/solution.py
+++ b/solution.py
@@ -15,7 +15,7 @@
 SHIFT = 8
 CHUNK = 1 << SHIFT
 GROUP = 8
-ORDER = (4, 7, 2, 6, 1, 0, 5, 3)
+ORDER = (5, 2, 3, 7, 1, 0, 4, 6)
 INDEX_ROWS = 16
 VMEM = pl.BlockSpec(memory_space=pltpu.VMEM)
 SMEM = pl.BlockSpec(memory_space=pltpu.SMEM)
@@ -576,7 +576,7 @@
     )
     blocks = gather((mean_two,))
     total = self_part
-    for start, stop in ((0, 2), (2, 3), (3, 4)):
+    for start, stop in ((0, 3), (3, 4)):
         weights = neigh_two_own[:, start * hidden_feats : stop * hidden_feats]
         total = embed(weights, total, blocks[start:stop], BF16 if stop == feat else F32)
     return total

time: 81.4 us -> 80.1 us (0.984)
  blocking collectives: 27.9 us -> 26.6 us
  starting transfers between devices: 30.6 us -> 31.5 us
    ppermute x12, starting transfers between devices: 17.5 us -> 19.4 us  [swap(): return lax.ppermute(values, 'feat', [(i, i ^ k) for i in range(feat)])]
    all_to_all x2, blocking collectives: 27.9 us -> 26.6 us  [exchange(): lax.all_to_all(blocks, 'dom', split_axis=0, concat_axis=0, tiled=True, ax...]
    all_to_all x1, starting transfers between devices: 5.47 us -> 4.46 us  [exchange(): lax.all_to_all(blocks, 'dom', split_axis=0, concat_axis=0, tiled=True, ax...]
    pallas_call x12 -> x11, Pallas kernels: 18 us -> 17.8 us  [call(): pl.pallas_call(body, out_shape=out_shape, in_specs=[place(i) for i in ran...]
where the time goes in v5:
time: 80.1 us; the launch traced here: 79.3 us
  starting transfers between devices  31.5 us (39%)
  blocking collectives  26.6 us (33%)
  Pallas kernels  17.8 us (22%)
  waiting for transfers between devices  2.98 us (4%)
    all_to_all x2, blocking collectives, exchange(): lax.all_to_all(blocks, 'dom', split_axis=0, concat_axis=0, tiled=True, ax...  26.6 us
    ppermute x12, starting transfers between devices, swap(): return lax.ppermute(values, 'feat', [(i, i ^ k) for i in range(feat)])  19.4 us
    pallas_call x11, Pallas kernels, call(): pl.pallas_call(body, out_shape=out_shape, in_specs=[place(i) for i in ran...  17.8 us
    ppermute x7, starting transfers between devices, swap(): return lax.ppermute(values, 'dom', [(i, i ^ k) for i in range(dom)])  7.67 us
    all_to_all x1, starting transfers between devices, exchange(): lax.all_to_all(blocks, 'dom', split_axis=0, concat_axis=0, tiled=True, ax...  4.46 us
    ppermute x12, waiting for transfers between devices, swap(): return lax.ppermute(values, 'feat', [(i, i ^ k) for i in range(feat)])  2.96 us
  transfers between devices with their start and end apart: 20, of which 4 were waited for; matrix products, arithmetic and copies ran while one was open for 0% of the time, Pallas kernels for 9%

profile of v5, /device:TPU:5, one launch (start us, length us, event | category | flops | bytes accessed | tf_op | source)
XLA Modules:
  0.0 79.3 jit_solution(14731960294958875383)
XLA Ops:
  0.1 2.4 %collective-permute-start.3 = (bf16[32,1024]{1,0:T(8,128)(2,1)}, bf16[32,1024]{1,0:T(8,128)(2,1)S(1)}, u32[]{:S(2)}, u32[]{:S(2)}) collective-permute-start(bf16[32,1024]{1,0:T(8,128)(2,1)} %features.1), channel_id=1, source_target_pairs={{0,16},{4,20},{8,24},{12,28},{16,0},{20,4},{24,8},{28,12},{1,17},{... | collective-permute-start | bytes 196616 | tf_op jit(solution)/shard_map/ppermute | solution.py:516
  2.4 0.2 collective-permute-start
  2.7 1.3 %collective-permute-start.1 = (bf16[32,1024]{1,0:T(8,128)(2,1)}, bf16[32,1024]{1,0:T(8,128)(2,1)S(1)}, u32[]{:S(2)}, u32[]{:S(2)}) collective-permute-start(bf16[32,1024]{1,0:T(8,128)(2,1)} %features.1), channel_id=1, source_target_pairs={{0,8},{4,12},{8,0},{12,4},{16,24},{20,28},{24,16},{28,20},{1,9},{5... | collective-permute-start | bytes 196616 | tf_op jit(solution)/shard_map/ppermute | solution.py:516
  4.0 1.1 %collective-permute-start.2 = (bf16[32,1024]{1,0:T(8,128)(2,1)}, bf16[32,1024]{1,0:T(8,128)(2,1)S(1)}, u32[]{:S(2)}, u32[]{:S(2)}) collective-permute-start(bf16[32,1024]{1,0:T(8,128)(2,1)} %features.1), channel_id=1, source_target_pairs={{0,12},{4,8},{8,4},{12,0},{16,28},{20,24},{24,20},{28,16},{1,13},{... | collective-permute-start | bytes 196616 | tf_op jit(solution)/shard_map/ppermute | solution.py:516
  5.1 0.0 collective-permute-done.3.refs_3_
  5.1 0.2 collective-permute-start.4
  5.3 1.6 %collective-permute-start.5 = (bf16[32,1024]{1,0:T(8,128)(2,1)S(1)}, bf16[32,1024]{1,0:T(8,128)(2,1)S(1)}, u32[]{:S(2)}, u32[]{:S(2)}) collective-permute-start(bf16[32,1024]{1,0:T(8,128)(2,1)S(1)} %collective-permute-done.3.refs_3_), channel_id=1, source_target_pairs={{0,8},{4,12},{8,0},{12,4},{16,24},{20,28},{24,16},{28,20},{1,9},{5... | collective-permute-start | bytes 196616 | tf_op jit(solution)/shard_map/ppermute | solution.py:516
  6.9 0.0 collective-permute-done.refs_0_
  6.9 0.9 %collective-permute-start.6 = (bf16[32,1024]{1,0:T(8,128)(2,1)S(1)}, bf16[32,1024]{1,0:T(8,128)(2,1)S(1)}, u32[]{:S(2)}, u32[]{:S(2)}) collective-permute-start(bf16[32,1024]{1,0:T(8,128)(2,1)S(1)} %collective-permute-done.3.refs_3_), channel_id=1, source_target_pairs={{0,12},{4,8},{8,4},{12,0},{16,28},{20,24},{24,20},{28,16},{1,13},{... | collective-permute-start | bytes 196616 | tf_op jit(solution)/shard_map/ppermute | solution.py:516
  7.7 4.0 %shard_map.91.masks = bf16[24,768,128]{2,1,0:T(8,128)(2,1)S(1)} custom-call(s32[24,6,128,128]{3,2,1,0:T(8,128)} %tile_mask.1), custom_call_target="tpu_custom_call" | custom-call | bytes 14155776 | tf_op jit(solution)/shard_map/pallas_call | solution.py:32
  11.7 0.0 collective-permute-done.1.refs_1_
  11.7 0.0 collective-permute-done.2.refs_2_
  11.8 0.0 collective-permute-done.4.refs_4_
  11.8 0.0 collective-permute-done.5.refs_5_
  11.8 0.0 collective-permute-done.6.refs_6_
  11.8 3.8 %shard_map.92 = (f32[32,1024]{1,0:T(8,128)S(1)}, bf16[32,2048]{1,0:T(8,128)(2,1)S(1)}, bf16[8,144,128]{2,1,0:T(8,128)(2,1)S(1)}, f8e4m3fn[240,768,128]{2,1,0:T(32,128)(4,1)}) custom-call(s32[6,24]{1,0:T(8,128)S(1)} %bitcast.5, bf16[32,1024]{1,0:T(8,128)(2,1)S(1)} %copy-done.3, bf16[24,768,128]{2,1,0:T(8,128)(2,1)S(1)} %shard_map.91.masks, ...), custom_call_target="tpu_custom_call" | custom-call | flops 150994944 | bytes 4718592 | tf_op jit(solution)/shard_map/pallas_call | solution.py:32
  15.7 11.4 %all_to_all.15.received = bf16[8,144,128]{2,1,0:T(8,128)(2,1)S(1)} all-to-all(bf16[8,144,128]{2,1,0:T(8,128)(2,1)S(1)} %get-tuple-element.41), channel_id=1, replica_groups={{20,8,12,28,4,0,16,24},{21,9,13,29,5,1,17,25},{22,10,14,30,6,2,18,26},{..., dimensions={0} | all-to-all | bytes 589824 | tf_op jit(solution)/shard_map/all_to_all | solution.py:490
  27.1 2.4 %shard_map.93 = (bf16[64,1024]{1,0:T(8,128)(2,1)S(1)}, bf16[8,32,512]{2,1,0:T(8,128)(2,1)}, s32[8,512]{1,0:T(8,128)S(1)}) custom-call(bf16[8,144,128]{2,1,0:T(8,128)(2,1)S(1)} %all_to_all.15.received, bf16[32,1024]{1,0:T(8,128)(2,1)S(1)} %copy-done.3, f32[32,1024]{1,0:T(8,128)S(1)} %get-tuple-element.42.own, s32[1,1024]{1,0:T(1,128)S(1)} %bitcast.7), custom_call_target="tpu_custom_call" | custom-call | flops 301989888 | bytes 294912 | tf_op jit(solution)/shard_map/pallas_call | solution.py:32
  29.4 4.5 %all-to-all-start.1 = ((bf16[8,32,512]{2,1,0:T(8,128)(2,1)}), bf16[8,32,512]{2,1,0:T(8,128)(2,1)S(1)}, u32[]{:S(2)}, u32[]{:S(2)}) async-start(bf16[8,32,512]{2,1,0:T(8,128)(2,1)} %get-tuple-element.43), calls=%async_computation.1 | async-start | bytes 524288 | tf_op jit(solution)/shard_map/all_to_all | solution.py:490
  33.9 1.2 %collective-permute-start.10 = (bf16[64,1024]{1,0:T(8,128)(2,1)S(1)}, bf16[64,1024]{1,0:T(8,128)(2,1)S(1)}, u32[]{:S(2)}, u32[]{:S(2)}) collective-permute-start(bf16[64,1024]{1,0:T(8,128)(2,1)S(1)} %get-tuple-element.61.refs_0_), channel_id=1, source_target_pairs={{0,2},{1,3},{2,0},{3,1},{4,6},{5,7},{6,4},{7,5},{8,10},{9,11},{10,... | collective-permute-start | bytes 393224 | tf_op jit(solution)/shard_map/ppermute | solution.py:497
  35.1 0.3 collective-permute-start.13
  35.3 4.5 %collective-permute-start.9 = (bf16[64,1024]{1,0:T(8,128)(2,1)S(1)}, bf16[64,1024]{1,0:T(8,128)(2,1)S(1)}, u32[]{:S(2)}, u32[]{:S(2)}) collective-permute-start(bf16[64,1024]{1,0:T(8,128)(2,1)S(1)} %get-tuple-element.61.refs_0_), channel_id=1, source_target_pairs={{0,1},{1,0},{2,3},{3,2},{4,5},{5,4},{6,7},{7,6},{8,9},{9,8},{10,11... | collective-permute-start | bytes 393224 | tf_op jit(solution)/shard_map/ppermute | solution.py:497
  39.8 0.2 shard_map.94
  40.0 0.0 collective-permute-done.10.refs_2_
  40.1 2.7 %collective-permute-start.11 = (bf16[64,1024]{1,0:T(8,128)(2,1)S(1)}, bf16[64,1024]{1,0:T(8,128)(2,1)S(1)}, u32[]{:S(2)}, u32[]{:S(2)}) collective-permute-start(bf16[64,1024]{1,0:T(8,128)(2,1)S(1)} %collective-permute-done.10.refs_2_), channel_id=1, source_target_pairs={{0,1},{1,0},{2,3},{3,2},{4,5},{5,4},{6,7},{7,6},{8,9},{9,8},{10,11... | collective-permute-start | bytes 393224 | tf_op jit(solution)/shard_map/ppermute | solution.py:497
  42.8 0.0 all-to-all-done.1.received
  42.8 0.7 shard_map.95.refs_4_
  43.5 1.1 %collective-permute-start.7 = (bf16[32,2048]{1,0:T(8,128)(2,1)S(1)}, bf16[32,2048]{1,0:T(8,128)(2,1)S(1)}, u32[]{:S(2)}, u32[]{:S(2)}) collective-permute-start(bf16[32,2048]{1,0:T(8,128)(2,1)S(1)} %shard_map.95.refs_4_), channel_id=1, source_target_pairs={{0,1},{1,0},{2,3},{3,2},{4,5},{5,4},{6,7},{7,6},{8,9},{9,8},{10,11... | collective-permute-start | bytes 393224 | tf_op jit(solution)/shard_map/ppermute | solution.py:497
  44.6 1.2 %collective-permute-start.8 = (bf16[32,2048]{1,0:T(8,128)(2,1)S(1)}, bf16[32,2048]{1,0:T(8,128)(2,1)S(1)}, u32[]{:S(2)}, u32[]{:S(2)}) collective-permute-start(bf16[32,2048]{1,0:T(8,128)(2,1)S(1)} %shard_map.95.refs_4_), channel_id=1, source_target_pairs={{0,2},{1,3},{2,0},{3,1},{4,6},{5,7},{6,4},{7,5},{8,10},{9,11},{10,... | collective-permute-start | bytes 393224 | tf_op jit(solution)/shard_map/ppermute | solution.py:497
  45.8 1.6 %shard_map.96.masks = f8e4m3fn[24,768,128]{2,1,0:T(32,128)(4,1)S(1)} custom-call(f8e4m3fn[240,768,128]{2,1,0:T(32,128)(4,1)} %get-tuple-element.57.masks_hbm), custom_call_target="tpu_custom_call" | custom-call | bytes 4718592 | tf_op jit(solution)/shard_map/pallas_call | solution.py:32
  47.5 0.4 collective-permute-start.12
  47.9 0.2 collective-permute-start.14
  48.0 0.5 shard_map.97
  48.6 0.0 collective-permute-done.7.refs_5_
  48.6 1.1 %collective-permute-done.8.refs_6_ = bf16[32,2048]{1,0:T(8,128)(2,1)S(1)} collective-permute-done((bf16[32,2048]{1,0:T(8,128)(2,1)S(1)}, bf16[32,2048]{1,0:T(8,128)(2,1)S(1)}, u32[]{:S(2)}, u32[]{:S(2)}) %collective-permute-start.8) | collective-permute-done | bytes 131104 | tf_op jit(solution)/shard_map/ppermute | solution.py:497
  49.7 0.8 %collective-permute-start.15 = (bf16[32,2048]{1,0:T(8,128)(2,1)S(1)}, bf16[32,2048]{1,0:T(8,128)(2,1)S(1)}, u32[]{:S(2)}, u32[]{:S(2)}) collective-permute-start(bf16[32,2048]{1,0:T(8,128)(2,1)S(1)} %collective-permute-done.8.refs_6_), channel_id=1, source_target_pairs={{0,1},{1,0},{2,3},{3,2},{4,5},{5,4},{6,7},{7,6},{8,9},{9,8},{10,11... | collective-permute-start | bytes 393224 | tf_op jit(solution)/shard_map/ppermute | solution.py:497
  50.5 1.0 %collective-permute-done.15.refs_7_ = bf16[32,2048]{1,0:T(8,128)(2,1)S(1)} collective-permute-done((bf16[32,2048]{1,0:T(8,128)(2,1)S(1)}, bf16[32,2048]{1,0:T(8,128)(2,1)S(1)}, u32[]{:S(2)}, u32[]{:S(2)}) %collective-permute-start.15) | collective-permute-done | bytes 131104 | tf_op jit(solution)/shard_map/ppermute | solution.py:497
  51.5 2.8 %shard_map.98 = (f32[64,1024]{1,0:T(8,128)S(1)}, bf16[8,256,128]{2,1,0:T(8,128)(2,1)S(1)}) custom-call(s32[6,24]{1,0:T(8,128)S(1)} %bitcast.6, bf16[64,256]{1,0:T(8,128)(2,1)S(1)} %get-tuple-element.67.mirror_own, bf16[64,1024]{1,0:T(8,128)(2,1)S(1)} %get-tuple-element.68.own, f8e4m3fn[24,768,128]{2,1,0:T(32,128)(4,1)S(1)} %shard_map.96.masks, ...), custom_call_target="tpu_custom_call" | custom-call | flops 301989888 | bytes 2359296 | tf_op jit(solution)/shard_map/pallas_call | solution.py:32
  54.3 15.2 %all_to_all.16.received = bf16[8,256,128]{2,1,0:T(8,128)(2,1)S(1)} all-to-all(bf16[8,256,128]{2,1,0:T(8,128)(2,1)S(1)} %get-tuple-element.74), channel_id=1, replica_groups={{20,8,12,28,4,0,16,24},{21,9,13,29,5,1,17,25},{22,10,14,30,6,2,18,26},{..., dimensions={0} | all-to-all | bytes 1048576 | tf_op jit(solution)/shard_map/all_to_all | solution.py:490
  69.5 0.8 shard_map.99.refs_0_
  70.3 1.3 %collective-permute-start.17 = (bf16[64,1024]{1,0:T(8,128)(2,1)S(1)}, bf16[64,1024]{1,0:T(8,128)(2,1)S(1)}, u32[]{:S(2)}, u32[]{:S(2)}) collective-permute-start(bf16[64,1024]{1,0:T(8,128)(2,1)S(1)} %shard_map.99.refs_0_), channel_id=1, source_target_pairs={{0,2},{1,3},{2,0},{3,1},{4,6},{5,7},{6,4},{7,5},{8,10},{9,11},{10,... | collective-permute-start | bytes 393224 | tf_op jit(solution)/shard_map/ppermute | solution.py:497
  71.6 2.4 %collective-permute-start.16 = (bf16[64,1024]{1,0:T(8,128)(2,1)S(1)}, bf16[64,1024]{1,0:T(8,128)(2,1)S(1)}, u32[]{:S(2)}, u32[]{:S(2)}) collective-permute-start(bf16[64,1024]{1,0:T(8,128)(2,1)S(1)} %shard_map.99.refs_0_), channel_id=1, source_target_pairs={{0,1},{1,0},{2,3},{3,2},{4,5},{5,4},{6,7},{7,6},{8,9},{9,8},{10,11... | collective-permute-start | bytes 393224 | tf_op jit(solution)/shard_map/ppermute | solution.py:497
  74.0 0.2 collective-permute-done.17.refs_2_
  74.2 3.3 %collective-permute-start.18 = (bf16[64,1024]{1,0:T(8,128)(2,1)S(1)}, bf16[64,1024]{1,0:T(8,128)(2,1)S(1)}, u32[]{:S(2)}, u32[]{:S(2)}) collective-permute-start(bf16[64,1024]{1,0:T(8,128)(2,1)S(1)} %collective-permute-done.17.refs_2_), channel_id=1, source_target_pairs={{0,1},{1,0},{2,3},{3,2},{4,5},{5,4},{6,7},{7,6},{8,9},{9,8},{10,11... | collective-permute-start | bytes 393224 | tf_op jit(solution)/shard_map/ppermute | solution.py:497
  77.5 0.1 slice.6.neigh_t
  77.5 0.2 shard_map.100.total
  77.7 0.7 collective-permute-done.18.refs_0_
  78.4 0.8 %shard_map.101 = bf16[64,1024]{1,0:T(8,128)(2,1)} custom-call(bf16[64,64]{1,0:T(8,128)(2,1)S(1)} %slice.6.neigh_t, f32[64,1024]{1,0:T(8,128)S(1)} %shard_map.100.total, bf16[64,1024]{1,0:T(8,128)(2,1)S(1)} %collective-permute-done.18.refs_0_), custom_call_target="tpu_custom_call" | custom-call | flops 8388608 | bytes 655360 | tf_op jit(solution)/shard_map/pallas_call | solution.py:32
  (22 shorter events, 0.0 us)
Async XLA Ops:
  0.0 11.8 %copy-start.3 = (bf16[32,1024]{1,0:T(8,128)(2,1)S(1)}, bf16[32,1024]{1,0:T(8,128)(2,1)}, u32[]{:S(2)}) copy-start(bf16[32,1024]{1,0:T(8,128)(2,1)} %features.1) | copy-start | bytes 196612
  0.0 11.8 %copy-start.6 = (s32[24,6]{0,1:T(8,128)S(1)}, s32[24,6]{0,1:T(8,128)}, u32[]{:S(2)}) copy-start(s32[24,6]{0,1:T(8,128)} %param.11) | copy-start | bytes 1732
  0.0 11.8 %copy-start = (s32[3,2048]{1,0:T(4,128)S(1)}, s32[3,2048]{1,0:T(4,128)}, u32[]{:S(2)}) copy-start(s32[3,2048]{1,0:T(4,128)} %reps.5) | copy-start | bytes 73732
  0.0 27.0 %copy-start.7 = (s32[1024]{0:T(1024)S(1)}, s32[1024]{0:T(1024)}, u32[]{:S(2)}) copy-start(s32[1024]{0:T(1024)} %param.13) | copy-start | bytes 12292
  0.0 39.8 %copy-start.4 = (bf16[128,256]{1,0:T(8,128)(2,1)S(1)}, bf16[128,256]{1,0:T(8,128)(2,1)}, u32[]{:S(2)}) copy-start(bf16[128,256]{1,0:T(8,128)(2,1)} %self_one) | copy-start | bytes 196612
  0.0 39.8 %copy-start.5 = (bf16[128,256]{1,0:T(8,128)(2,1)S(1)}, bf16[128,256]{1,0:T(8,128)(2,1)}, u32[]{:S(2)}) copy-start(bf16[128,256]{1,0:T(8,128)(2,1)} %neigh_one) | copy-start | bytes 196612
  0.0 39.8 %copy-start.1 = (bf16[256,256]{1,0:T(8,128)(2,1)S(1)}, bf16[256,256]{1,0:T(8,128)(2,1)}, u32[]{:S(2)}) copy-start(bf16[256,256]{1,0:T(8,128)(2,1)} %self_two) | copy-start | bytes 393220
  0.0 39.8 %copy-start.2 = (bf16[256,256]{1,0:T(8,128)(2,1)S(1)}, bf16[256,256]{1,0:T(8,128)(2,1)}, u32[]{:S(2)}) copy-start(bf16[256,256]{1,0:T(8,128)(2,1)} %neigh_two) | copy-start | bytes 393220
  0.1 5.0 %collective-permute-start.3 = (bf16[32,1024]{1,0:T(8,128)(2,1)}, bf16[32,1024]{1,0:T(8,128)(2,1)S(1)}, u32[]{:S(2)}, u32[]{:S(2)}) collective-permute-start(bf16[32,1024]{1,0:T(8,128)(2,1)} %features.1), channel_id=1, source_target_pairs={{0,16},{4,20},{8,24},{12,28},{16,0},{20,4},{24,8},{28,12},{1,17},{... | collective-permute-start | bytes 196616 | tf_op jit(solution)/shard_map/ppermute | solution.py:516
  2.4 4.5 %collective-permute-start = (bf16[32,1024]{1,0:T(8,128)(2,1)}, bf16[32,1024]{1,0:T(8,128)(2,1)S(1)}, u32[]{:S(2)}, u32[]{:S(2)}) collective-permute-start(bf16[32,1024]{1,0:T(8,128)(2,1)} %features.1), channel_id=1, source_target_pairs={{0,4},{4,0},{8,12},{12,8},{16,20},{20,16},{24,28},{28,24},{1,5},{5... | collective-permute-start | bytes 196616 | tf_op jit(solution)/shard_map/ppermute | solution.py:516
  2.7 9.1 %collective-permute-start.1 = (bf16[32,1024]{1,0:T(8,128)(2,1)}, bf16[32,1024]{1,0:T(8,128)(2,1)S(1)}, u32[]{:S(2)}, u32[]{:S(2)}) collective-permute-start(bf16[32,1024]{1,0:T(8,128)(2,1)} %features.1), channel_id=1, source_target_pairs={{0,8},{4,12},{8,0},{12,4},{16,24},{20,28},{24,16},{28,20},{1,9},{5... | collective-permute-start | bytes 196616 | tf_op jit(solution)/shard_map/ppermute | solution.py:516
  4.0 7.8 %collective-permute-start.2 = (bf16[32,1024]{1,0:T(8,128)(2,1)}, bf16[32,1024]{1,0:T(8,128)(2,1)S(1)}, u32[]{:S(2)}, u32[]{:S(2)}) collective-permute-start(bf16[32,1024]{1,0:T(8,128)(2,1)} %features.1), channel_id=1, source_target_pairs={{0,12},{4,8},{8,4},{12,0},{16,28},{20,24},{24,20},{28,16},{1,13},{... | collective-permute-start | bytes 196616 | tf_op jit(solution)/shard_map/ppermute | solution.py:516
  5.1 6.7 %collective-permute-start.4 = (bf16[32,1024]{1,0:T(8,128)(2,1)S(1)}, bf16[32,1024]{1,0:T(8,128)(2,1)S(1)}, u32[]{:S(2)}, u32[]{:S(2)}) collective-permute-start(bf16[32,1024]{1,0:T(8,128)(2,1)S(1)} %collective-permute-done.3.refs_3_), channel_id=1, source_target_pairs={{0,4},{4,0},{8,12},{12,8},{16,20},{20,16},{24,28},{28,24},{1,5},{5... | collective-permute-start | bytes 196616 | tf_op jit(solution)/shard_map/ppermute | solution.py:516
  5.3 6.5 %collective-permute-start.5 = (bf16[32,1024]{1,0:T(8,128)(2,1)S(1)}, bf16[32,1024]{1,0:T(8,128)(2,1)S(1)}, u32[]{:S(2)}, u32[]{:S(2)}) collective-permute-start(bf16[32,1024]{1,0:T(8,128)(2,1)S(1)} %collective-permute-done.3.refs_3_), channel_id=1, source_target_pairs={{0,8},{4,12},{8,0},{12,4},{16,24},{20,28},{24,16},{28,20},{1,9},{5... | collective-permute-start | bytes 196616 | tf_op jit(solution)/shard_map/ppermute | solution.py:516
  6.9 4.9 %collective-permute-start.6 = (bf16[32,1024]{1,0:T(8,128)(2,1)S(1)}, bf16[32,1024]{1,0:T(8,128)(2,1)S(1)}, u32[]{:S(2)}, u32[]{:S(2)}) collective-permute-start(bf16[32,1024]{1,0:T(8,128)(2,1)S(1)} %collective-permute-done.3.refs_3_), channel_id=1, source_target_pairs={{0,12},{4,8},{8,4},{12,0},{16,28},{20,24},{24,20},{28,16},{1,13},{... | collective-permute-start | bytes 196616 | tf_op jit(solution)/shard_map/ppermute | solution.py:516
  29.4 13.4 %all-to-all-start.1 = ((bf16[8,32,512]{2,1,0:T(8,128)(2,1)}), bf16[8,32,512]{2,1,0:T(8,128)(2,1)S(1)}, u32[]{:S(2)}, u32[]{:S(2)}) async-start(bf16[8,32,512]{2,1,0:T(8,128)(2,1)} %get-tuple-element.43), calls=%async_computation.1 | async-start | bytes 524288 | tf_op jit(solution)/shard_map/all_to_all | solution.py:490
  33.9 6.2 %collective-permute-start.10 = (bf16[64,1024]{1,0:T(8,128)(2,1)S(1)}, bf16[64,1024]{1,0:T(8,128)(2,1)S(1)}, u32[]{:S(2)}, u32[]{:S(2)}) collective-permute-start(bf16[64,1024]{1,0:T(8,128)(2,1)S(1)} %get-tuple-element.61.refs_0_), channel_id=1, source_target_pairs={{0,2},{1,3},{2,0},{3,1},{4,6},{5,7},{6,4},{7,5},{8,10},{9,11},{10,... | collective-permute-start | bytes 393224 | tf_op jit(solution)/shard_map/ppermute | solution.py:497
  35.1 12.4 %collective-permute-start.13 = (bf16[32,2048]{1,0:T(8,128)(2,1)S(1)}, bf16[32,2048]{1,0:T(8,128)(2,1)S(1)}, u32[]{:S(2)}, u32[]{:S(2)}) collective-permute-start(bf16[32,2048]{1,0:T(8,128)(2,1)S(1)} %get-tuple-element.70.refs_0_), channel_id=1, source_target_pairs={{0,2},{1,3},{2,0},{3,1},{4,6},{5,7},{6,4},{7,5},{8,10},{9,11},{10,... | collective-permute-start | bytes 393224 | tf_op jit(solution)/shard_map/ppermute | solution.py:497
  35.3 12.5 %collective-permute-start.9 = (bf16[64,1024]{1,0:T(8,128)(2,1)S(1)}, bf16[64,1024]{1,0:T(8,128)(2,1)S(1)}, u32[]{:S(2)}, u32[]{:S(2)}) collective-permute-start(bf16[64,1024]{1,0:T(8,128)(2,1)S(1)} %get-tuple-element.61.refs_0_), channel_id=1, source_target_pairs={{0,1},{1,0},{2,3},{3,2},{4,5},{5,4},{6,7},{7,6},{8,9},{9,8},{10,11... | collective-permute-start | bytes 393224 | tf_op jit(solution)/shard_map/ppermute | solution.py:497
  40.1 8.0 %collective-permute-start.11 = (bf16[64,1024]{1,0:T(8,128)(2,1)S(1)}, bf16[64,1024]{1,0:T(8,128)(2,1)S(1)}, u32[]{:S(2)}, u32[]{:S(2)}) collective-permute-start(bf16[64,1024]{1,0:T(8,128)(2,1)S(1)} %collective-permute-done.10.refs_2_), channel_id=1, source_target_pairs={{0,1},{1,0},{2,3},{3,2},{4,5},{5,4},{6,7},{7,6},{8,9},{9,8},{10,11... | collective-permute-start | bytes 393224 | tf_op jit(solution)/shard_map/ppermute | solution.py:497
  43.5 5.1 %collective-permute-start.7 = (bf16[32,2048]{1,0:T(8,128)(2,1)S(1)}, bf16[32,2048]{1,0:T(8,128)(2,1)S(1)}, u32[]{:S(2)}, u32[]{:S(2)}) collective-permute-start(bf16[32,2048]{1,0:T(8,128)(2,1)S(1)} %shard_map.95.refs_4_), channel_id=1, source_target_pairs={{0,1},{1,0},{2,3},{3,2},{4,5},{5,4},{6,7},{7,6},{8,9},{9,8},{10,11... | collective-permute-start | bytes 393224 | tf_op jit(solution)/shard_map/ppermute | solution.py:497
  44.6 5.1 %collective-permute-start.8 = (bf16[32,2048]{1,0:T(8,128)(2,1)S(1)}, bf16[32,2048]{1,0:T(8,128)(2,1)S(1)}, u32[]{:S(2)}, u32[]{:S(2)}) collective-permute-start(bf16[32,2048]{1,0:T(8,128)(2,1)S(1)} %shard_map.95.refs_4_), channel_id=1, source_target_pairs={{0,2},{1,3},{2,0},{3,1},{4,6},{5,7},{6,4},{7,5},{8,10},{9,11},{10,... | collective-permute-start | bytes 393224 | tf_op jit(solution)/shard_map/ppermute | solution.py:497
  47.5 3.1 %collective-permute-start.12 = (bf16[32,2048]{1,0:T(8,128)(2,1)S(1)}, bf16[32,2048]{1,0:T(8,128)(2,1)S(1)}, u32[]{:S(2)}, u32[]{:S(2)}) collective-permute-start(bf16[32,2048]{1,0:T(8,128)(2,1)S(1)} %get-tuple-element.70.refs_0_), channel_id=1, source_target_pairs={{0,1},{1,0},{2,3},{3,2},{4,5},{5,4},{6,7},{7,6},{8,9},{9,8},{10,11... | collective-permute-start | bytes 393224 | tf_op jit(solution)/shard_map/ppermute | solution.py:497
  47.9 2.6 %collective-permute-start.14 = (bf16[32,2048]{1,0:T(8,128)(2,1)S(1)}, bf16[32,2048]{1,0:T(8,128)(2,1)S(1)}, u32[]{:S(2)}, u32[]{:S(2)}) collective-permute-start(bf16[32,2048]{1,0:T(8,128)(2,1)S(1)} %collective-permute-done.13.refs_2_), channel_id=1, source_target_pairs={{0,1},{1,0},{2,3},{3,2},{4,5},{5,4},{6,7},{7,6},{8,9},{9,8},{10,11... | collective-permute-start | bytes 393224 | tf_op jit(solution)/shard_map/ppermute | solution.py:497
  49.7 1.8 %collective-permute-start.15 = (bf16[32,2048]{1,0:T(8,128)(2,1)S(1)}, bf16[32,2048]{1,0:T(8,128)(2,1)S(1)}, u32[]{:S(2)}, u32[]{:S(2)}) collective-permute-start(bf16[32,2048]{1,0:T(8,128)(2,1)S(1)} %collective-permute-done.8.refs_6_), channel_id=1, source_target_pairs={{0,1},{1,0},{2,3},{3,2},{4,5},{5,4},{6,7},{7,6},{8,9},{9,8},{10,11... | collective-permute-start | bytes 393224 | tf_op jit(solution)/shard_map/ppermute | solution.py:497
  70.3 3.9 %collective-permute-start.17 = (bf16[64,1024]{1,0:T(8,128)(2,1)S(1)}, bf16[64,1024]{1,0:T(8,128)(2,1)S(1)}, u32[]{:S(2)}, u32[]{:S(2)}) collective-permute-start(bf16[64,1024]{1,0:T(8,128)(2,1)S(1)} %shard_map.99.refs_0_), channel_id=1, source_target_pairs={{0,2},{1,3},{2,0},{3,1},{4,6},{5,7},{6,4},{7,5},{8,10},{9,11},{10,... | collective-permute-start | bytes 393224 | tf_op jit(solution)/shard_map/ppermute | solution.py:497
  71.6 6.0 %collective-permute-start.16 = (bf16[64,1024]{1,0:T(8,128)(2,1)S(1)}, bf16[64,1024]{1,0:T(8,128)(2,1)S(1)}, u32[]{:S(2)}, u32[]{:S(2)}) collective-permute-start(bf16[64,1024]{1,0:T(8,128)(2,1)S(1)} %shard_map.99.refs_0_), channel_id=1, source_target_pairs={{0,1},{1,0},{2,3},{3,2},{4,5},{5,4},{6,7},{7,6},{8,9},{9,8},{10,11... | collective-permute-start | bytes 393224 | tf_op jit(solution)/shard_map/ppermute | solution.py:497
  74.2 4.3 %collective-permute-start.18 = (bf16[64,1024]{1,0:T(8,128)(2,1)S(1)}, bf16[64,1024]{1,0:T(8,128)(2,1)S(1)}, u32[]{:S(2)}, u32[]{:S(2)}) collective-permute-start(bf16[64,1024]{1,0:T(8,128)(2,1)S(1)} %collective-permute-done.17.refs_2_), channel_id=1, source_target_pairs={{0,1},{1,0},{2,3},{3,2},{4,5},{5,4},{6,7},{7,6},{8,9},{9,8},{10,11... | collective-permute-start | bytes 393224 | tf_op jit(solution)/shard_map/ppermute | solution.py:497

commit v6 on v5

--- a/solution.py
+++ b/solution.py
@@ -15,7 +15,7 @@
 SHIFT = 8
 CHUNK = 1 << SHIFT
 GROUP = 8
-ORDER = (5, 2, 3, 7, 1, 0, 4, 6)
+ORDER = (5, 3, 2, 7, 1, 0, 4, 6)
 INDEX_ROWS = 16
 VMEM = pl.BlockSpec(memory_space=pltpu.VMEM)
 SMEM = pl.BlockSpec(memory_space=pltpu.SMEM)
@@ -561,9 +561,7 @@
         flops=2 * masters * (4 * self_one.size + self_two_own.size),
         moved=masters * 1024,
     )
-    means, near_masks, hidden, self_part, neigh_two_own = together(
-        (means, near_masks, hidden, self_part, neigh_two_own)
-    )
+    means, near_masks, neigh_two_own = together((means, near_masks, neigh_two_own))
     own_two, outgoing = second_sums(
         order, cols, gather((mirror_in,)), gather(means), mirror_own, hidden, near_masks, replicas, capacity
     )

time: 80.1 us -> 80.1 us (level)
  waiting for transfers between devices: 2.98 us -> 5.88 us
  starting transfers between devices: 31.5 us -> 28.7 us
    all_to_all x1, waiting for transfers between devices: 0.01 us -> 3.44 us  [exchange(): lax.all_to_all(blocks, 'dom', split_axis=0, concat_axis=0, tiled=True, ax...]
    ppermute x12, starting transfers between devices: 19.4 us -> 16.5 us  [swap(): return lax.ppermute(values, 'feat', [(i, i ^ k) for i in range(feat)])]
  transfers between devices with their start and end apart: 20 -> 20, of which waited for: 4 -> 5; matrix products, arithmetic and copies ran while one was open for 0% -> 0% of each run, Pallas kernels for 9% -> 9%
where the time goes in v6:
time: 80.1 us; the launch traced here: 79.3 us
  starting transfers between devices  28.7 us (36%)
  blocking collectives  26.6 us (33%)
  Pallas kernels  17.8 us (22%)
  waiting for transfers between devices  5.88 us (7%)
    all_to_all x2, blocking collectives, exchange(): lax.all_to_all(blocks, 'dom', split_axis=0, concat_axis=0, tiled=True, ax...  26.6 us
    pallas_call x11, Pallas kernels, call(): pl.pallas_call(body, out_shape=out_shape, in_specs=[place(i) for i in ran...  17.8 us
    ppermute x12, starting transfers between devices, swap(): return lax.ppermute(values, 'feat', [(i, i ^ k) for i in range(feat)])  16.5 us
    ppermute x7, starting transfers between devices, swap(): return lax.ppermute(values, 'dom', [(i, i ^ k) for i in range(dom)])  7.67 us
    all_to_all x1, starting transfers between devices, exchange(): lax.all_to_all(blocks, 'dom', split_axis=0, concat_axis=0, tiled=True, ax...  4.46 us
    all_to_all x1, waiting for transfers between devices, exchange(): lax.all_to_all(blocks, 'dom', split_axis=0, concat_axis=0, tiled=True, ax...  3.44 us
    ppermute x12, waiting for transfers between devices, swap(): return lax.ppermute(values, 'feat', [(i, i ^ k) for i in range(feat)])  2.42 us
  transfers between devices with their start and end apart: 20, of which 5 were waited for; matrix products, arithmetic and copies ran while one was open for 0% of the time, Pallas kernels for 9%

profile of v6, /device:TPU:5, one launch (start us, length us, event | category | flops | bytes accessed | tf_op | source)
XLA Modules:
  0.0 79.3 jit_solution(18000735963747155683)
XLA Ops:
  0.1 2.4 %collective-permute-start.3 = (bf16[32,1024]{1,0:T(8,128)(2,1)}, bf16[32,1024]{1,0:T(8,128)(2,1)S(1)}, u32[]{:S(2)}, u32[]{:S(2)}) collective-permute-start(bf16[32,1024]{1,0:T(8,128)(2,1)} %features.1), channel_id=1, source_target_pairs={{0,16},{4,20},{8,24},{12,28},{16,0},{20,4},{24,8},{28,12},{1,17},{... | collective-permute-start | bytes 196616 | tf_op jit(solution)/shard_map/ppermute | solution.py:516
  2.4 0.2 collective-permute-start
  2.7 1.3 %collective-permute-start.1 = (bf16[32,1024]{1,0:T(8,128)(2,1)}, bf16[32,1024]{1,0:T(8,128)(2,1)S(1)}, u32[]{:S(2)}, u32[]{:S(2)}) collective-permute-start(bf16[32,1024]{1,0:T(8,128)(2,1)} %features.1), channel_id=1, source_target_pairs={{0,8},{4,12},{8,0},{12,4},{16,24},{20,28},{24,16},{28,20},{1,9},{5... | collective-permute-start | bytes 196616 | tf_op jit(solution)/shard_map/ppermute | solution.py:516
  4.0 1.1 %collective-permute-start.2 = (bf16[32,1024]{1,0:T(8,128)(2,1)}, bf16[32,1024]{1,0:T(8,128)(2,1)S(1)}, u32[]{:S(2)}, u32[]{:S(2)}) collective-permute-start(bf16[32,1024]{1,0:T(8,128)(2,1)} %features.1), channel_id=1, source_target_pairs={{0,12},{4,8},{8,4},{12,0},{16,28},{20,24},{24,20},{28,16},{1,13},{... | collective-permute-start | bytes 196616 | tf_op jit(solution)/shard_map/ppermute | solution.py:516
  5.1 0.0 collective-permute-done.3.refs_3_
  5.1 0.2 collective-permute-start.4
  5.3 1.6 %collective-permute-start.5 = (bf16[32,1024]{1,0:T(8,128)(2,1)S(1)}, bf16[32,1024]{1,0:T(8,128)(2,1)S(1)}, u32[]{:S(2)}, u32[]{:S(2)}) collective-permute-start(bf16[32,1024]{1,0:T(8,128)(2,1)S(1)} %collective-permute-done.3.refs_3_), channel_id=1, source_target_pairs={{0,8},{4,12},{8,0},{12,4},{16,24},{20,28},{24,16},{28,20},{1,9},{5... | collective-permute-start | bytes 196616 | tf_op jit(solution)/shard_map/ppermute | solution.py:516
  6.9 0.0 collective-permute-done.refs_0_
  6.9 0.9 %collective-permute-start.6 = (bf16[32,1024]{1,0:T(8,128)(2,1)S(1)}, bf16[32,1024]{1,0:T(8,128)(2,1)S(1)}, u32[]{:S(2)}, u32[]{:S(2)}) collective-permute-start(bf16[32,1024]{1,0:T(8,128)(2,1)S(1)} %collective-permute-done.3.refs_3_), channel_id=1, source_target_pairs={{0,12},{4,8},{8,4},{12,0},{16,28},{20,24},{24,20},{28,16},{1,13},{... | collective-permute-start | bytes 196616 | tf_op jit(solution)/shard_map/ppermute | solution.py:516
  7.7 4.0 %shard_map.91.masks = bf16[24,768,128]{2,1,0:T(8,128)(2,1)S(1)} custom-call(s32[24,6,128,128]{3,2,1,0:T(8,128)} %tile_mask.1), custom_call_target="tpu_custom_call" | custom-call | bytes 14155776 | tf_op jit(solution)/shard_map/pallas_call | solution.py:32
  11.7 0.0 collective-permute-done.1.refs_1_
  11.7 0.0 collective-permute-done.2.refs_2_
  11.8 0.0 collective-permute-done.4.refs_4_
  11.8 0.0 collective-permute-done.5.refs_5_
  11.8 0.0 collective-permute-done.6.refs_6_
  11.8 3.8 %shard_map.92 = (f32[32,1024]{1,0:T(8,128)S(1)}, bf16[32,2048]{1,0:T(8,128)(2,1)S(1)}, bf16[8,144,128]{2,1,0:T(8,128)(2,1)S(1)}, f8e4m3fn[240,768,128]{2,1,0:T(32,128)(4,1)}) custom-call(s32[6,24]{1,0:T(8,128)S(1)} %bitcast.5, bf16[32,1024]{1,0:T(8,128)(2,1)S(1)} %copy-done.3, bf16[24,768,128]{2,1,0:T(8,128)(2,1)S(1)} %shard_map.91.masks, ...), custom_call_target="tpu_custom_call" | custom-call | flops 150994944 | bytes 4718592 | tf_op jit(solution)/shard_map/pallas_call | solution.py:32
  15.7 11.4 %all_to_all.15.received = bf16[8,144,128]{2,1,0:T(8,128)(2,1)S(1)} all-to-all(bf16[8,144,128]{2,1,0:T(8,128)(2,1)S(1)} %get-tuple-element.39), channel_id=1, replica_groups={{20,12,8,28,4,0,16,24},{21,13,9,29,5,1,17,25},{22,14,10,30,6,2,18,26},{..., dimensions={0} | all-to-all | bytes 589824 | tf_op jit(solution)/shard_map/all_to_all | solution.py:490
  27.0 2.4 %shard_map.93 = (bf16[64,1024]{1,0:T(8,128)(2,1)S(1)}, bf16[8,32,512]{2,1,0:T(8,128)(2,1)}, s32[8,512]{1,0:T(8,128)S(1)}) custom-call(bf16[8,144,128]{2,1,0:T(8,128)(2,1)S(1)} %all_to_all.15.received, bf16[32,1024]{1,0:T(8,128)(2,1)S(1)} %copy-done.3, f32[32,1024]{1,0:T(8,128)S(1)} %get-tuple-element.40.own, s32[1,1024]{1,0:T(1,128)S(1)} %bitcast.7), custom_call_target="tpu_custom_call" | custom-call | flops 301989888 | bytes 294912 | tf_op jit(solution)/shard_map/pallas_call | solution.py:32
  29.4 4.5 %all-to-all-start.1 = ((bf16[8,32,512]{2,1,0:T(8,128)(2,1)}), bf16[8,32,512]{2,1,0:T(8,128)(2,1)S(1)}, u32[]{:S(2)}, u32[]{:S(2)}) async-start(bf16[8,32,512]{2,1,0:T(8,128)(2,1)} %get-tuple-element.41), calls=%async_computation.1 | async-start | bytes 524288 | tf_op jit(solution)/shard_map/all_to_all | solution.py:490
  33.9 1.2 %collective-permute-start.13 = (bf16[32,2048]{1,0:T(8,128)(2,1)S(1)}, bf16[32,2048]{1,0:T(8,128)(2,1)S(1)}, u32[]{:S(2)}, u32[]{:S(2)}) collective-permute-start(bf16[32,2048]{1,0:T(8,128)(2,1)S(1)} %get-tuple-element.66.refs_0_), channel_id=1, source_target_pairs={{0,2},{1,3},{2,0},{3,1},{4,6},{5,7},{6,4},{7,5},{8,10},{9,11},{10,... | collective-permute-start | bytes 393224 | tf_op jit(solution)/shard_map/ppermute | solution.py:497
  35.1 0.3 collective-permute-start.10
  35.3 0.2 shard_map.94
  35.5 3.4 %all-to-all-done.1.received = bf16[8,32,512]{2,1,0:T(8,128)(2,1)S(1)} async-done(((bf16[8,32,512]{2,1,0:T(8,128)(2,1)}), bf16[8,32,512]{2,1,0:T(8,128)(2,1)S(1)}, u32[]{:S(2)}, u32[]{:S(2)}) %all-to-all-start.1) | async-done | bytes 262176 | tf_op jit(solution)/shard_map/all_to_all | solution.py:490
  39.0 0.7 shard_map.95.refs_4_
  39.7 4.9 %collective-permute-start.7 = (bf16[32,2048]{1,0:T(8,128)(2,1)S(1)}, bf16[32,2048]{1,0:T(8,128)(2,1)S(1)}, u32[]{:S(2)}, u32[]{:S(2)}) collective-permute-start(bf16[32,2048]{1,0:T(8,128)(2,1)S(1)} %shard_map.95.refs_4_), channel_id=1, source_target_pairs={{0,1},{1,0},{2,3},{3,2},{4,5},{5,4},{6,7},{7,6},{8,9},{9,8},{10,11... | collective-permute-start | bytes 393224 | tf_op jit(solution)/shard_map/ppermute | solution.py:497
  44.6 1.2 %collective-permute-start.8 = (bf16[32,2048]{1,0:T(8,128)(2,1)S(1)}, bf16[32,2048]{1,0:T(8,128)(2,1)S(1)}, u32[]{:S(2)}, u32[]{:S(2)}) collective-permute-start(bf16[32,2048]{1,0:T(8,128)(2,1)S(1)} %shard_map.95.refs_4_), channel_id=1, source_target_pairs={{0,2},{1,3},{2,0},{3,1},{4,6},{5,7},{6,4},{7,5},{8,10},{9,11},{10,... | collective-permute-start | bytes 393224 | tf_op jit(solution)/shard_map/ppermute | solution.py:497
  45.8 0.3 collective-permute-start.9
  46.2 0.2 collective-permute-start.11
  46.3 1.6 %shard_map.96.masks = f8e4m3fn[24,768,128]{2,1,0:T(32,128)(4,1)S(1)} custom-call(f8e4m3fn[240,768,128]{2,1,0:T(32,128)(4,1)} %get-tuple-element.55.masks_hbm), custom_call_target="tpu_custom_call" | custom-call | bytes 4718592 | tf_op jit(solution)/shard_map/pallas_call | solution.py:32
  48.0 0.4 collective-permute-start.12
  48.4 0.0 collective-permute-done.7.refs_5_
  48.4 0.2 collective-permute-start.14
  48.6 1.1 %collective-permute-done.8.refs_6_ = bf16[32,2048]{1,0:T(8,128)(2,1)S(1)} collective-permute-done((bf16[32,2048]{1,0:T(8,128)(2,1)S(1)}, bf16[32,2048]{1,0:T(8,128)(2,1)S(1)}, u32[]{:S(2)}, u32[]{:S(2)}) %collective-permute-start.8) | collective-permute-done | bytes 131104 | tf_op jit(solution)/shard_map/ppermute | solution.py:497
  49.7 0.8 %collective-permute-start.15 = (bf16[32,2048]{1,0:T(8,128)(2,1)S(1)}, bf16[32,2048]{1,0:T(8,128)(2,1)S(1)}, u32[]{:S(2)}, u32[]{:S(2)}) collective-permute-start(bf16[32,2048]{1,0:T(8,128)(2,1)S(1)} %collective-permute-done.8.refs_6_), channel_id=1, source_target_pairs={{0,1},{1,0},{2,3},{3,2},{4,5},{5,4},{6,7},{7,6},{8,9},{9,8},{10,11... | collective-permute-start | bytes 393224 | tf_op jit(solution)/shard_map/ppermute | solution.py:497
  50.5 0.5 shard_map.97
  51.1 0.0 collective-permute-done.12.refs_1_
  51.1 0.4 collective-permute-done.15.refs_7_
  51.5 2.8 %shard_map.98 = (f32[64,1024]{1,0:T(8,128)S(1)}, bf16[8,256,128]{2,1,0:T(8,128)(2,1)S(1)}) custom-call(s32[6,24]{1,0:T(8,128)S(1)} %bitcast.6, bf16[64,256]{1,0:T(8,128)(2,1)S(1)} %get-tuple-element.63.mirror_own, bf16[64,1024]{1,0:T(8,128)(2,1)S(1)} %get-tuple-element.64.own, f8e4m3fn[24,768,128]{2,1,0:T(32,128)(4,1)S(1)} %shard_map.96.masks, ...), custom_call_target="tpu_custom_call" | custom-call | flops 301989888 | bytes 2359296 | tf_op jit(solution)/shard_map/pallas_call | solution.py:32
  54.3 15.2 %all_to_all.16.received = bf16[8,256,128]{2,1,0:T(8,128)(2,1)S(1)} all-to-all(bf16[8,256,128]{2,1,0:T(8,128)(2,1)S(1)} %get-tuple-element.70), channel_id=1, replica_groups={{20,12,8,28,4,0,16,24},{21,13,9,29,5,1,17,25},{22,14,10,30,6,2,18,26},{..., dimensions={0} | all-to-all | bytes 1048576 | tf_op jit(solution)/shard_map/all_to_all | solution.py:490
  69.5 0.7 shard_map.99.refs_0_
  70.3 1.3 %collective-permute-start.17 = (bf16[64,1024]{1,0:T(8,128)(2,1)S(1)}, bf16[64,1024]{1,0:T(8,128)(2,1)S(1)}, u32[]{:S(2)}, u32[]{:S(2)}) collective-permute-start(bf16[64,1024]{1,0:T(8,128)(2,1)S(1)} %shard_map.99.refs_0_), channel_id=1, source_target_pairs={{0,2},{1,3},{2,0},{3,1},{4,6},{5,7},{6,4},{7,5},{8,10},{9,11},{10,... | collective-permute-start | bytes 393224 | tf_op jit(solution)/shard_map/ppermute | solution.py:497
  71.6 2.4 %collective-permute-start.16 = (bf16[64,1024]{1,0:T(8,128)(2,1)S(1)}, bf16[64,1024]{1,0:T(8,128)(2,1)S(1)}, u32[]{:S(2)}, u32[]{:S(2)}) collective-permute-start(bf16[64,1024]{1,0:T(8,128)(2,1)S(1)} %shard_map.99.refs_0_), channel_id=1, source_target_pairs={{0,1},{1,0},{2,3},{3,2},{4,5},{5,4},{6,7},{7,6},{8,9},{9,8},{10,11... | collective-permute-start | bytes 393224 | tf_op jit(solution)/shard_map/ppermute | solution.py:497
  74.0 0.2 collective-permute-done.17.refs_2_
  74.2 3.3 %collective-permute-start.18 = (bf16[64,1024]{1,0:T(8,128)(2,1)S(1)}, bf16[64,1024]{1,0:T(8,128)(2,1)S(1)}, u32[]{:S(2)}, u32[]{:S(2)}) collective-permute-start(bf16[64,1024]{1,0:T(8,128)(2,1)S(1)} %collective-permute-done.17.refs_2_), channel_id=1, source_target_pairs={{0,1},{1,0},{2,3},{3,2},{4,5},{5,4},{6,7},{7,6},{8,9},{9,8},{10,11... | collective-permute-start | bytes 393224 | tf_op jit(solution)/shard_map/ppermute | solution.py:497
  77.5 0.1 slice.6.neigh_t
  77.5 0.2 shard_map.100.total
  77.7 0.7 collective-permute-done.18.refs_0_
  78.4 0.8 %shard_map.101 = bf16[64,1024]{1,0:T(8,128)(2,1)} custom-call(bf16[64,64]{1,0:T(8,128)(2,1)S(1)} %slice.6.neigh_t, f32[64,1024]{1,0:T(8,128)S(1)} %shard_map.100.total, bf16[64,1024]{1,0:T(8,128)(2,1)S(1)} %collective-permute-done.18.refs_0_), custom_call_target="tpu_custom_call" | custom-call | flops 8388608 | bytes 655360 | tf_op jit(solution)/shard_map/pallas_call | solution.py:32
  (22 shorter events, 0.0 us)
Async XLA Ops:
  0.0 11.8 %copy-start.3 = (bf16[32,1024]{1,0:T(8,128)(2,1)S(1)}, bf16[32,1024]{1,0:T(8,128)(2,1)}, u32[]{:S(2)}) copy-start(bf16[32,1024]{1,0:T(8,128)(2,1)} %features.1) | copy-start | bytes 196612
  0.0 11.8 %copy-start.6 = (s32[24,6]{0,1:T(8,128)S(1)}, s32[24,6]{0,1:T(8,128)}, u32[]{:S(2)}) copy-start(s32[24,6]{0,1:T(8,128)} %param.11) | copy-start | bytes 1732
  0.0 11.8 %copy-start = (s32[3,2048]{1,0:T(4,128)S(1)}, s32[3,2048]{1,0:T(4,128)}, u32[]{:S(2)}) copy-start(s32[3,2048]{1,0:T(4,128)} %reps.5) | copy-start | bytes 73732
  0.0 27.0 %copy-start.7 = (s32[1024]{0:T(1024)S(1)}, s32[1024]{0:T(1024)}, u32[]{:S(2)}) copy-start(s32[1024]{0:T(1024)} %param.13) | copy-start | bytes 12292
  0.0 35.3 %copy-start.4 = (bf16[128,256]{1,0:T(8,128)(2,1)S(1)}, bf16[128,256]{1,0:T(8,128)(2,1)}, u32[]{:S(2)}) copy-start(bf16[128,256]{1,0:T(8,128)(2,1)} %self_one) | copy-start | bytes 196612
  0.0 35.3 %copy-start.5 = (bf16[128,256]{1,0:T(8,128)(2,1)S(1)}, bf16[128,256]{1,0:T(8,128)(2,1)}, u32[]{:S(2)}) copy-start(bf16[128,256]{1,0:T(8,128)(2,1)} %neigh_one) | copy-start | bytes 196612
  0.0 35.3 %copy-start.1 = (bf16[256,256]{1,0:T(8,128)(2,1)S(1)}, bf16[256,256]{1,0:T(8,128)(2,1)}, u32[]{:S(2)}) copy-start(bf16[256,256]{1,0:T(8,128)(2,1)} %self_two) | copy-start | bytes 393220
  0.0 35.3 %copy-start.2 = (bf16[256,256]{1,0:T(8,128)(2,1)S(1)}, bf16[256,256]{1,0:T(8,128)(2,1)}, u32[]{:S(2)}) copy-start(bf16[256,256]{1,0:T(8,128)(2,1)} %neigh_two) | copy-start | bytes 393220
  0.1 5.0 %collective-permute-start.3 = (bf16[32,1024]{1,0:T(8,128)(2,1)}, bf16[32,1024]{1,0:T(8,128)(2,1)S(1)}, u32[]{:S(2)}, u32[]{:S(2)}) collective-permute-start(bf16[32,1024]{1,0:T(8,128)(2,1)} %features.1), channel_id=1, source_target_pairs={{0,16},{4,20},{8,24},{12,28},{16,0},{20,4},{24,8},{28,12},{1,17},{... | collective-permute-start | bytes 196616 | tf_op jit(solution)/shard_map/ppermute | solution.py:516
  2.4 4.5 %collective-permute-start = (bf16[32,1024]{1,0:T(8,128)(2,1)}, bf16[32,1024]{1,0:T(8,128)(2,1)S(1)}, u32[]{:S(2)}, u32[]{:S(2)}) collective-permute-start(bf16[32,1024]{1,0:T(8,128)(2,1)} %features.1), channel_id=1, source_target_pairs={{0,4},{4,0},{8,12},{12,8},{16,20},{20,16},{24,28},{28,24},{1,5},{5... | collective-permute-start | bytes 196616 | tf_op jit(solution)/shard_map/ppermute | solution.py:516
  2.7 9.1 %collective-permute-start.1 = (bf16[32,1024]{1,0:T(8,128)(2,1)}, bf16[32,1024]{1,0:T(8,128)(2,1)S(1)}, u32[]{:S(2)}, u32[]{:S(2)}) collective-permute-start(bf16[32,1024]{1,0:T(8,128)(2,1)} %features.1), channel_id=1, source_target_pairs={{0,8},{4,12},{8,0},{12,4},{16,24},{20,28},{24,16},{28,20},{1,9},{5... | collective-permute-start | bytes 196616 | tf_op jit(solution)/shard_map/ppermute | solution.py:516
  4.0 7.8 %collective-permute-start.2 = (bf16[32,1024]{1,0:T(8,128)(2,1)}, bf16[32,1024]{1,0:T(8,128)(2,1)S(1)}, u32[]{:S(2)}, u32[]{:S(2)}) collective-permute-start(bf16[32,1024]{1,0:T(8,128)(2,1)} %features.1), channel_id=1, source_target_pairs={{0,12},{4,8},{8,4},{12,0},{16,28},{20,24},{24,20},{28,16},{1,13},{... | collective-permute-start | bytes 196616 | tf_op jit(solution)/shard_map/ppermute | solution.py:516
  5.1 6.7 %collective-permute-start.4 = (bf16[32,1024]{1,0:T(8,128)(2,1)S(1)}, bf16[32,1024]{1,0:T(8,128)(2,1)S(1)}, u32[]{:S(2)}, u32[]{:S(2)}) collective-permute-start(bf16[32,1024]{1,0:T(8,128)(2,1)S(1)} %collective-permute-done.3.refs_3_), channel_id=1, source_target_pairs={{0,4},{4,0},{8,12},{12,8},{16,20},{20,16},{24,28},{28,24},{1,5},{5... | collective-permute-start | bytes 196616 | tf_op jit(solution)/shard_map/ppermute | solution.py:516
  5.3 6.5 %collective-permute-start.5 = (bf16[32,1024]{1,0:T(8,128)(2,1)S(1)}, bf16[32,1024]{1,0:T(8,128)(2,1)S(1)}, u32[]{:S(2)}, u32[]{:S(2)}) collective-permute-start(bf16[32,1024]{1,0:T(8,128)(2,1)S(1)} %collective-permute-done.3.refs_3_), channel_id=1, source_target_pairs={{0,8},{4,12},{8,0},{12,4},{16,24},{20,28},{24,16},{28,20},{1,9},{5... | collective-permute-start | bytes 196616 | tf_op jit(solution)/shard_map/ppermute | solution.py:516
  6.9 4.9 %collective-permute-start.6 = (bf16[32,1024]{1,0:T(8,128)(2,1)S(1)}, bf16[32,1024]{1,0:T(8,128)(2,1)S(1)}, u32[]{:S(2)}, u32[]{:S(2)}) collective-permute-start(bf16[32,1024]{1,0:T(8,128)(2,1)S(1)} %collective-permute-done.3.refs_3_), channel_id=1, source_target_pairs={{0,12},{4,8},{8,4},{12,0},{16,28},{20,24},{24,20},{28,16},{1,13},{... | collective-permute-start | bytes 196616 | tf_op jit(solution)/shard_map/ppermute | solution.py:516
  29.4 9.6 %all-to-all-start.1 = ((bf16[8,32,512]{2,1,0:T(8,128)(2,1)}), bf16[8,32,512]{2,1,0:T(8,128)(2,1)S(1)}, u32[]{:S(2)}, u32[]{:S(2)}) async-start(bf16[8,32,512]{2,1,0:T(8,128)(2,1)} %get-tuple-element.41), calls=%async_computation.1 | async-start | bytes 524288 | tf_op jit(solution)/shard_map/all_to_all | solution.py:490
  33.9 14.1 %collective-permute-start.13 = (bf16[32,2048]{1,0:T(8,128)(2,1)S(1)}, bf16[32,2048]{1,0:T(8,128)(2,1)S(1)}, u32[]{:S(2)}, u32[]{:S(2)}) collective-permute-start(bf16[32,2048]{1,0:T(8,128)(2,1)S(1)} %get-tuple-element.66.refs_0_), channel_id=1, source_target_pairs={{0,2},{1,3},{2,0},{3,1},{4,6},{5,7},{6,4},{7,5},{8,10},{9,11},{10,... | collective-permute-start | bytes 393224 | tf_op jit(solution)/shard_map/ppermute | solution.py:497
  35.1 11.1 %collective-permute-start.10 = (bf16[64,1024]{1,0:T(8,128)(2,1)S(1)}, bf16[64,1024]{1,0:T(8,128)(2,1)S(1)}, u32[]{:S(2)}, u32[]{:S(2)}) collective-permute-start(bf16[64,1024]{1,0:T(8,128)(2,1)S(1)} %get-tuple-element.61.refs_0_), channel_id=1, source_target_pairs={{0,2},{1,3},{2,0},{3,1},{4,6},{5,7},{6,4},{7,5},{8,10},{9,11},{10,... | collective-permute-start | bytes 393224 | tf_op jit(solution)/shard_map/ppermute | solution.py:497
  39.7 8.7 %collective-permute-start.7 = (bf16[32,2048]{1,0:T(8,128)(2,1)S(1)}, bf16[32,2048]{1,0:T(8,128)(2,1)S(1)}, u32[]{:S(2)}, u32[]{:S(2)}) collective-permute-start(bf16[32,2048]{1,0:T(8,128)(2,1)S(1)} %shard_map.95.refs_4_), channel_id=1, source_target_pairs={{0,1},{1,0},{2,3},{3,2},{4,5},{5,4},{6,7},{7,6},{8,9},{9,8},{10,11... | collective-permute-start | bytes 393224 | tf_op jit(solution)/shard_map/ppermute | solution.py:497
  44.6 5.1 %collective-permute-start.8 = (bf16[32,2048]{1,0:T(8,128)(2,1)S(1)}, bf16[32,2048]{1,0:T(8,128)(2,1)S(1)}, u32[]{:S(2)}, u32[]{:S(2)}) collective-permute-start(bf16[32,2048]{1,0:T(8,128)(2,1)S(1)} %shard_map.95.refs_4_), channel_id=1, source_target_pairs={{0,2},{1,3},{2,0},{3,1},{4,6},{5,7},{6,4},{7,5},{8,10},{9,11},{10,... | collective-permute-start | bytes 393224 | tf_op jit(solution)/shard_map/ppermute | solution.py:497
  45.8 4.7 %collective-permute-start.9 = (bf16[64,1024]{1,0:T(8,128)(2,1)S(1)}, bf16[64,1024]{1,0:T(8,128)(2,1)S(1)}, u32[]{:S(2)}, u32[]{:S(2)}) collective-permute-start(bf16[64,1024]{1,0:T(8,128)(2,1)S(1)} %get-tuple-element.61.refs_0_), channel_id=1, source_target_pairs={{0,1},{1,0},{2,3},{3,2},{4,5},{5,4},{6,7},{7,6},{8,9},{9,8},{10,11... | collective-permute-start | bytes 393224 | tf_op jit(solution)/shard_map/ppermute | solution.py:497
  46.2 4.4 %collective-permute-start.11 = (bf16[64,1024]{1,0:T(8,128)(2,1)S(1)}, bf16[64,1024]{1,0:T(8,128)(2,1)S(1)}, u32[]{:S(2)}, u32[]{:S(2)}) collective-permute-start(bf16[64,1024]{1,0:T(8,128)(2,1)S(1)} %collective-permute-done.10.refs_2_), channel_id=1, source_target_pairs={{0,1},{1,0},{2,3},{3,2},{4,5},{5,4},{6,7},{7,6},{8,9},{9,8},{10,11... | collective-permute-start | bytes 393224 | tf_op jit(solution)/shard_map/ppermute | solution.py:497
  48.0 3.1 %collective-permute-start.12 = (bf16[32,2048]{1,0:T(8,128)(2,1)S(1)}, bf16[32,2048]{1,0:T(8,128)(2,1)S(1)}, u32[]{:S(2)}, u32[]{:S(2)}) collective-permute-start(bf16[32,2048]{1,0:T(8,128)(2,1)S(1)} %get-tuple-element.66.refs_0_), channel_id=1, source_target_pairs={{0,1},{1,0},{2,3},{3,2},{4,5},{5,4},{6,7},{7,6},{8,9},{9,8},{10,11... | collective-permute-start | bytes 393224 | tf_op jit(solution)/shard_map/ppermute | solution.py:497
  48.4 2.7 %collective-permute-start.14 = (bf16[32,2048]{1,0:T(8,128)(2,1)S(1)}, bf16[32,2048]{1,0:T(8,128)(2,1)S(1)}, u32[]{:S(2)}, u32[]{:S(2)}) collective-permute-start(bf16[32,2048]{1,0:T(8,128)(2,1)S(1)} %collective-permute-done.13.refs_2_), channel_id=1, source_target_pairs={{0,1},{1,0},{2,3},{3,2},{4,5},{5,4},{6,7},{7,6},{8,9},{9,8},{10,11... | collective-permute-start | bytes 393224 | tf_op jit(solution)/shard_map/ppermute | solution.py:497
  49.7 1.8 %collective-permute-start.15 = (bf16[32,2048]{1,0:T(8,128)(2,1)S(1)}, bf16[32,2048]{1,0:T(8,128)(2,1)S(1)}, u32[]{:S(2)}, u32[]{:S(2)}) collective-permute-start(bf16[32,2048]{1,0:T(8,128)(2,1)S(1)} %collective-permute-done.8.refs_6_), channel_id=1, source_target_pairs={{0,1},{1,0},{2,3},{3,2},{4,5},{5,4},{6,7},{7,6},{8,9},{9,8},{10,11... | collective-permute-start | bytes 393224 | tf_op jit(solution)/shard_map/ppermute | solution.py:497
  70.3 3.9 %collective-permute-start.17 = (bf16[64,1024]{1,0:T(8,128)(2,1)S(1)}, bf16[64,1024]{1,0:T(8,128)(2,1)S(1)}, u32[]{:S(2)}, u32[]{:S(2)}) collective-permute-start(bf16[64,1024]{1,0:T(8,128)(2,1)S(1)} %shard_map.99.refs_0_), channel_id=1, source_target_pairs={{0,2},{1,3},{2,0},{3,1},{4,6},{5,7},{6,4},{7,5},{8,10},{9,11},{10,... | collective-permute-start | bytes 393224 | tf_op jit(solution)/shard_map/ppermute | solution.py:497
  71.6 6.0 %collective-permute-start.16 = (bf16[64,1024]{1,0:T(8,128)(2,1)S(1)}, bf16[64,1024]{1,0:T(8,128)(2,1)S(1)}, u32[]{:S(2)}, u32[]{:S(2)}) collective-permute-start(bf16[64,1024]{1,0:T(8,128)(2,1)S(1)} %shard_map.99.refs_0_), channel_id=1, source_target_pairs={{0,1},{1,0},{2,3},{3,2},{4,5},{5,4},{6,7},{7,6},{8,9},{9,8},{10,11... | collective-permute-start | bytes 393224 | tf_op jit(solution)/shard_map/ppermute | solution.py:497
  74.2 4.3 %collective-permute-start.18 = (bf16[64,1024]{1,0:T(8,128)(2,1)S(1)}, bf16[64,1024]{1,0:T(8,128)(2,1)S(1)}, u32[]{:S(2)}, u32[]{:S(2)}) collective-permute-start(bf16[64,1024]{1,0:T(8,128)(2,1)S(1)} %collective-permute-done.17.refs_2_), channel_id=1, source_target_pairs={{0,1},{1,0},{2,3},{3,2},{4,5},{5,4},{6,7},{7,6},{8,9},{9,8},{10,11... | collective-permute-start | bytes 393224 | tf_op jit(solution)/shard_map/ppermute | solution.py:497

commit v7 on v5

--- a/solution.py
+++ b/solution.py
@@ -15,7 +15,7 @@
 SHIFT = 8
 CHUNK = 1 << SHIFT
 GROUP = 8
-ORDER = (5, 2, 3, 7, 1, 0, 4, 6)
+ORDER = (5, 3, 2, 7, 1, 0, 4, 6)
 INDEX_ROWS = 16
 VMEM = pl.BlockSpec(memory_space=pltpu.VMEM)
 SMEM = pl.BlockSpec(memory_space=pltpu.SMEM)

time: 80.1 us -> 80.2 us (level)
  no operation moved by 1% of the time
where the time goes in v7:
time: 80.2 us; the launch traced here: 79.3 us
  starting transfers between devices  31.6 us (39%)
  blocking collectives  26.6 us (33%)
  Pallas kernels  17.8 us (22%)
  waiting for transfers between devices  2.96 us (4%)
    all_to_all x2, blocking collectives, exchange(): lax.all_to_all(blocks, 'dom', split_axis=0, concat_axis=0, tiled=True, ax...  26.6 us
    ppermute x12, starting transfers between devices, swap(): return lax.ppermute(values, 'feat', [(i, i ^ k) for i in range(feat)])  19.4 us
    pallas_call x11, Pallas kernels, call(): pl.pallas_call(body, out_shape=out_shape, in_specs=[place(i) for i in ran...  17.8 us
    ppermute x7, starting transfers between devices, swap(): return lax.ppermute(values, 'dom', [(i, i ^ k) for i in range(dom)])  7.67 us
    all_to_all x1, starting transfers between devices, exchange(): lax.all_to_all(blocks, 'dom', split_axis=0, concat_axis=0, tiled=True, ax...  4.46 us
    ppermute x12, waiting for transfers between devices, swap(): return lax.ppermute(values, 'feat', [(i, i ^ k) for i in range(feat)])  2.94 us
  transfers between devices with their start and end apart: 20, of which 4 were waited for; matrix products, arithmetic and copies ran while one was open for 0% of the time, Pallas kernels for 9%

profile of v7, /device:TPU:5, one launch (start us, length us, event | category | flops | bytes accessed | tf_op | source)
XLA Modules:
  0.0 79.3 jit_solution(9011793585748099070)
XLA Ops:
  0.1 2.4 %collective-permute-start.3 = (bf16[32,1024]{1,0:T(8,128)(2,1)}, bf16[32,1024]{1,0:T(8,128)(2,1)S(1)}, u32[]{:S(2)}, u32[]{:S(2)}) collective-permute-start(bf16[32,1024]{1,0:T(8,128)(2,1)} %features.1), channel_id=1, source_target_pairs={{0,16},{4,20},{8,24},{12,28},{16,0},{20,4},{24,8},{28,12},{1,17},{... | collective-permute-start | bytes 196616 | tf_op jit(solution)/shard_map/ppermute | solution.py:516
  2.4 0.2 collective-permute-start
  2.7 1.3 %collective-permute-start.1 = (bf16[32,1024]{1,0:T(8,128)(2,1)}, bf16[32,1024]{1,0:T(8,128)(2,1)S(1)}, u32[]{:S(2)}, u32[]{:S(2)}) collective-permute-start(bf16[32,1024]{1,0:T(8,128)(2,1)} %features.1), channel_id=1, source_target_pairs={{0,8},{4,12},{8,0},{12,4},{16,24},{20,28},{24,16},{28,20},{1,9},{5... | collective-permute-start | bytes 196616 | tf_op jit(solution)/shard_map/ppermute | solution.py:516
  4.0 1.1 %collective-permute-start.2 = (bf16[32,1024]{1,0:T(8,128)(2,1)}, bf16[32,1024]{1,0:T(8,128)(2,1)S(1)}, u32[]{:S(2)}, u32[]{:S(2)}) collective-permute-start(bf16[32,1024]{1,0:T(8,128)(2,1)} %features.1), channel_id=1, source_target_pairs={{0,12},{4,8},{8,4},{12,0},{16,28},{20,24},{24,20},{28,16},{1,13},{... | collective-permute-start | bytes 196616 | tf_op jit(solution)/shard_map/ppermute | solution.py:516
  5.1 0.0 collective-permute-done.3.refs_3_
  5.1 0.2 collective-permute-start.4
  5.3 1.6 %collective-permute-start.5 = (bf16[32,1024]{1,0:T(8,128)(2,1)S(1)}, bf16[32,1024]{1,0:T(8,128)(2,1)S(1)}, u32[]{:S(2)}, u32[]{:S(2)}) collective-permute-start(bf16[32,1024]{1,0:T(8,128)(2,1)S(1)} %collective-permute-done.3.refs_3_), channel_id=1, source_target_pairs={{0,8},{4,12},{8,0},{12,4},{16,24},{20,28},{24,16},{28,20},{1,9},{5... | collective-permute-start | bytes 196616 | tf_op jit(solution)/shard_map/ppermute | solution.py:516
  6.9 0.0 collective-permute-done.refs_0_
  6.9 0.9 %collective-permute-start.6 = (bf16[32,1024]{1,0:T(8,128)(2,1)S(1)}, bf16[32,1024]{1,0:T(8,128)(2,1)S(1)}, u32[]{:S(2)}, u32[]{:S(2)}) collective-permute-start(bf16[32,1024]{1,0:T(8,128)(2,1)S(1)} %collective-permute-done.3.refs_3_), channel_id=1, source_target_pairs={{0,12},{4,8},{8,4},{12,0},{16,28},{20,24},{24,20},{28,16},{1,13},{... | collective-permute-start | bytes 196616 | tf_op jit(solution)/shard_map/ppermute | solution.py:516
  7.7 4.0 %shard_map.91.masks = bf16[24,768,128]{2,1,0:T(8,128)(2,1)S(1)} custom-call(s32[24,6,128,128]{3,2,1,0:T(8,128)} %tile_mask.1), custom_call_target="tpu_custom_call" | custom-call | bytes 14155776 | tf_op jit(solution)/shard_map/pallas_call | solution.py:32
  11.7 0.0 collective-permute-done.1.refs_1_
  11.7 0.0 collective-permute-done.2.refs_2_
  11.8 0.0 collective-permute-done.4.refs_4_
  11.8 0.0 collective-permute-done.5.refs_5_
  11.8 0.0 collective-permute-done.6.refs_6_
  11.8 3.8 %shard_map.92 = (f32[32,1024]{1,0:T(8,128)S(1)}, bf16[32,2048]{1,0:T(8,128)(2,1)S(1)}, bf16[8,144,128]{2,1,0:T(8,128)(2,1)S(1)}, f8e4m3fn[240,768,128]{2,1,0:T(32,128)(4,1)}) custom-call(s32[6,24]{1,0:T(8,128)S(1)} %bitcast.5, bf16[32,1024]{1,0:T(8,128)(2,1)S(1)} %copy-done.3, bf16[24,768,128]{2,1,0:T(8,128)(2,1)S(1)} %shard_map.91.masks, ...), custom_call_target="tpu_custom_call" | custom-call | flops 150994944 | bytes 4718592 | tf_op jit(solution)/shard_map/pallas_call | solution.py:32
  15.7 11.4 %all_to_all.15.received = bf16[8,144,128]{2,1,0:T(8,128)(2,1)S(1)} all-to-all(bf16[8,144,128]{2,1,0:T(8,128)(2,1)S(1)} %get-tuple-element.41), channel_id=1, replica_groups={{20,12,8,28,4,0,16,24},{21,13,9,29,5,1,17,25},{22,14,10,30,6,2,18,26},{..., dimensions={0} | all-to-all | bytes 589824 | tf_op jit(solution)/shard_map/all_to_all | solution.py:490
  27.0 2.4 %shard_map.93 = (bf16[64,1024]{1,0:T(8,128)(2,1)S(1)}, bf16[8,32,512]{2,1,0:T(8,128)(2,1)}, s32[8,512]{1,0:T(8,128)S(1)}) custom-call(bf16[8,144,128]{2,1,0:T(8,128)(2,1)S(1)} %all_to_all.15.received, bf16[32,1024]{1,0:T(8,128)(2,1)S(1)} %copy-done.3, f32[32,1024]{1,0:T(8,128)S(1)} %get-tuple-element.42.own, s32[1,1024]{1,0:T(1,128)S(1)} %bitcast.7), custom_call_target="tpu_custom_call" | custom-call | flops 301989888 | bytes 294912 | tf_op jit(solution)/shard_map/pallas_call | solution.py:32
  29.4 4.5 %all-to-all-start.1 = ((bf16[8,32,512]{2,1,0:T(8,128)(2,1)}), bf16[8,32,512]{2,1,0:T(8,128)(2,1)S(1)}, u32[]{:S(2)}, u32[]{:S(2)}) async-start(bf16[8,32,512]{2,1,0:T(8,128)(2,1)} %get-tuple-element.43), calls=%async_computation.1 | async-start | bytes 524288 | tf_op jit(solution)/shard_map/all_to_all | solution.py:490
  33.9 1.2 %collective-permute-start.10 = (bf16[64,1024]{1,0:T(8,128)(2,1)S(1)}, bf16[64,1024]{1,0:T(8,128)(2,1)S(1)}, u32[]{:S(2)}, u32[]{:S(2)}) collective-permute-start(bf16[64,1024]{1,0:T(8,128)(2,1)S(1)} %get-tuple-element.61.refs_0_), channel_id=1, source_target_pairs={{0,2},{1,3},{2,0},{3,1},{4,6},{5,7},{6,4},{7,5},{8,10},{9,11},{10,... | collective-permute-start | bytes 393224 | tf_op jit(solution)/shard_map/ppermute | solution.py:497
  35.1 0.2 collective-permute-start.13
  35.3 4.5 %collective-permute-start.9 = (bf16[64,1024]{1,0:T(8,128)(2,1)S(1)}, bf16[64,1024]{1,0:T(8,128)(2,1)S(1)}, u32[]{:S(2)}, u32[]{:S(2)}) collective-permute-start(bf16[64,1024]{1,0:T(8,128)(2,1)S(1)} %get-tuple-element.61.refs_0_), channel_id=1, source_target_pairs={{0,1},{1,0},{2,3},{3,2},{4,5},{5,4},{6,7},{7,6},{8,9},{9,8},{10,11... | collective-permute-start | bytes 393224 | tf_op jit(solution)/shard_map/ppermute | solution.py:497
  39.8 0.2 shard_map.94
  40.0 2.7 %collective-permute-start.11 = (bf16[64,1024]{1,0:T(8,128)(2,1)S(1)}, bf16[64,1024]{1,0:T(8,128)(2,1)S(1)}, u32[]{:S(2)}, u32[]{:S(2)}) collective-permute-start(bf16[64,1024]{1,0:T(8,128)(2,1)S(1)} %collective-permute-done.10.refs_2_), channel_id=1, source_target_pairs={{0,1},{1,0},{2,3},{3,2},{4,5},{5,4},{6,7},{7,6},{8,9},{9,8},{10,11... | collective-permute-start | bytes 393224 | tf_op jit(solution)/shard_map/ppermute | solution.py:497
  42.8 0.0 all-to-all-done.1.received
  42.8 0.7 shard_map.95.refs_4_
  43.5 1.1 %collective-permute-start.7 = (bf16[32,2048]{1,0:T(8,128)(2,1)S(1)}, bf16[32,2048]{1,0:T(8,128)(2,1)S(1)}, u32[]{:S(2)}, u32[]{:S(2)}) collective-permute-start(bf16[32,2048]{1,0:T(8,128)(2,1)S(1)} %shard_map.95.refs_4_), channel_id=1, source_target_pairs={{0,1},{1,0},{2,3},{3,2},{4,5},{5,4},{6,7},{7,6},{8,9},{9,8},{10,11... | collective-permute-start | bytes 393224 | tf_op jit(solution)/shard_map/ppermute | solution.py:497
  44.6 1.2 %collective-permute-start.8 = (bf16[32,2048]{1,0:T(8,128)(2,1)S(1)}, bf16[32,2048]{1,0:T(8,128)(2,1)S(1)}, u32[]{:S(2)}, u32[]{:S(2)}) collective-permute-start(bf16[32,2048]{1,0:T(8,128)(2,1)S(1)} %shard_map.95.refs_4_), channel_id=1, source_target_pairs={{0,2},{1,3},{2,0},{3,1},{4,6},{5,7},{6,4},{7,5},{8,10},{9,11},{10,... | collective-permute-start | bytes 393224 | tf_op jit(solution)/shard_map/ppermute | solution.py:497
  45.8 1.6 %shard_map.96.masks = f8e4m3fn[24,768,128]{2,1,0:T(32,128)(4,1)S(1)} custom-call(f8e4m3fn[240,768,128]{2,1,0:T(32,128)(4,1)} %get-tuple-element.57.masks_hbm), custom_call_target="tpu_custom_call" | custom-call | bytes 4718592 | tf_op jit(solution)/shard_map/pallas_call | solution.py:32
  47.5 0.4 collective-permute-start.12
  47.9 0.2 collective-permute-start.14
  48.0 0.5 shard_map.97
  48.6 0.0 collective-permute-done.7.refs_5_
  48.6 1.1 %collective-permute-done.8.refs_6_ = bf16[32,2048]{1,0:T(8,128)(2,1)S(1)} collective-permute-done((bf16[32,2048]{1,0:T(8,128)(2,1)S(1)}, bf16[32,2048]{1,0:T(8,128)(2,1)S(1)}, u32[]{:S(2)}, u32[]{:S(2)}) %collective-permute-start.8) | collective-permute-done | bytes 131104 | tf_op jit(solution)/shard_map/ppermute | solution.py:497
  49.7 0.8 %collective-permute-start.15 = (bf16[32,2048]{1,0:T(8,128)(2,1)S(1)}, bf16[32,2048]{1,0:T(8,128)(2,1)S(1)}, u32[]{:S(2)}, u32[]{:S(2)}) collective-permute-start(bf16[32,2048]{1,0:T(8,128)(2,1)S(1)} %collective-permute-done.8.refs_6_), channel_id=1, source_target_pairs={{0,1},{1,0},{2,3},{3,2},{4,5},{5,4},{6,7},{7,6},{8,9},{9,8},{10,11... | collective-permute-start | bytes 393224 | tf_op jit(solution)/shard_map/ppermute | solution.py:497
  50.5 0.0 collective-permute-done.12.refs_1_
  50.5 1.0 %collective-permute-done.15.refs_7_ = bf16[32,2048]{1,0:T(8,128)(2,1)S(1)} collective-permute-done((bf16[32,2048]{1,0:T(8,128)(2,1)S(1)}, bf16[32,2048]{1,0:T(8,128)(2,1)S(1)}, u32[]{:S(2)}, u32[]{:S(2)}) %collective-permute-start.15) | collective-permute-done | bytes 131104 | tf_op jit(solution)/shard_map/ppermute | solution.py:497
  51.5 2.8 %shard_map.98 = (f32[64,1024]{1,0:T(8,128)S(1)}, bf16[8,256,128]{2,1,0:T(8,128)(2,1)S(1)}) custom-call(s32[6,24]{1,0:T(8,128)S(1)} %bitcast.6, bf16[64,256]{1,0:T(8,128)(2,1)S(1)} %get-tuple-element.67.mirror_own, bf16[64,1024]{1,0:T(8,128)(2,1)S(1)} %get-tuple-element.68.own, f8e4m3fn[24,768,128]{2,1,0:T(32,128)(4,1)S(1)} %shard_map.96.masks, ...), custom_call_target="tpu_custom_call" | custom-call | flops 301989888 | bytes 2359296 | tf_op jit(solution)/shard_map/pallas_call | solution.py:32
  54.3 15.2 %all_to_all.16.received = bf16[8,256,128]{2,1,0:T(8,128)(2,1)S(1)} all-to-all(bf16[8,256,128]{2,1,0:T(8,128)(2,1)S(1)} %get-tuple-element.74), channel_id=1, replica_groups={{20,12,8,28,4,0,16,24},{21,13,9,29,5,1,17,25},{22,14,10,30,6,2,18,26},{..., dimensions={0} | all-to-all | bytes 1048576 | tf_op jit(solution)/shard_map/all_to_all | solution.py:490
  69.5 0.8 shard_map.99.refs_0_
  70.3 1.3 %collective-permute-start.17 = (bf16[64,1024]{1,0:T(8,128)(2,1)S(1)}, bf16[64,1024]{1,0:T(8,128)(2,1)S(1)}, u32[]{:S(2)}, u32[]{:S(2)}) collective-permute-start(bf16[64,1024]{1,0:T(8,128)(2,1)S(1)} %shard_map.99.refs_0_), channel_id=1, source_target_pairs={{0,2},{1,3},{2,0},{3,1},{4,6},{5,7},{6,4},{7,5},{8,10},{9,11},{10,... | collective-permute-start | bytes 393224 | tf_op jit(solution)/shard_map/ppermute | solution.py:497
  71.6 2.4 %collective-permute-start.16 = (bf16[64,1024]{1,0:T(8,128)(2,1)S(1)}, bf16[64,1024]{1,0:T(8,128)(2,1)S(1)}, u32[]{:S(2)}, u32[]{:S(2)}) collective-permute-start(bf16[64,1024]{1,0:T(8,128)(2,1)S(1)} %shard_map.99.refs_0_), channel_id=1, source_target_pairs={{0,1},{1,0},{2,3},{3,2},{4,5},{5,4},{6,7},{7,6},{8,9},{9,8},{10,11... | collective-permute-start | bytes 393224 | tf_op jit(solution)/shard_map/ppermute | solution.py:497
  74.0 0.2 collective-permute-done.17.refs_2_
  74.2 3.3 %collective-permute-start.18 = (bf16[64,1024]{1,0:T(8,128)(2,1)S(1)}, bf16[64,1024]{1,0:T(8,128)(2,1)S(1)}, u32[]{:S(2)}, u32[]{:S(2)}) collective-permute-start(bf16[64,1024]{1,0:T(8,128)(2,1)S(1)} %collective-permute-done.17.refs_2_), channel_id=1, source_target_pairs={{0,1},{1,0},{2,3},{3,2},{4,5},{5,4},{6,7},{7,6},{8,9},{9,8},{10,11... | collective-permute-start | bytes 393224 | tf_op jit(solution)/shard_map/ppermute | solution.py:497
  77.5 0.1 slice.6.neigh_t
  77.5 0.2 shard_map.100.total
  77.7 0.7 collective-permute-done.18.refs_0_
  78.4 0.8 %shard_map.101 = bf16[64,1024]{1,0:T(8,128)(2,1)} custom-call(bf16[64,64]{1,0:T(8,128)(2,1)S(1)} %slice.6.neigh_t, f32[64,1024]{1,0:T(8,128)S(1)} %shard_map.100.total, bf16[64,1024]{1,0:T(8,128)(2,1)S(1)} %collective-permute-done.18.refs_0_), custom_call_target="tpu_custom_call" | custom-call | flops 8388608 | bytes 655360 | tf_op jit(solution)/shard_map/pallas_call | solution.py:32
  (22 shorter events, 0.0 us)
Async XLA Ops:
  0.0 11.8 %copy-start.3 = (bf16[32,1024]{1,0:T(8,128)(2,1)S(1)}, bf16[32,1024]{1,0:T(8,128)(2,1)}, u32[]{:S(2)}) copy-start(bf16[32,1024]{1,0:T(8,128)(2,1)} %features.1) | copy-start | bytes 196612
  0.0 11.8 %copy-start.6 = (s32[24,6]{0,1:T(8,128)S(1)}, s32[24,6]{0,1:T(8,128)}, u32[]{:S(2)}) copy-start(s32[24,6]{0,1:T(8,128)} %param.11) | copy-start | bytes 1732
  0.0 11.8 %copy-start = (s32[3,2048]{1,0:T(4,128)S(1)}, s32[3,2048]{1,0:T(4,128)}, u32[]{:S(2)}) copy-start(s32[3,2048]{1,0:T(4,128)} %reps.5) | copy-start | bytes 73732
  0.0 27.0 %copy-start.7 = (s32[1024]{0:T(1024)S(1)}, s32[1024]{0:T(1024)}, u32[]{:S(2)}) copy-start(s32[1024]{0:T(1024)} %param.13) | copy-start | bytes 12292
  0.0 39.8 %copy-start.4 = (bf16[128,256]{1,0:T(8,128)(2,1)S(1)}, bf16[128,256]{1,0:T(8,128)(2,1)}, u32[]{:S(2)}) copy-start(bf16[128,256]{1,0:T(8,128)(2,1)} %self_one) | copy-start | bytes 196612
  0.0 39.8 %copy-start.5 = (bf16[128,256]{1,0:T(8,128)(2,1)S(1)}, bf16[128,256]{1,0:T(8,128)(2,1)}, u32[]{:S(2)}) copy-start(bf16[128,256]{1,0:T(8,128)(2,1)} %neigh_one) | copy-start | bytes 196612
  0.0 39.8 %copy-start.1 = (bf16[256,256]{1,0:T(8,128)(2,1)S(1)}, bf16[256,256]{1,0:T(8,128)(2,1)}, u32[]{:S(2)}) copy-start(bf16[256,256]{1,0:T(8,128)(2,1)} %self_two) | copy-start | bytes 393220
  0.0 39.8 %copy-start.2 = (bf16[256,256]{1,0:T(8,128)(2,1)S(1)}, bf16[256,256]{1,0:T(8,128)(2,1)}, u32[]{:S(2)}) copy-start(bf16[256,256]{1,0:T(8,128)(2,1)} %neigh_two) | copy-start | bytes 393220
  0.1 5.0 %collective-permute-start.3 = (bf16[32,1024]{1,0:T(8,128)(2,1)}, bf16[32,1024]{1,0:T(8,128)(2,1)S(1)}, u32[]{:S(2)}, u32[]{:S(2)}) collective-permute-start(bf16[32,1024]{1,0:T(8,128)(2,1)} %features.1), channel_id=1, source_target_pairs={{0,16},{4,20},{8,24},{12,28},{16,0},{20,4},{24,8},{28,12},{1,17},{... | collective-permute-start | bytes 196616 | tf_op jit(solution)/shard_map/ppermute | solution.py:516
  2.4 4.5 %collective-permute-start = (bf16[32,1024]{1,0:T(8,128)(2,1)}, bf16[32,1024]{1,0:T(8,128)(2,1)S(1)}, u32[]{:S(2)}, u32[]{:S(2)}) collective-permute-start(bf16[32,1024]{1,0:T(8,128)(2,1)} %features.1), channel_id=1, source_target_pairs={{0,4},{4,0},{8,12},{12,8},{16,20},{20,16},{24,28},{28,24},{1,5},{5... | collective-permute-start | bytes 196616 | tf_op jit(solution)/shard_map/ppermute | solution.py:516
  2.7 9.1 %collective-permute-start.1 = (bf16[32,1024]{1,0:T(8,128)(2,1)}, bf16[32,1024]{1,0:T(8,128)(2,1)S(1)}, u32[]{:S(2)}, u32[]{:S(2)}) collective-permute-start(bf16[32,1024]{1,0:T(8,128)(2,1)} %features.1), channel_id=1, source_target_pairs={{0,8},{4,12},{8,0},{12,4},{16,24},{20,28},{24,16},{28,20},{1,9},{5... | collective-permute-start | bytes 196616 | tf_op jit(solution)/shard_map/ppermute | solution.py:516
  4.0 7.8 %collective-permute-start.2 = (bf16[32,1024]{1,0:T(8,128)(2,1)}, bf16[32,1024]{1,0:T(8,128)(2,1)S(1)}, u32[]{:S(2)}, u32[]{:S(2)}) collective-permute-start(bf16[32,1024]{1,0:T(8,128)(2,1)} %features.1), channel_id=1, source_target_pairs={{0,12},{4,8},{8,4},{12,0},{16,28},{20,24},{24,20},{28,16},{1,13},{... | collective-permute-start | bytes 196616 | tf_op jit(solution)/shard_map/ppermute | solution.py:516
  5.1 6.7 %collective-permute-start.4 = (bf16[32,1024]{1,0:T(8,128)(2,1)S(1)}, bf16[32,1024]{1,0:T(8,128)(2,1)S(1)}, u32[]{:S(2)}, u32[]{:S(2)}) collective-permute-start(bf16[32,1024]{1,0:T(8,128)(2,1)S(1)} %collective-permute-done.3.refs_3_), channel_id=1, source_target_pairs={{0,4},{4,0},{8,12},{12,8},{16,20},{20,16},{24,28},{28,24},{1,5},{5... | collective-permute-start | bytes 196616 | tf_op jit(solution)/shard_map/ppermute | solution.py:516
  5.3 6.5 %collective-permute-start.5 = (bf16[32,1024]{1,0:T(8,128)(2,1)S(1)}, bf16[32,1024]{1,0:T(8,128)(2,1)S(1)}, u32[]{:S(2)}, u32[]{:S(2)}) collective-permute-start(bf16[32,1024]{1,0:T(8,128)(2,1)S(1)} %collective-permute-done.3.refs_3_), channel_id=1, source_target_pairs={{0,8},{4,12},{8,0},{12,4},{16,24},{20,28},{24,16},{28,20},{1,9},{5... | collective-permute-start | bytes 196616 | tf_op jit(solution)/shard_map/ppermute | solution.py:516
  6.9 4.9 %collective-permute-start.6 = (bf16[32,1024]{1,0:T(8,128)(2,1)S(1)}, bf16[32,1024]{1,0:T(8,128)(2,1)S(1)}, u32[]{:S(2)}, u32[]{:S(2)}) collective-permute-start(bf16[32,1024]{1,0:T(8,128)(2,1)S(1)} %collective-permute-done.3.refs_3_), channel_id=1, source_target_pairs={{0,12},{4,8},{8,4},{12,0},{16,28},{20,24},{24,20},{28,16},{1,13},{... | collective-permute-start | bytes 196616 | tf_op jit(solution)/shard_map/ppermute | solution.py:516
  29.4 13.4 %all-to-all-start.1 = ((bf16[8,32,512]{2,1,0:T(8,128)(2,1)}), bf16[8,32,512]{2,1,0:T(8,128)(2,1)S(1)}, u32[]{:S(2)}, u32[]{:S(2)}) async-start(bf16[8,32,512]{2,1,0:T(8,128)(2,1)} %get-tuple-element.43), calls=%async_computation.1 | async-start | bytes 524288 | tf_op jit(solution)/shard_map/all_to_all | solution.py:490
  33.9 6.2 %collective-permute-start.10 = (bf16[64,1024]{1,0:T(8,128)(2,1)S(1)}, bf16[64,1024]{1,0:T(8,128)(2,1)S(1)}, u32[]{:S(2)}, u32[]{:S(2)}) collective-permute-start(bf16[64,1024]{1,0:T(8,128)(2,1)S(1)} %get-tuple-element.61.refs_0_), channel_id=1, source_target_pairs={{0,2},{1,3},{2,0},{3,1},{4,6},{5,7},{6,4},{7,5},{8,10},{9,11},{10,... | collective-permute-start | bytes 393224 | tf_op jit(solution)/shard_map/ppermute | solution.py:497
  35.1 12.4 %collective-permute-start.13 = (bf16[32,2048]{1,0:T(8,128)(2,1)S(1)}, bf16[32,2048]{1,0:T(8,128)(2,1)S(1)}, u32[]{:S(2)}, u32[]{:S(2)}) collective-permute-start(bf16[32,2048]{1,0:T(8,128)(2,1)S(1)} %get-tuple-element.70.refs_0_), channel_id=1, source_target_pairs={{0,2},{1,3},{2,0},{3,1},{4,6},{5,7},{6,4},{7,5},{8,10},{9,11},{10,... | collective-permute-start | bytes 393224 | tf_op jit(solution)/shard_map/ppermute | solution.py:497
  35.3 12.6 %collective-permute-start.9 = (bf16[64,1024]{1,0:T(8,128)(2,1)S(1)}, bf16[64,1024]{1,0:T(8,128)(2,1)S(1)}, u32[]{:S(2)}, u32[]{:S(2)}) collective-permute-start(bf16[64,1024]{1,0:T(8,128)(2,1)S(1)} %get-tuple-element.61.refs_0_), channel_id=1, source_target_pairs={{0,1},{1,0},{2,3},{3,2},{4,5},{5,4},{6,7},{7,6},{8,9},{9,8},{10,11... | collective-permute-start | bytes 393224 | tf_op jit(solution)/shard_map/ppermute | solution.py:497
  40.0 8.0 %collective-permute-start.11 = (bf16[64,1024]{1,0:T(8,128)(2,1)S(1)}, bf16[64,1024]{1,0:T(8,128)(2,1)S(1)}, u32[]{:S(2)}, u32[]{:S(2)}) collective-permute-start(bf16[64,1024]{1,0:T(8,128)(2,1)S(1)} %collective-permute-done.10.refs_2_), channel_id=1, source_target_pairs={{0,1},{1,0},{2,3},{3,2},{4,5},{5,4},{6,7},{7,6},{8,9},{9,8},{10,11... | collective-permute-start | bytes 393224 | tf_op jit(solution)/shard_map/ppermute | solution.py:497
  43.5 5.1 %collective-permute-start.7 = (bf16[32,2048]{1,0:T(8,128)(2,1)S(1)}, bf16[32,2048]{1,0:T(8,128)(2,1)S(1)}, u32[]{:S(2)}, u32[]{:S(2)}) collective-permute-start(bf16[32,2048]{1,0:T(8,128)(2,1)S(1)} %shard_map.95.refs_4_), channel_id=1, source_target_pairs={{0,1},{1,0},{2,3},{3,2},{4,5},{5,4},{6,7},{7,6},{8,9},{9,8},{10,11... | collective-permute-start | bytes 393224 | tf_op jit(solution)/shard_map/ppermute | solution.py:497
  44.6 5.1 %collective-permute-start.8 = (bf16[32,2048]{1,0:T(8,128)(2,1)S(1)}, bf16[32,2048]{1,0:T(8,128)(2,1)S(1)}, u32[]{:S(2)}, u32[]{:S(2)}) collective-permute-start(bf16[32,2048]{1,0:T(8,128)(2,1)S(1)} %shard_map.95.refs_4_), channel_id=1, source_target_pairs={{0,2},{1,3},{2,0},{3,1},{4,6},{5,7},{6,4},{7,5},{8,10},{9,11},{10,... | collective-permute-start | bytes 393224 | tf_op jit(solution)/shard_map/ppermute | solution.py:497
  47.5 3.0 %collective-permute-start.12 = (bf16[32,2048]{1,0:T(8,128)(2,1)S(1)}, bf16[32,2048]{1,0:T(8,128)(2,1)S(1)}, u32[]{:S(2)}, u32[]{:S(2)}) collective-permute-start(bf16[32,2048]{1,0:T(8,128)(2,1)S(1)} %get-tuple-element.70.refs_0_), channel_id=1, source_target_pairs={{0,1},{1,0},{2,3},{3,2},{4,5},{5,4},{6,7},{7,6},{8,9},{9,8},{10,11... | collective-permute-start | bytes 393224 | tf_op jit(solution)/shard_map/ppermute | solution.py:497
  47.9 2.6 %collective-permute-start.14 = (bf16[32,2048]{1,0:T(8,128)(2,1)S(1)}, bf16[32,2048]{1,0:T(8,128)(2,1)S(1)}, u32[]{:S(2)}, u32[]{:S(2)}) collective-permute-start(bf16[32,2048]{1,0:T(8,128)(2,1)S(1)} %collective-permute-done.13.refs_2_), channel_id=1, source_target_pairs={{0,1},{1,0},{2,3},{3,2},{4,5},{5,4},{6,7},{7,6},{8,9},{9,8},{10,11... | collective-permute-start | bytes 393224 | tf_op jit(solution)/shard_map/ppermute | solution.py:497
  49.7 1.8 %collective-permute-start.15 = (bf16[32,2048]{1,0:T(8,128)(2,1)S(1)}, bf16[32,2048]{1,0:T(8,128)(2,1)S(1)}, u32[]{:S(2)}, u32[]{:S(2)}) collective-permute-start(bf16[32,2048]{1,0:T(8,128)(2,1)S(1)} %collective-permute-done.8.refs_6_), channel_id=1, source_target_pairs={{0,1},{1,0},{2,3},{3,2},{4,5},{5,4},{6,7},{7,6},{8,9},{9,8},{10,11... | collective-permute-start | bytes 393224 | tf_op jit(solution)/shard_map/ppermute | solution.py:497
  70.3 3.9 %collective-permute-start.17 = (bf16[64,1024]{1,0:T(8,128)(2,1)S(1)}, bf16[64,1024]{1,0:T(8,128)(2,1)S(1)}, u32[]{:S(2)}, u32[]{:S(2)}) collective-permute-start(bf16[64,1024]{1,0:T(8,128)(2,1)S(1)} %shard_map.99.refs_0_), channel_id=1, source_target_pairs={{0,2},{1,3},{2,0},{3,1},{4,6},{5,7},{6,4},{7,5},{8,10},{9,11},{10,... | collective-permute-start | bytes 393224 | tf_op jit(solution)/shard_map/ppermute | solution.py:497
  71.6 6.0 %collective-permute-start.16 = (bf16[64,1024]{1,0:T(8,128)(2,1)S(1)}, bf16[64,1024]{1,0:T(8,128)(2,1)S(1)}, u32[]{:S(2)}, u32[]{:S(2)}) collective-permute-start(bf16[64,1024]{1,0:T(8,128)(2,1)S(1)} %shard_map.99.refs_0_), channel_id=1, source_target_pairs={{0,1},{1,0},{2,3},{3,2},{4,5},{5,4},{6,7},{7,6},{8,9},{9,8},{10,11... | collective-permute-start | bytes 393224 | tf_op jit(solution)/shard_map/ppermute | solution.py:497
  74.2 4.3 %collective-permute-start.18 = (bf16[64,1024]{1,0:T(8,128)(2,1)S(1)}, bf16[64,1024]{1,0:T(8,128)(2,1)S(1)}, u32[]{:S(2)}, u32[]{:S(2)}) collective-permute-start(bf16[64,1024]{1,0:T(8,128)(2,1)S(1)} %collective-permute-done.17.refs_2_), channel_id=1, source_target_pairs={{0,1},{1,0},{2,3},{3,2},{4,5},{5,4},{6,7},{7,6},{8,9},{9,8},{10,11... | collective-permute-start | bytes 393224 | tf_op jit(solution)/shard_map/ppermute | solution.py:497
